TPU v7x, 256 devices: a whole 4x4x8 slice. The times are simulated.
256 devices in a mesh: lat: 4 (over x_hi, core), lon: 64 (over z, y, x_lo).
Axes of the slice: x: 4 (x_hi: 2, x_lo: 2; x = x_hi * 2 + x_lo), y: 4, z: 8, core: 2. Of those that a mesh axis runs over, the one named last changes fastest.
Arguments:
- adjoint_state: float32 [3, 1024, 32768], P(None, 'lat', 'lon'), may hold values from -6 to 6
- face_depth: float32 [2, 1024, 32768], P(None, 'lat', 'lon'), may hold values from 0.1 to 0.45
- innovation: float32 [8192, 128], P(('lat', 'lon')), may hold values from -6 to 6
- interp_weight: float32 [8192, 4, 128], P(('lat', 'lon')), may hold values from 0 to 1
- block_tile: int32 [8192, 1], P(('lat', 'lon')), may hold values from 0 to 63; in each aligned block of 32 rows (0 to 31, 32 to 63, ...) at most 2 rows name the same one
- block_count: int32 [8192, 1], P(('lat', 'lon')), may hold values from 1 to 128
- obs_row: int32 [8192, 128], P(('lat', 'lon')), may hold values from 0 to 254
- obs_col: int32 [8192, 128], P(('lat', 'lon')), may hold values from 0 to 510
Outputs:
- gradient: float32 [3, 1024, 32768], P(None, 'lat', 'lon')
Inputs may be any that keep to these rules, and one draw needn't show every extreme that they name: `block_tile`: among the 32 blocks held by one device, no tile is named by more than 2 blocks, a bound that some block reaches.
All inputs are finite; a program needn't handle non-finite values.
Results may differ from a plain program's by a relative error of at most 0.00029.
Values sent between devices are 32-bit elements; how exact they have to be, the bound alone decides.
A program may use at most 64 MiB of HBM per device.

v0:
```python
import math

import jax
import jax.numpy as jnp
from jax import lax
from jax.sharding import PartitionSpec as P

WIN = 6
WINDOWS = 4


def from_behind(block, axis, distance):
    devices = range(lax.axis_size(axis))
    route = [((i - distance) % len(devices), i) for i in devices]
    return lax.ppermute(block, axis, route)


def from_behind_2(block, axis, distance):
    devices = range(lax.axis_size(axis))
    route = [(i - distance, i) for i in devices if i - distance in devices]
    return lax.ppermute(block, axis, route)


def edge_step(adj_state, depth_east, depth_north):
    height = adj_state[0]
    east_vel = adj_state[1]
    north_vel = adj_state[2]
    east_col = from_behind(height[:, :1], "lon", -1)
    north_line = from_behind_2(height[:1, :], "lat", -1)
    height_east = jnp.concatenate([height[:, 1:], east_col], axis=1)
    height_north = jnp.concatenate([height[1:], north_line], axis=0)
    east_bar = east_vel + depth_east * (height_east - height)
    north_bar = north_vel + depth_north * (height_north - height)
    west_col = from_behind(east_bar[:, -1:], "lon", 1)
    south_line = from_behind_2(north_bar[-1:, :], "lat", 1)
    east_west = jnp.concatenate([west_col, east_bar[:, :-1]], axis=1)
    north_south = jnp.concatenate([south_line, north_bar[:-1]], axis=0)
    height_new = height + east_bar - east_west + north_bar - north_south
    return jnp.stack([height_new, east_bar, north_bar])


def spread_values(values, cells, rows_dev, cols_dev):
    items = values.shape[0]
    slot_num = values.shape[2]
    group = math.gcd(items, 8)
    turns = items // group
    grouped_vals = (
        values.reshape(turns, group, 4, slot_num)
        .transpose(0, 2, 1, 3)
        .reshape(turns, 4, group * slot_num)
    )
    grouped_cells = cells.reshape(turns, group * slot_num)
    col_ids = jnp.arange(cols_dev, dtype=jnp.int32)[None, :]
    row_ids = jnp.arange(rows_dev, dtype=jnp.int32)[None, :]
    dims = (((0,), (0,)), ((), ()))

    def add_group(total, piece):
        vals, cell_vals = piece
        base_cell = cell_vals.astype(jnp.int32)
        row_of = base_cell // cols_dev
        col_of = base_cell - row_of * cols_dev
        col_lo = (col_of[:, None] == col_ids).astype(jnp.float32)
        col_hi = (col_of[:, None] + 1 == col_ids).astype(jnp.float32)
        row_lo = (row_of[:, None] == row_ids).astype(jnp.float32)
        row_hi = (row_of[:, None] + 1 == row_ids).astype(jnp.float32)
        lower = vals[0][:, None] * col_lo + vals[1][:, None] * col_hi
        upper = vals[2][:, None] * col_lo + vals[3][:, None] * col_hi
        total = total + lax.dot_general(
            row_lo, lower, dims, precision=lax.Precision.HIGHEST, preferred_element_type=jnp.float32
        )
        total = total + lax.dot_general(
            row_hi, upper, dims, precision=lax.Precision.HIGHEST, preferred_element_type=jnp.float32
        )
        return (total, None)

    start = jnp.zeros((rows_dev, cols_dev), jnp.float32)
    total, _ = lax.scan(add_group, start, (grouped_vals, grouped_cells))
    return total


def observe(
    innovation, interp_weight, block_tile, block_count, obs_row, obs_col, rows_dev, cols_dev
):
    block_num = block_tile.shape[0]
    slot_num = innovation.shape[1]
    lon_count = lax.axis_size("lon")
    capacity = max(2, 4 * block_num // lon_count)
    slot_total = lon_count * capacity
    target = block_tile[:, 0]
    onehot = (target[:, None] == jnp.arange(lon_count, dtype=jnp.int32)[None, :]).astype(jnp.int32)
    counted = jnp.cumsum(onehot, axis=0) - onehot
    rank_of = jnp.sum(counted * onehot, axis=1)
    slot_of = target * capacity + rank_of
    chosen = slot_of[None, :] == jnp.arange(slot_total, dtype=jnp.int32)[:, None]
    source = jnp.sum(jnp.where(chosen, jnp.arange(block_num, dtype=jnp.int32)[None, :], 0), axis=1)
    filled = jnp.any(chosen, axis=1)
    usable = jnp.arange(slot_num, dtype=jnp.int32)[None, :] < block_count
    masked = jnp.where(usable, innovation, jnp.float32(0.0))
    cell_index = (obs_row * cols_dev + obs_col).astype(jnp.float32)
    cell_sent = cell_index[source]
    keep_slot = filled[:, None]
    sent_innov = jnp.where(keep_slot, masked[source], jnp.float32(0.0))
    innov_got, weight_got, cells_got = (
        lax.all_to_all(sent_innov, "lon", split_axis=0, concat_axis=0, tiled=True),
        lax.all_to_all(interp_weight[source], "lon", split_axis=0, concat_axis=0, tiled=True),
        lax.all_to_all(cell_sent, "lon", split_axis=0, concat_axis=0, tiled=True),
    )
    values = weight_got * innov_got[:, None, :]
    return spread_values(values, cells_got, rows_dev, cols_dev)


def per_device(
    adjoint_state, face_depth, innovation, interp_weight, block_tile, block_count, obs_row, obs_col
):
    rows_dev = adjoint_state.shape[1]
    cols_dev = adjoint_state.shape[2]
    lat_count = lax.axis_size("lat")
    lat_pos = lax.axis_index("lat")
    last_row = jnp.logical_and(
        lat_pos == lat_count - 1, jnp.arange(rows_dev, dtype=jnp.int32) == rows_dev - 1
    )
    depth_east = face_depth[0]
    depth_north = jnp.where(last_row[:, None], jnp.float32(0.0), face_depth[1])
    forcing = observe(
        innovation, interp_weight, block_tile, block_count, obs_row, obs_col, rows_dev, cols_dev
    )
    adj_state = adjoint_state
    for window in range(WINDOWS):
        if window == 2:
            adj_state = adj_state.at[0].add(forcing)
        adj_state = lax.fori_loop(
            0, WIN, lambda step_index, carry: edge_step(carry, depth_east, depth_north), adj_state
        )
    return adj_state


def solution(mesh):
    return jax.shard_map(
        per_device,
        mesh=mesh,
        in_specs=(
            P(None, "lat", "lon"),
            P(None, "lat", "lon"),
            P(("lat", "lon"), None),
            P(("lat", "lon"), None, None),
            P(("lat", "lon"), None),
            P(("lat", "lon"), None),
            P(("lat", "lon"), None),
            P(("lat", "lon"), None),
        ),
        out_specs=P(None, "lat", "lon"),
        check_vma=False,
    )
```

profile of v0, /device:TPU:1, one launch (start us, length us, event | category | flops | bytes accessed | tf_op | source)
XLA Modules:
  0.0 663.8 jit_solution(8489265563889057642)
XLA Ops:
  2.4 13.6 %all-to-all-start = ((f32[64,2,128]{2,1,0:T(2,128)}), f32[64,2,128]{2,1,0:T(2,128)S(1)}, u32[]{:S(2)}, u32[]{:S(2)}) async-start(f32[64,2,128]{2,1,0:T(2,128)} %bitcast.61), calls=%async_computation | async-start | bytes 131072 | tf_op jit(solution)/shard_map/all_to_all | solution.py:106
  17.7 7.8 %all-to-all-done = f32[64,2,128]{2,1,0:T(2,128)S(1)} async-done(((f32[64,2,128]{2,1,0:T(2,128)}), f32[64,2,128]{2,1,0:T(2,128)S(1)}, u32[]{:S(2)}, u32[]{:S(2)}) %all-to-all-start) | async-done | bytes 65568 | tf_op jit(solution)/shard_map/all_to_all | solution.py:106
  31.6 8.0 %all-to-all-done.2 = f32[64,2,128]{2,1,0:T(2,128)S(1)} async-done(((f32[64,2,128]{2,1,0:T(2,128)}), f32[64,2,128]{2,1,0:T(2,128)S(1)}, u32[]{:S(2)}, u32[]{:S(2)}) %all-to-all-start.2) | async-done | bytes 65568 | tf_op jit(solution)/shard_map/all_to_all | solution.py:104
  44.7 10.2 %all-to-all-done.1 = f32[128,4,128]{2,1,0:T(4,128)S(1)} async-done(((f32[128,4,128]{2,1,0:T(4,128)}), f32[128,4,128]{2,1,0:T(4,128)S(1)}, u32[]{:S(2)}, u32[]{:S(2)}) %all-to-all-start.1) | async-done | bytes 262176 | tf_op jit(solution)/shard_map/all_to_all | solution.py:105
  55.2 90.9 %while.59 = (s32[]{:T(128)}, f32[256,512]{1,0:T(8,128)S(1)}, f32[16,1024]{1,0:T(8,128)S(1)}, f32[16,4,1024]{2,1,0:T(4,128)S(1)}, s32[]{:T(128)}, /*index=5*/s32[]{:T(128)}, s32[]{}, s32[]{}, s32[]{}) while((s32[]{:T(128)}, f32[256,512]{1,0:T(8,128)S(1)}, f32[16,1024]{1,0:T(8,128)S(1)}, f32[16,4,1024]{2,1,0:T(4,128)S(1)}, ...), condition=%wide.region_9.10_spmd.clone.clone, body=%wide.region_8.9_spmd.clone.clone.sunk | while | flops 3227406336 | bytes 2248955 | solution.py:77
  146.8 125.7 %while.55 = (s32[]{:T(128)}, f32[3,256,512]{2,1,0:T(8,128)S(1)}, f32[256,512]{1,0:T(8,128)S(1)}, f32[256,512]{1,0:T(8,128)S(1)}, s32[]{:T(128)}) while((s32[]{:T(128)}, f32[3,256,512]{2,1,0:T(8,128)S(1)}, f32[256,512]{1,0:T(8,128)S(1)}, f32[256,512]{1,0:T(8,128)S(1)}, s32[]{:T(128)}) %tuple.167), condition=%wide.region_1.2_spmd, body=%wide.region_0.1_spmd.sunk | while | flops 3670018 | bytes 24651028 | solution.py:131
  146.8 6.5 collective-permute-start
  200.1 7.1 %collective-permute-start.3 = (f32[1,512]{1,0:T(1,128)S(1)}, f32[1,512]{1,0:T(1,128)S(1)}, u32[]{:S(2)}, u32[]{:S(2)}) collective-permute-start(f32[1,512]{1,0:T(1,128)S(1)} %slice.415), channel_id=1, source_target_pairs={{0,64},{64,128},{128,192},{1,65},{65,129},{129,193},{2,66},{66,130... | collective-permute-start | bytes 6152 | tf_op jit(solution)/shard_map/while/body/eval_jaxpr/ppermute | solution.py:21
  221.0 7.5 %collective-permute-start.3 = (f32[1,512]{1,0:T(1,128)S(1)}, f32[1,512]{1,0:T(1,128)S(1)}, u32[]{:S(2)}, u32[]{:S(2)}) collective-permute-start(f32[1,512]{1,0:T(1,128)S(1)} %slice.415), channel_id=1, source_target_pairs={{0,64},{64,128},{128,192},{1,65},{65,129},{129,193},{2,66},{66,130... | collective-permute-start | bytes 6152 | tf_op jit(solution)/shard_map/while/body/eval_jaxpr/ppermute | solution.py:21
  242.3 7.5 %collective-permute-start.3 = (f32[1,512]{1,0:T(1,128)S(1)}, f32[1,512]{1,0:T(1,128)S(1)}, u32[]{:S(2)}, u32[]{:S(2)}) collective-permute-start(f32[1,512]{1,0:T(1,128)S(1)} %slice.415), channel_id=1, source_target_pairs={{0,64},{64,128},{128,192},{1,65},{65,129},{129,193},{2,66},{66,130... | collective-permute-start | bytes 6152 | tf_op jit(solution)/shard_map/while/body/eval_jaxpr/ppermute | solution.py:21
  263.6 7.4 %collective-permute-start.3 = (f32[1,512]{1,0:T(1,128)S(1)}, f32[1,512]{1,0:T(1,128)S(1)}, u32[]{:S(2)}, u32[]{:S(2)}) collective-permute-start(f32[1,512]{1,0:T(1,128)S(1)} %slice.415), channel_id=1, source_target_pairs={{0,64},{64,128},{128,192},{1,65},{65,129},{129,193},{2,66},{66,130... | collective-permute-start | bytes 6152 | tf_op jit(solution)/shard_map/while/body/eval_jaxpr/ppermute | solution.py:21
  272.6 130.1 %while.56 = (s32[]{:T(128)}, f32[3,256,512]{2,1,0:T(8,128)S(1)}, f32[256,512]{1,0:T(8,128)S(1)}, f32[256,512]{1,0:T(8,128)S(1)}, s32[]{:T(128)}) while((s32[]{:T(128)}, f32[3,256,512]{2,1,0:T(8,128)S(1)}, f32[256,512]{1,0:T(8,128)S(1)}, f32[256,512]{1,0:T(8,128)S(1)}, s32[]{:T(128)}) %tuple.171), condition=%wide.region_3.4_spmd, body=%wide.region_2.3_spmd.sunk | while | flops 3670018 | bytes 24651028 | solution.py:131
  284.9 7.4 %collective-permute-start.7 = (f32[1,512]{1,0:T(1,128)S(1)}, f32[1,512]{1,0:T(1,128)S(1)}, u32[]{:S(2)}, u32[]{:S(2)}) collective-permute-start(f32[1,512]{1,0:T(1,128)S(1)} %slice.427), channel_id=1, source_target_pairs={{0,64},{64,128},{128,192},{1,65},{65,129},{129,193},{2,66},{66,130... | collective-permute-start | bytes 6152 | tf_op jit(solution)/shard_map/while/body/eval_jaxpr/ppermute | solution.py:21
  306.0 8.9 %collective-permute-start.7 = (f32[1,512]{1,0:T(1,128)S(1)}, f32[1,512]{1,0:T(1,128)S(1)}, u32[]{:S(2)}, u32[]{:S(2)}) collective-permute-start(f32[1,512]{1,0:T(1,128)S(1)} %slice.427), channel_id=1, source_target_pairs={{0,64},{64,128},{128,192},{1,65},{65,129},{129,193},{2,66},{66,130... | collective-permute-start | bytes 6152 | tf_op jit(solution)/shard_map/while/body/eval_jaxpr/ppermute | solution.py:21
  328.6 7.5 %collective-permute-start.7 = (f32[1,512]{1,0:T(1,128)S(1)}, f32[1,512]{1,0:T(1,128)S(1)}, u32[]{:S(2)}, u32[]{:S(2)}) collective-permute-start(f32[1,512]{1,0:T(1,128)S(1)} %slice.427), channel_id=1, source_target_pairs={{0,64},{64,128},{128,192},{1,65},{65,129},{129,193},{2,66},{66,130... | collective-permute-start | bytes 6152 | tf_op jit(solution)/shard_map/while/body/eval_jaxpr/ppermute | solution.py:21
  349.9 7.5 %collective-permute-start.7 = (f32[1,512]{1,0:T(1,128)S(1)}, f32[1,512]{1,0:T(1,128)S(1)}, u32[]{:S(2)}, u32[]{:S(2)}) collective-permute-start(f32[1,512]{1,0:T(1,128)S(1)} %slice.427), channel_id=1, source_target_pairs={{0,64},{64,128},{128,192},{1,65},{65,129},{129,193},{2,66},{66,130... | collective-permute-start | bytes 6152 | tf_op jit(solution)/shard_map/while/body/eval_jaxpr/ppermute | solution.py:21
  371.1 8.5 %collective-permute-start.7 = (f32[1,512]{1,0:T(1,128)S(1)}, f32[1,512]{1,0:T(1,128)S(1)}, u32[]{:S(2)}, u32[]{:S(2)}) collective-permute-start(f32[1,512]{1,0:T(1,128)S(1)} %slice.427), channel_id=1, source_target_pairs={{0,64},{64,128},{128,192},{1,65},{65,129},{129,193},{2,66},{66,130... | collective-permute-start | bytes 6152 | tf_op jit(solution)/shard_map/while/body/eval_jaxpr/ppermute | solution.py:21
  393.3 7.8 %collective-permute-start.7 = (f32[1,512]{1,0:T(1,128)S(1)}, f32[1,512]{1,0:T(1,128)S(1)}, u32[]{:S(2)}, u32[]{:S(2)}) collective-permute-start(f32[1,512]{1,0:T(1,128)S(1)} %slice.427), channel_id=1, source_target_pairs={{0,64},{64,128},{128,192},{1,65},{65,129},{129,193},{2,66},{66,130... | collective-permute-start | bytes 6152 | tf_op jit(solution)/shard_map/while/body/eval_jaxpr/ppermute | solution.py:21
  403.8 129.3 %while.57 = (s32[]{:T(128)}, f32[3,256,512]{2,1,0:T(8,128)S(1)}, f32[256,512]{1,0:T(8,128)S(1)}, f32[256,512]{1,0:T(8,128)S(1)}, s32[]{:T(128)}) while((s32[]{:T(128)}, f32[3,256,512]{2,1,0:T(8,128)S(1)}, f32[256,512]{1,0:T(8,128)S(1)}, f32[256,512]{1,0:T(8,128)S(1)}, s32[]{:T(128)}) %tuple.172), condition=%wide.region_11.12_spmd, body=%wide.region_10.11_spmd.sunk | while | flops 3670018 | bytes 24651028 | solution.py:131
  416.3 7.6 %collective-permute-start.11 = (f32[1,512]{1,0:T(1,128)S(1)}, f32[1,512]{1,0:T(1,128)S(1)}, u32[]{:S(2)}, u32[]{:S(2)}) collective-permute-start(f32[1,512]{1,0:T(1,128)S(1)} %slice.439), channel_id=1, source_target_pairs={{0,64},{64,128},{128,192},{1,65},{65,129},{129,193},{2,66},{66,130... | collective-permute-start | bytes 6152 | tf_op jit(solution)/shard_map/while/body/eval_jaxpr/ppermute | solution.py:21
  437.6 7.8 %collective-permute-start.11 = (f32[1,512]{1,0:T(1,128)S(1)}, f32[1,512]{1,0:T(1,128)S(1)}, u32[]{:S(2)}, u32[]{:S(2)}) collective-permute-start(f32[1,512]{1,0:T(1,128)S(1)} %slice.439), channel_id=1, source_target_pairs={{0,64},{64,128},{128,192},{1,65},{65,129},{129,193},{2,66},{66,130... | collective-permute-start | bytes 6152 | tf_op jit(solution)/shard_map/while/body/eval_jaxpr/ppermute | solution.py:21
  459.1 8.1 %collective-permute-start.11 = (f32[1,512]{1,0:T(1,128)S(1)}, f32[1,512]{1,0:T(1,128)S(1)}, u32[]{:S(2)}, u32[]{:S(2)}) collective-permute-start(f32[1,512]{1,0:T(1,128)S(1)} %slice.439), channel_id=1, source_target_pairs={{0,64},{64,128},{128,192},{1,65},{65,129},{129,193},{2,66},{66,130... | collective-permute-start | bytes 6152 | tf_op jit(solution)/shard_map/while/body/eval_jaxpr/ppermute | solution.py:21
  480.8 7.9 %collective-permute-start.11 = (f32[1,512]{1,0:T(1,128)S(1)}, f32[1,512]{1,0:T(1,128)S(1)}, u32[]{:S(2)}, u32[]{:S(2)}) collective-permute-start(f32[1,512]{1,0:T(1,128)S(1)} %slice.439), channel_id=1, source_target_pairs={{0,64},{64,128},{128,192},{1,65},{65,129},{129,193},{2,66},{66,130... | collective-permute-start | bytes 6152 | tf_op jit(solution)/shard_map/while/body/eval_jaxpr/ppermute | solution.py:21
  502.4 7.7 %collective-permute-start.11 = (f32[1,512]{1,0:T(1,128)S(1)}, f32[1,512]{1,0:T(1,128)S(1)}, u32[]{:S(2)}, u32[]{:S(2)}) collective-permute-start(f32[1,512]{1,0:T(1,128)S(1)} %slice.439), channel_id=1, source_target_pairs={{0,64},{64,128},{128,192},{1,65},{65,129},{129,193},{2,66},{66,130... | collective-permute-start | bytes 6152 | tf_op jit(solution)/shard_map/while/body/eval_jaxpr/ppermute | solution.py:21
  523.8 7.8 %collective-permute-start.11 = (f32[1,512]{1,0:T(1,128)S(1)}, f32[1,512]{1,0:T(1,128)S(1)}, u32[]{:S(2)}, u32[]{:S(2)}) collective-permute-start(f32[1,512]{1,0:T(1,128)S(1)} %slice.439), channel_id=1, source_target_pairs={{0,64},{64,128},{128,192},{1,65},{65,129},{129,193},{2,66},{66,130... | collective-permute-start | bytes 6152 | tf_op jit(solution)/shard_map/while/body/eval_jaxpr/ppermute | solution.py:21
  533.1 129.5 %while.58 = (s32[]{:T(128)}, f32[3,256,512]{2,1,0:T(8,128)S(1)}, f32[256,512]{1,0:T(8,128)S(1)}, f32[256,512]{1,0:T(8,128)S(1)}, s32[]{:T(128)}) while((s32[]{:T(128)}, f32[3,256,512]{2,1,0:T(8,128)S(1)}, f32[256,512]{1,0:T(8,128)S(1)}, f32[256,512]{1,0:T(8,128)S(1)}, s32[]{:T(128)}) %tuple.173), condition=%wide.region_13.14_spmd, body=%wide.region_12.13_spmd.sunk | while | flops 3670018 | bytes 24651028 | solution.py:131
  545.2 8.1 %collective-permute-start.15 = (f32[1,512]{1,0:T(1,128)S(1)}, f32[1,512]{1,0:T(1,128)S(1)}, u32[]{:S(2)}, u32[]{:S(2)}) collective-permute-start(f32[1,512]{1,0:T(1,128)S(1)} %slice.451), channel_id=1, source_target_pairs={{0,64},{64,128},{128,192},{1,65},{65,129},{129,193},{2,66},{66,130... | collective-permute-start | bytes 6152 | tf_op jit(solution)/shard_map/while/body/eval_jaxpr/ppermute | solution.py:21
  567.2 7.7 %collective-permute-start.15 = (f32[1,512]{1,0:T(1,128)S(1)}, f32[1,512]{1,0:T(1,128)S(1)}, u32[]{:S(2)}, u32[]{:S(2)}) collective-permute-start(f32[1,512]{1,0:T(1,128)S(1)} %slice.451), channel_id=1, source_target_pairs={{0,64},{64,128},{128,192},{1,65},{65,129},{129,193},{2,66},{66,130... | collective-permute-start | bytes 6152 | tf_op jit(solution)/shard_map/while/body/eval_jaxpr/ppermute | solution.py:21
  588.6 7.7 %collective-permute-start.15 = (f32[1,512]{1,0:T(1,128)S(1)}, f32[1,512]{1,0:T(1,128)S(1)}, u32[]{:S(2)}, u32[]{:S(2)}) collective-permute-start(f32[1,512]{1,0:T(1,128)S(1)} %slice.451), channel_id=1, source_target_pairs={{0,64},{64,128},{128,192},{1,65},{65,129},{129,193},{2,66},{66,130... | collective-permute-start | bytes 6152 | tf_op jit(solution)/shard_map/while/body/eval_jaxpr/ppermute | solution.py:21
  610.0 7.8 %collective-permute-start.15 = (f32[1,512]{1,0:T(1,128)S(1)}, f32[1,512]{1,0:T(1,128)S(1)}, u32[]{:S(2)}, u32[]{:S(2)}) collective-permute-start(f32[1,512]{1,0:T(1,128)S(1)} %slice.451), channel_id=1, source_target_pairs={{0,64},{64,128},{128,192},{1,65},{65,129},{129,193},{2,66},{66,130... | collective-permute-start | bytes 6152 | tf_op jit(solution)/shard_map/while/body/eval_jaxpr/ppermute | solution.py:21
  631.4 8.1 %collective-permute-start.15 = (f32[1,512]{1,0:T(1,128)S(1)}, f32[1,512]{1,0:T(1,128)S(1)}, u32[]{:S(2)}, u32[]{:S(2)}) collective-permute-start(f32[1,512]{1,0:T(1,128)S(1)} %slice.451), channel_id=1, source_target_pairs={{0,64},{64,128},{128,192},{1,65},{65,129},{129,193},{2,66},{66,130... | collective-permute-start | bytes 6152 | tf_op jit(solution)/shard_map/while/body/eval_jaxpr/ppermute | solution.py:21
  653.2 8.0 %collective-permute-start.15 = (f32[1,512]{1,0:T(1,128)S(1)}, f32[1,512]{1,0:T(1,128)S(1)}, u32[]{:S(2)}, u32[]{:S(2)}) collective-permute-start(f32[1,512]{1,0:T(1,128)S(1)} %slice.451), channel_id=1, source_target_pairs={{0,64},{64,128},{128,192},{1,65},{65,129},{129,193},{2,66},{66,130... | collective-permute-start | bytes 6152 | tf_op jit(solution)/shard_map/while/body/eval_jaxpr/ppermute | solution.py:21
  (775 shorter events, 441.2 us)
Async XLA Ops:
  2.4 23.1 %all-to-all-start = ((f32[64,2,128]{2,1,0:T(2,128)}), f32[64,2,128]{2,1,0:T(2,128)S(1)}, u32[]{:S(2)}, u32[]{:S(2)}) async-start(f32[64,2,128]{2,1,0:T(2,128)} %bitcast.61), calls=%async_computation | async-start | bytes 131072 | tf_op jit(solution)/shard_map/all_to_all | solution.py:106
  25.6 14.1 %all-to-all-start.2 = ((f32[64,2,128]{2,1,0:T(2,128)}), f32[64,2,128]{2,1,0:T(2,128)S(1)}, u32[]{:S(2)}, u32[]{:S(2)}) async-start(f32[64,2,128]{2,1,0:T(2,128)} %broadcast_select_fusion), calls=%async_computation.2 | async-start | bytes 131072 | tf_op jit(solution)/shard_map/all_to_all | solution.py:104
  39.6 15.3 %all-to-all-start.1 = ((f32[128,4,128]{2,1,0:T(4,128)}), f32[128,4,128]{2,1,0:T(4,128)S(1)}, u32[]{:S(2)}, u32[]{:S(2)}) async-start(f32[128,4,128]{2,1,0:T(4,128)} %gather_fusion.1), calls=%async_computation.1 | async-start | bytes 524288 | tf_op jit(solution)/shard_map/all_to_all | solution.py:105
  146.8 11.9 %collective-permute-start = (f32[1,512]{1,0:T(1,128)S(1)}, f32[1,512]{1,0:T(1,128)S(1)}, u32[]{:S(2)}, u32[]{:S(2)}) collective-permute-start(f32[1,512]{1,0:T(1,128)S(1)} %slice_bitcast_fusion.45), channel_id=1, source_target_pairs={{64,0},{128,64},{192,128},{65,1},{129,65},{193,129},{66,2},{130,66... | collective-permute-start | bytes 6152 | tf_op jit(solution)/shard_map/while/body/eval_jaxpr/ppermute | solution.py:21
  160.3 9.1 %collective-permute-start.2 = (f32[256,1]{1,0:T(8,128)S(1)}, f32[256,1]{1,0:T(8,128)S(1)}, u32[]{:S(2)}, u32[]{:S(2)}) collective-permute-start(f32[256,1]{1,0:T(8,128)S(1)} %slice.414), channel_id=1, source_target_pairs={{63,0},{0,1},{1,2},{2,3},{3,4},{4,5},{5,6},{6,7},{7,8},{8,9},{9,10... | collective-permute-start | bytes 3080 | tf_op jit(solution)/shard_map/while/body/eval_jaxpr/ppermute | solution.py:15
  180.2 9.0 %collective-permute-start.2 = (f32[256,1]{1,0:T(8,128)S(1)}, f32[256,1]{1,0:T(8,128)S(1)}, u32[]{:S(2)}, u32[]{:S(2)}) collective-permute-start(f32[256,1]{1,0:T(8,128)S(1)} %slice.414), channel_id=1, source_target_pairs={{63,0},{0,1},{1,2},{2,3},{3,4},{4,5},{5,6},{6,7},{7,8},{8,9},{9,10... | collective-permute-start | bytes 3080 | tf_op jit(solution)/shard_map/while/body/eval_jaxpr/ppermute | solution.py:15
  209.7 9.6 %collective-permute-start = (f32[1,512]{1,0:T(1,128)S(1)}, f32[1,512]{1,0:T(1,128)S(1)}, u32[]{:S(2)}, u32[]{:S(2)}) collective-permute-start(f32[1,512]{1,0:T(1,128)S(1)} %slice_bitcast_fusion.45), channel_id=1, source_target_pairs={{64,0},{128,64},{192,128},{65,1},{129,65},{193,129},{66,2},{130,66... | collective-permute-start | bytes 6152 | tf_op jit(solution)/shard_map/while/body/eval_jaxpr/ppermute | solution.py:21
  220.9 9.4 %collective-permute-start.2 = (f32[256,1]{1,0:T(8,128)S(1)}, f32[256,1]{1,0:T(8,128)S(1)}, u32[]{:S(2)}, u32[]{:S(2)}) collective-permute-start(f32[256,1]{1,0:T(8,128)S(1)} %slice.414), channel_id=1, source_target_pairs={{63,0},{0,1},{1,2},{2,3},{3,4},{4,5},{5,6},{6,7},{7,8},{8,9},{9,10... | collective-permute-start | bytes 3080 | tf_op jit(solution)/shard_map/while/body/eval_jaxpr/ppermute | solution.py:15
  221.0 9.3 %collective-permute-start.3 = (f32[1,512]{1,0:T(1,128)S(1)}, f32[1,512]{1,0:T(1,128)S(1)}, u32[]{:S(2)}, u32[]{:S(2)}) collective-permute-start(f32[1,512]{1,0:T(1,128)S(1)} %slice.415), channel_id=1, source_target_pairs={{0,64},{64,128},{128,192},{1,65},{65,129},{129,193},{2,66},{66,130... | collective-permute-start | bytes 6152 | tf_op jit(solution)/shard_map/while/body/eval_jaxpr/ppermute | solution.py:21
  231.1 9.6 %collective-permute-start = (f32[1,512]{1,0:T(1,128)S(1)}, f32[1,512]{1,0:T(1,128)S(1)}, u32[]{:S(2)}, u32[]{:S(2)}) collective-permute-start(f32[1,512]{1,0:T(1,128)S(1)} %slice_bitcast_fusion.45), channel_id=1, source_target_pairs={{64,0},{128,64},{192,128},{65,1},{129,65},{193,129},{66,2},{130,66... | collective-permute-start | bytes 6152 | tf_op jit(solution)/shard_map/while/body/eval_jaxpr/ppermute | solution.py:21
  251.6 10.4 %collective-permute-start = (f32[1,512]{1,0:T(1,128)S(1)}, f32[1,512]{1,0:T(1,128)S(1)}, u32[]{:S(2)}, u32[]{:S(2)}) collective-permute-start(f32[1,512]{1,0:T(1,128)S(1)} %slice_bitcast_fusion.45), channel_id=1, source_target_pairs={{64,0},{128,64},{192,128},{65,1},{129,65},{193,129},{66,2},{130,66... | collective-permute-start | bytes 6152 | tf_op jit(solution)/shard_map/while/body/eval_jaxpr/ppermute | solution.py:21
  272.6 10.7 %collective-permute-start.4 = (f32[1,512]{1,0:T(1,128)S(1)}, f32[1,512]{1,0:T(1,128)S(1)}, u32[]{:S(2)}, u32[]{:S(2)}) collective-permute-start(f32[1,512]{1,0:T(1,128)S(1)} %slice_bitcast_fusion.50), channel_id=1, source_target_pairs={{64,0},{128,64},{192,128},{65,1},{129,65},{193,129},{66,2},{130,66... | collective-permute-start | bytes 6152 | tf_op jit(solution)/shard_map/while/body/eval_jaxpr/ppermute | solution.py:21
  293.8 10.5 %collective-permute-start.4 = (f32[1,512]{1,0:T(1,128)S(1)}, f32[1,512]{1,0:T(1,128)S(1)}, u32[]{:S(2)}, u32[]{:S(2)}) collective-permute-start(f32[1,512]{1,0:T(1,128)S(1)} %slice_bitcast_fusion.50), channel_id=1, source_target_pairs={{64,0},{128,64},{192,128},{65,1},{129,65},{193,129},{66,2},{130,66... | collective-permute-start | bytes 6152 | tf_op jit(solution)/shard_map/while/body/eval_jaxpr/ppermute | solution.py:21
  305.9 9.1 %collective-permute-start.6 = (f32[256,1]{1,0:T(8,128)S(1)}, f32[256,1]{1,0:T(8,128)S(1)}, u32[]{:S(2)}, u32[]{:S(2)}) collective-permute-start(f32[256,1]{1,0:T(8,128)S(1)} %slice.426), channel_id=1, source_target_pairs={{63,0},{0,1},{1,2},{2,3},{3,4},{4,5},{5,6},{6,7},{7,8},{8,9},{9,10... | collective-permute-start | bytes 3080 | tf_op jit(solution)/shard_map/while/body/eval_jaxpr/ppermute | solution.py:15
  306.0 9.6 %collective-permute-start.7 = (f32[1,512]{1,0:T(1,128)S(1)}, f32[1,512]{1,0:T(1,128)S(1)}, u32[]{:S(2)}, u32[]{:S(2)}) collective-permute-start(f32[1,512]{1,0:T(1,128)S(1)} %slice.427), channel_id=1, source_target_pairs={{0,64},{64,128},{128,192},{1,65},{65,129},{129,193},{2,66},{66,130... | collective-permute-start | bytes 6152 | tf_op jit(solution)/shard_map/while/body/eval_jaxpr/ppermute | solution.py:21
  316.4 10.6 %collective-permute-start.4 = (f32[1,512]{1,0:T(1,128)S(1)}, f32[1,512]{1,0:T(1,128)S(1)}, u32[]{:S(2)}, u32[]{:S(2)}) collective-permute-start(f32[1,512]{1,0:T(1,128)S(1)} %slice_bitcast_fusion.50), channel_id=1, source_target_pairs={{64,0},{128,64},{192,128},{65,1},{129,65},{193,129},{66,2},{130,66... | collective-permute-start | bytes 6152 | tf_op jit(solution)/shard_map/while/body/eval_jaxpr/ppermute | solution.py:21
  337.7 10.6 %collective-permute-start.4 = (f32[1,512]{1,0:T(1,128)S(1)}, f32[1,512]{1,0:T(1,128)S(1)}, u32[]{:S(2)}, u32[]{:S(2)}) collective-permute-start(f32[1,512]{1,0:T(1,128)S(1)} %slice_bitcast_fusion.50), channel_id=1, source_target_pairs={{64,0},{128,64},{192,128},{65,1},{129,65},{193,129},{66,2},{130,66... | collective-permute-start | bytes 6152 | tf_op jit(solution)/shard_map/while/body/eval_jaxpr/ppermute | solution.py:21
  358.9 10.6 %collective-permute-start.4 = (f32[1,512]{1,0:T(1,128)S(1)}, f32[1,512]{1,0:T(1,128)S(1)}, u32[]{:S(2)}, u32[]{:S(2)}) collective-permute-start(f32[1,512]{1,0:T(1,128)S(1)} %slice_bitcast_fusion.50), channel_id=1, source_target_pairs={{64,0},{128,64},{192,128},{65,1},{129,65},{193,129},{66,2},{130,66... | collective-permute-start | bytes 6152 | tf_op jit(solution)/shard_map/while/body/eval_jaxpr/ppermute | solution.py:21
  371.1 9.2 %collective-permute-start.7 = (f32[1,512]{1,0:T(1,128)S(1)}, f32[1,512]{1,0:T(1,128)S(1)}, u32[]{:S(2)}, u32[]{:S(2)}) collective-permute-start(f32[1,512]{1,0:T(1,128)S(1)} %slice.427), channel_id=1, source_target_pairs={{0,64},{64,128},{128,192},{1,65},{65,129},{129,193},{2,66},{66,130... | collective-permute-start | bytes 6152 | tf_op jit(solution)/shard_map/while/body/eval_jaxpr/ppermute | solution.py:21
  381.1 10.6 %collective-permute-start.4 = (f32[1,512]{1,0:T(1,128)S(1)}, f32[1,512]{1,0:T(1,128)S(1)}, u32[]{:S(2)}, u32[]{:S(2)}) collective-permute-start(f32[1,512]{1,0:T(1,128)S(1)} %slice_bitcast_fusion.50), channel_id=1, source_target_pairs={{64,0},{128,64},{192,128},{65,1},{129,65},{193,129},{66,2},{130,66... | collective-permute-start | bytes 6152 | tf_op jit(solution)/shard_map/while/body/eval_jaxpr/ppermute | solution.py:21
  404.0 10.6 %collective-permute-start.8 = (f32[1,512]{1,0:T(1,128)S(1)}, f32[1,512]{1,0:T(1,128)S(1)}, u32[]{:S(2)}, u32[]{:S(2)}) collective-permute-start(f32[1,512]{1,0:T(1,128)S(1)} %slice_bitcast_fusion.55), channel_id=1, source_target_pairs={{64,0},{128,64},{192,128},{65,1},{129,65},{193,129},{66,2},{130,66... | collective-permute-start | bytes 6152 | tf_op jit(solution)/shard_map/while/body/eval_jaxpr/ppermute | solution.py:21
  425.4 10.5 %collective-permute-start.8 = (f32[1,512]{1,0:T(1,128)S(1)}, f32[1,512]{1,0:T(1,128)S(1)}, u32[]{:S(2)}, u32[]{:S(2)}) collective-permute-start(f32[1,512]{1,0:T(1,128)S(1)} %slice_bitcast_fusion.55), channel_id=1, source_target_pairs={{64,0},{128,64},{192,128},{65,1},{129,65},{193,129},{66,2},{130,66... | collective-permute-start | bytes 6152 | tf_op jit(solution)/shard_map/while/body/eval_jaxpr/ppermute | solution.py:21
  446.9 10.5 %collective-permute-start.8 = (f32[1,512]{1,0:T(1,128)S(1)}, f32[1,512]{1,0:T(1,128)S(1)}, u32[]{:S(2)}, u32[]{:S(2)}) collective-permute-start(f32[1,512]{1,0:T(1,128)S(1)} %slice_bitcast_fusion.55), channel_id=1, source_target_pairs={{64,0},{128,64},{192,128},{65,1},{129,65},{193,129},{66,2},{130,66... | collective-permute-start | bytes 6152 | tf_op jit(solution)/shard_map/while/body/eval_jaxpr/ppermute | solution.py:21
  468.7 10.5 %collective-permute-start.8 = (f32[1,512]{1,0:T(1,128)S(1)}, f32[1,512]{1,0:T(1,128)S(1)}, u32[]{:S(2)}, u32[]{:S(2)}) collective-permute-start(f32[1,512]{1,0:T(1,128)S(1)} %slice_bitcast_fusion.55), channel_id=1, source_target_pairs={{64,0},{128,64},{192,128},{65,1},{129,65},{193,129},{66,2},{130,66... | collective-permute-start | bytes 6152 | tf_op jit(solution)/shard_map/while/body/eval_jaxpr/ppermute | solution.py:21
  490.2 10.5 %collective-permute-start.8 = (f32[1,512]{1,0:T(1,128)S(1)}, f32[1,512]{1,0:T(1,128)S(1)}, u32[]{:S(2)}, u32[]{:S(2)}) collective-permute-start(f32[1,512]{1,0:T(1,128)S(1)} %slice_bitcast_fusion.55), channel_id=1, source_target_pairs={{64,0},{128,64},{192,128},{65,1},{129,65},{193,129},{66,2},{130,66... | collective-permute-start | bytes 6152 | tf_op jit(solution)/shard_map/while/body/eval_jaxpr/ppermute | solution.py:21
  511.6 10.5 %collective-permute-start.8 = (f32[1,512]{1,0:T(1,128)S(1)}, f32[1,512]{1,0:T(1,128)S(1)}, u32[]{:S(2)}, u32[]{:S(2)}) collective-permute-start(f32[1,512]{1,0:T(1,128)S(1)} %slice_bitcast_fusion.55), channel_id=1, source_target_pairs={{64,0},{128,64},{192,128},{65,1},{129,65},{193,129},{66,2},{130,66... | collective-permute-start | bytes 6152 | tf_op jit(solution)/shard_map/while/body/eval_jaxpr/ppermute | solution.py:21
  533.1 10.5 %collective-permute-start.12 = (f32[1,512]{1,0:T(1,128)S(1)}, f32[1,512]{1,0:T(1,128)S(1)}, u32[]{:S(2)}, u32[]{:S(2)}) collective-permute-start(f32[1,512]{1,0:T(1,128)S(1)} %slice_bitcast_fusion.60), channel_id=1, source_target_pairs={{64,0},{128,64},{192,128},{65,1},{129,65},{193,129},{66,2},{130,66... | collective-permute-start | bytes 6152 | tf_op jit(solution)/shard_map/while/body/eval_jaxpr/ppermute | solution.py:21
  554.9 10.7 %collective-permute-start.12 = (f32[1,512]{1,0:T(1,128)S(1)}, f32[1,512]{1,0:T(1,128)S(1)}, u32[]{:S(2)}, u32[]{:S(2)}) collective-permute-start(f32[1,512]{1,0:T(1,128)S(1)} %slice_bitcast_fusion.60), channel_id=1, source_target_pairs={{64,0},{128,64},{192,128},{65,1},{129,65},{193,129},{66,2},{130,66... | collective-permute-start | bytes 6152 | tf_op jit(solution)/shard_map/while/body/eval_jaxpr/ppermute | solution.py:21
  576.4 10.5 %collective-permute-start.12 = (f32[1,512]{1,0:T(1,128)S(1)}, f32[1,512]{1,0:T(1,128)S(1)}, u32[]{:S(2)}, u32[]{:S(2)}) collective-permute-start(f32[1,512]{1,0:T(1,128)S(1)} %slice_bitcast_fusion.60), channel_id=1, source_target_pairs={{64,0},{128,64},{192,128},{65,1},{129,65},{193,129},{66,2},{130,66... | collective-permute-start | bytes 6152 | tf_op jit(solution)/shard_map/while/body/eval_jaxpr/ppermute | solution.py:21
  597.8 10.5 %collective-permute-start.12 = (f32[1,512]{1,0:T(1,128)S(1)}, f32[1,512]{1,0:T(1,128)S(1)}, u32[]{:S(2)}, u32[]{:S(2)}) collective-permute-start(f32[1,512]{1,0:T(1,128)S(1)} %slice_bitcast_fusion.60), channel_id=1, source_target_pairs={{64,0},{128,64},{192,128},{65,1},{129,65},{193,129},{66,2},{130,66... | collective-permute-start | bytes 6152 | tf_op jit(solution)/shard_map/while/body/eval_jaxpr/ppermute | solution.py:21
  619.3 10.5 %collective-permute-start.12 = (f32[1,512]{1,0:T(1,128)S(1)}, f32[1,512]{1,0:T(1,128)S(1)}, u32[]{:S(2)}, u32[]{:S(2)}) collective-permute-start(f32[1,512]{1,0:T(1,128)S(1)} %slice_bitcast_fusion.60), channel_id=1, source_target_pairs={{64,0},{128,64},{192,128},{65,1},{129,65},{193,129},{66,2},{130,66... | collective-permute-start | bytes 6152 | tf_op jit(solution)/shard_map/while/body/eval_jaxpr/ppermute | solution.py:21
  641.0 10.5 %collective-permute-start.12 = (f32[1,512]{1,0:T(1,128)S(1)}, f32[1,512]{1,0:T(1,128)S(1)}, u32[]{:S(2)}, u32[]{:S(2)}) collective-permute-start(f32[1,512]{1,0:T(1,128)S(1)} %slice_bitcast_fusion.60), channel_id=1, source_target_pairs={{64,0},{128,64},{192,128},{65,1},{129,65},{193,129},{66,2},{130,66... | collective-permute-start | bytes 6152 | tf_op jit(solution)/shard_map/while/body/eval_jaxpr/ppermute | solution.py:21
  (173 other events, 1310.9 us)
where the time goes:
time: 670 us; the launch traced here: 664 us
  starting transfers between devices  389 us (58%)
  matrix products  79 us (12%)
  other arithmetic  64.1 us (10%)
  waiting for transfers between devices  63.9 us (10%)
  local copies, waits for them, and re-layouts  63.1 us (9%)
    ppermute x48, starting transfers between devices, from_behind_2(): return lax.ppermute(block, axis, route)  237 us
    ppermute x48, starting transfers between devices, from_behind(): return lax.ppermute(block, axis, route)  129 us
    dot_general x16, matrix products, add_group(): lax.dot_general(row_lo, lower, dims, precision=lax.Precision.HIGHEST, pre...  46.2 us
    add x24, other arithmetic, edge_step(): north_bar = north_vel + depth_north * (height_north - height)  34 us
    dot_general x16, matrix products, add_group(): lax.dot_general(row_hi, upper, dims, precision=lax.Precision.HIGHEST, pre...  32.8 us
    concatenate x24, local copies, waits for them, and re-layouts, edge_step(): height_east = jnp.concatenate([height[:, 1:], east_col], axis=1)  28.4 us
    slice x24, local copies, waits for them, and re-layouts, edge_step(): height_north = jnp.concatenate([height[1:], north_line], axis=0)  22.2 us
    ppermute x48, waiting for transfers between devices, from_behind_2(): return lax.ppermute(block, axis, route)  19.8 us
  transfers between devices with their start and end apart: 99, of which 62 were waited for; matrix products, arithmetic and copies ran while one was open for 8% of the time, Pallas kernels for 0%

commit v1 on v0

v1 whole, which is shorter than its diff:
```python
import functools

import jax
import jax.numpy as jnp
from jax import lax
from jax.experimental import pallas as pl
from jax.experimental.pallas import tpu as pltpu
from jax.sharding import PartitionSpec as P

WIN = 6
WINDOWS = 4
CAP = 2
LANES = 128
ROWS8 = 8
HALO = WIN * WINDOWS
HALF = HALO // 2
FRINGE = 16
PIECES = 5
GROUP = 2
MESH = pl.DeviceIdType.MESH
F32 = jnp.float32
BF16 = jnp.bfloat16
I32 = jnp.int32


def lane_ids(shape):
    return lax.broadcasted_iota(I32, shape, len(shape) - 1)


def shift_to(me, index, lon):
    if lon != 64:
        return lax.rem(me + index, lon)
    z = (me // 8 + index % 8) % 8
    y = (me // 2 + index // 8) % 4
    x = (me + index // 32) % 2
    return (z * 4 + y) * 2 + x


def steps(fields, tiles, first, last, number):
    cols = tiles + 1
    lane = lane_ids((ROWS8, LANES))
    sub = lax.broadcasted_iota(I32, (ROWS8, LANES), 0)
    last_lane = lane == LANES - 1
    first_lane = lane == 0
    first_sub = sub == 0

    def group(index, above):
        base = pl.multiple_of(index * ROWS8, ROWS8)
        here = pl.ds(base, ROWS8)
        north = pl.ds(base + 1, ROWS8)
        height = [fields[0, t, here, :] for t in range(cols)]
        height_n = [fields[0, t, north, :] for t in range(cols)]
        turned = [pltpu.roll(x, LANES - 1, 1) for x in height]
        height_e = [jnp.where(last_lane, turned[(t + 1) % cols], turned[t]) for t in range(cols)]
        east = [fields[1, t, here, :] + fields[3, t, here, :] * (height_e[t] - height[t]) for t in range(cols)]
        north_v = [fields[2, t, here, :] + fields[4, t, here, :] * (height_n[t] - height[t]) for t in range(cols)]
        turned = [pltpu.roll(x, 1, 1) for x in east]
        below = [pltpu.roll(x, 1, 0) for x in north_v]
        for t in range(cols):
            west = jnp.where(first_lane, turned[(t - 1) % cols], turned[t])
            south = jnp.where(first_sub, above[t], below[t])
            fields[0, t, here, :] = height[t] + east[t] - west + north_v[t] - south
            fields[1, t, here, :] = east[t]
            fields[2, t, here, :] = north_v[t]
        return tuple(below)

    def step(_, carry):
        lax.fori_loop(first, last, group, tuple(jnp.zeros((ROWS8, LANES), F32) for _ in range(cols)), unroll=2)
        return carry

    lax.fori_loop(0, number, step, 0)


def route_kernel(dims, state, depth, innov, weight, tile, count, obs_row, obs_col, fields_out, recv_out, count_out,
                 fields, send, recv, east_pack, west_pack, east_got, west_got,
                 load_sem, row_sem, pack_sem, corner_sem, a2a_sem, own_sem, store_sem):
    rows, cols, lat, lon, blocks = dims
    tiles = cols // LANES
    ext = rows + 2 * HALO
    total = fields.shape[2]
    my_lat, my_lon = lax.axis_index("lat"), lax.axis_index("lon")
    east, west = lax.rem(my_lon + 1, lon), lax.rem(my_lon + lon - 1, lon)
    has_north, has_south = my_lat < lat - 1, my_lat > 0

    loads = []
    for t in range(tiles):
        span = pl.ds(t * LANES, LANES)
        for source, start, number in ((state, 0, 3), (depth, 3, 2)):
            loads.append(pltpu.make_async_copy(
                source.at[:, :, span], fields.at[pl.ds(start, number), t, pl.ds(HALO, rows), :], load_sem.at[len(loads)]))
    for load in loads:
        load.start()

    barrier = pltpu.get_barrier_semaphore()

    def greet(index, carry):
        pl.semaphore_signal(barrier, inc=1, device_id=(my_lat, shift_to(my_lon, index, lon)), device_id_type=MESH)
        return carry

    for has, where in ((has_north, my_lat + 1), (has_south, my_lat - 1)):
        @pl.when(has)
        def _():
            for column in (west, my_lon, east):
                pl.semaphore_signal(barrier, inc=1, device_id=(where, column), device_id_type=MESH)
    lax.fori_loop(1, lon, greet, 0)

    slots = innov.shape[1]
    live = lane_ids((blocks, slots)) < count[...]
    masked = jnp.where(live, innov[...], 0.0)
    cell = jnp.where(live, obs_row[...] * cols + obs_col[...] + 1, 0).astype(F32)
    data = jnp.concatenate([weight[:, k, :] * masked for k in range(4)] + [cell], axis=0)
    named = jnp.where(tile[...] == lane_ids((blocks, lon)), 1.0, 0.0).astype(F32)
    earlier = (lax.broadcasted_iota(I32, (blocks, blocks), 0) > lane_ids((blocks, blocks))).astype(F32)
    before = jnp.dot(earlier.astype(BF16), named.astype(BF16), preferred_element_type=F32)
    rank = jnp.sum(before * named, axis=1, keepdims=True)
    place = tile[...].astype(F32) * CAP + rank
    wide = (blocks, PIECES * blocks)
    ids = lane_ids(wide)
    row_of = jnp.where(lax.broadcasted_iota(I32, wide, 0) == ids % blocks, place * ROWS8 + (ids // blocks).astype(F32), 0.0)
    row_of = jnp.sum(row_of, axis=0, keepdims=True)
    pick = lax.broadcasted_iota(I32, (CAP * lon * ROWS8, PIECES * blocks), 0).astype(F32) == row_of
    pick = jnp.where(pick, 1.0, 0.0).astype(BF16)
    high = data.astype(BF16)
    rest = data - high.astype(F32)
    mid = rest.astype(BF16)
    low = (rest - mid.astype(F32)).astype(BF16)
    sent = (jnp.dot(pick, high, preferred_element_type=F32) + jnp.dot(pick, mid, preferred_element_type=F32)
            + jnp.dot(pick, low, preferred_element_type=F32))
    send[...] = sent.reshape(CAP * lon, ROWS8, slots)[:, :PIECES, :]

    zero_rows = jnp.zeros((5, tiles, HALO, LANES), F32)
    fields[:, :, pl.ds(ext, total - ext), :] = jnp.zeros((5, tiles + 1, total - ext, LANES), F32)

    @pl.when(jnp.logical_not(has_south))
    def _():
        fields[:, pl.ds(0, tiles), pl.ds(0, HALO), :] = zero_rows
        east_got[pl.ds(0, HALO), :] = zero_rows[0, 0]
        west_got[pl.ds(0, HALO), :] = zero_rows[0, 0]

    @pl.when(jnp.logical_not(has_north))
    def _():
        fields[:, pl.ds(0, tiles), pl.ds(HALO + rows, HALO), :] = zero_rows
        east_got[pl.ds(HALO + rows, HALO), :] = zero_rows[0, 0]
        west_got[pl.ds(HALO + rows, HALO), :] = zero_rows[0, 0]

    for load in loads:
        load.wait()

    @pl.when(jnp.logical_not(has_north))
    def _():
        wall = pl.ds(HALO + rows - ROWS8, ROWS8)
        keep = lax.broadcasted_iota(I32, (tiles, ROWS8, LANES), 1) < ROWS8 - 1
        fields[4, pl.ds(0, tiles), wall, :] = jnp.where(keep, fields[4, pl.ds(0, tiles), wall, :], 0.0)

    lane = lane_ids((ROWS8, LANES))

    def pack(index, carry):
        base = pl.multiple_of(index * ROWS8, ROWS8)
        here = pl.ds(HALO + base, ROWS8)
        to_west = jnp.zeros((ROWS8, LANES), F32)
        to_east = to_west
        for f in range(5):
            first = HALO * f
            inside = jnp.logical_and(lane >= first, lane < first + HALO)
            to_west = jnp.where(inside, pltpu.roll(fields[f, 0, here, :], first, 1) if f else fields[f, 0, here, :], to_west)
            first = (LANES - HALO + HALO * f) % LANES
            inside = jnp.logical_and(lane >= first, lane < first + HALO)
            value = fields[f, tiles - 1, here, :]
            to_east = jnp.where(inside, pltpu.roll(value, HALO * f, 1) if f else value, to_east)
        west_pack[pl.ds(base, ROWS8), :] = to_west
        east_pack[pl.ds(base, ROWS8), :] = to_east
        return carry

    lax.fori_loop(0, rows // ROWS8, pack, 0, unroll=2)

    number = lon - 1 + 3 * has_north.astype(I32) + 3 * has_south.astype(I32)
    pl.semaphore_wait(barrier, number)

    def remote(source, target, sems, where):
        return pltpu.make_async_remote_copy(src_ref=source, dst_ref=target, send_sem=sems.at[0], recv_sem=sems.at[1],
                                            device_id=where, device_id_type=MESH)

    main = pl.ds(HALO, rows)
    low_rows, high_rows = pl.ds(0, HALO), pl.ds(HALO + rows, HALO)
    inner = pl.ds(0, tiles)
    to_north = remote(fields.at[:, inner, pl.ds(rows, HALO), :], fields.at[:, inner, low_rows, :], row_sem.at[0], (my_lat + 1, my_lon))
    to_south = remote(fields.at[:, inner, pl.ds(HALO, HALO), :], fields.at[:, inner, high_rows, :], row_sem.at[1], (my_lat - 1, my_lon))
    to_east = remote(east_pack, west_got.at[main], pack_sem.at[0], (my_lat, east))
    to_west = remote(west_pack, east_got.at[main], pack_sem.at[1], (my_lat, west))
    tail = pl.ds(rows - HALO, HALO)
    north_east = remote(east_pack.at[tail], west_got.at[low_rows], corner_sem.at[0], (my_lat + 1, east))
    north_west = remote(west_pack.at[tail], east_got.at[low_rows], corner_sem.at[1], (my_lat + 1, west))
    south_east = remote(east_pack.at[low_rows], west_got.at[high_rows], corner_sem.at[2], (my_lat - 1, east))
    south_west = remote(west_pack.at[low_rows], east_got.at[high_rows], corner_sem.at[3], (my_lat - 1, west))
    northward, southward = (to_north, north_east, north_west), (to_south, south_east, south_west)

    @pl.when(has_north)
    def _():
        for copy in northward:
            copy.start()

    @pl.when(has_south)
    def _():
        for copy in southward:
            copy.start()

    to_east.start()
    to_west.start()

    def block_copy(index):
        where = shift_to(my_lon, index, lon)
        return remote(send.at[pl.ds(CAP * where, CAP)], recv.at[pl.ds(CAP * my_lon, CAP)], a2a_sem, (my_lat, where))

    def send_blocks(index, carry):
        block_copy(index).start()
        return carry

    lax.fori_loop(1, lon, send_blocks, 0)
    mine = pl.ds(CAP * my_lon, CAP)
    own = pltpu.make_async_copy(send.at[mine], recv.at[mine], own_sem)
    own.start()

    @pl.when(has_south)
    def _():
        for copy in northward:
            copy.wait_recv()

    @pl.when(has_north)
    def _():
        for copy in southward:
            copy.wait_recv()

    to_east.wait_recv()
    to_west.wait_recv()

    def unpack(index, carry):
        here = pl.ds(pl.multiple_of(index * ROWS8, ROWS8), ROWS8)
        from_east, from_west = east_got[here, :], west_got[here, :]
        for f in range(5):
            first = HALO * f
            right = jnp.logical_and(lane >= first, lane < first + HALO)
            first = (LANES - HALO + HALO * f) % LANES
            left = jnp.logical_and(lane >= first, lane < first + HALO)
            both = jnp.where(right, from_east, jnp.where(left, from_west, 0.0))
            fields[f, tiles, here, :] = pltpu.roll(both, LANES - HALO * f, 1) if f else both
        return carry

    lax.fori_loop(0, ext // ROWS8, unpack, 0, unroll=2)

    @pl.when(has_north)
    def _():
        for copy in northward:
            copy.wait_send()

    @pl.when(has_south)
    def _():
        for copy in southward:
            copy.wait_send()

    to_east.wait_send()
    to_west.wait_send()

    steps(fields, tiles, 0, ext // ROWS8, 8)
    steps(fields, tiles, 1, ext // ROWS8 - 1, HALF - 8)
    stores = [pltpu.make_async_copy(fields, fields_out, store_sem.at[0])]
    stores[0].start()

    own.wait()
    others = pl.ds(0, CAP * (lon - 1))
    every = pltpu.make_async_remote_copy(src_ref=send.at[others], dst_ref=recv.at[others], send_sem=a2a_sem.at[0],
                                         recv_sem=a2a_sem.at[1], device_id=(my_lat, east), device_id_type=MESH)
    every.wait_recv()
    stores.append(pltpu.make_async_copy(recv, recv_out, store_sem.at[1]))
    stores[1].start()
    filled = jnp.where(recv[:, PIECES - 1, :] > 0.0, 1.0, 0.0).astype(BF16)
    ones = jnp.ones((ROWS8, slots), BF16)
    live_of = lax.dot_general(ones, filled, (((1,), (1,)), ((), ())), preferred_element_type=F32)
    count_out[...] = live_of.astype(I32)
    every.wait_send()
    for store in stores:
        store.wait()


def spread_kernel(dims, counts, recv, out, packed, total):
    rows, cols, lat, lon, blocks = dims
    tiles = cols // LANES
    segments = CAP * lon
    lane = lane_ids((PIECES, LANES))

    def append(segment, carry):
        fill, current = carry
        number = counts[0, segment]
        chunk = fill // LANES
        shift = fill - chunk * LANES
        turned = pltpu.roll(recv[segment], shift, 1)
        current = jnp.where(lane >= shift, turned, current)
        packed[chunk] = current
        fill = fill + number
        current = jnp.where(fill // LANES > chunk, turned, current)
        return fill, current

    zero = jnp.zeros((PIECES, LANES), F32)
    fill, current = lax.fori_loop(0, segments, append, (jnp.int32(0), zero), unroll=4)
    chunk = fill // LANES
    packed[chunk] = jnp.where(lane < fill - chunk * LANES, current, 0.0)
    for extra in range(1, GROUP):
        packed[chunk + extra] = zero
    total[...] = jnp.zeros_like(total)
    groups = (fill + GROUP * LANES - 1) // (GROUP * LANES)

    depth = GROUP * LANES
    row_ids = lax.broadcasted_iota(I32, (rows, depth), 0)
    col_ids = lax.broadcasted_iota(I32, (cols, depth), 0)

    def add_group(index, carry):
        part = [packed[index * GROUP + j] for j in range(GROUP)]
        both = jnp.concatenate(part, axis=1)
        cell = both[PIECES - 1:, :].astype(I32) - 1
        row_at = cell // cols
        col_at = cell - row_at * cols
        here = row_ids == row_at
        past = row_ids == row_at + 1
        column = jnp.where(col_ids == col_at, 1.0, 0.0).astype(BF16)
        high = both[:4, :].astype(BF16).astype(F32)
        low = both[:4, :] - high

        def side(value, k):
            return jnp.where(here, value[k:k + 1, :], jnp.where(past, value[k + 2:k + 3, :], 0.0)).astype(BF16)

        left = jnp.concatenate([side(high, 0), side(low, 0)], axis=1)
        right = jnp.concatenate([side(high, 1), side(low, 1)], axis=1)
        both_sides = jnp.concatenate([left, right], axis=0)
        columns = jnp.concatenate([column, column], axis=1)
        total[...] += lax.dot_general(both_sides, columns, (((1,), (1,)), ((), ())), preferred_element_type=F32)
        return carry

    lax.fori_loop(0, groups, add_group, 0)

    lane = lane_ids((rows, LANES))
    turned = [pltpu.roll(total[pl.ds(rows, rows), pl.ds(t * LANES, LANES)], 1, 1) for t in range(tiles)]
    for t in range(tiles):
        before = turned[t - 1] if t else jnp.zeros((rows, LANES), F32)
        out[t] = total[pl.ds(0, rows), pl.ds(t * LANES, LANES)] + jnp.where(lane == 0, before, turned[t])


def finish_kernel(dims, fields_in, forcing, out, fields, east_pack, west_pack, east_got, west_got, south_got, north_got,
                  load_sem, row_sem, pack_sem, corner_sem, store_sem):
    rows, cols, lat, lon, blocks = dims
    tiles = cols // LANES
    ext = rows + 2 * HALO
    my_lat, my_lon = lax.axis_index("lat"), lax.axis_index("lon")
    east, west = lax.rem(my_lon + 1, lon), lax.rem(my_lon + lon - 1, lon)
    has_north, has_south = my_lat < lat - 1, my_lat > 0

    load = pltpu.make_async_copy(fields_in, fields, load_sem)
    load.start()
    barrier = pltpu.get_barrier_semaphore()
    for has, where in ((has_north, my_lat + 1), (has_south, my_lat - 1)):
        @pl.when(has)
        def _():
            for column in (west, my_lon, east):
                pl.semaphore_signal(barrier, inc=1, device_id=(where, column), device_id_type=MESH)
    for column in (west, east):
        pl.semaphore_signal(barrier, inc=1, device_id=(my_lat, column), device_id_type=MESH)

    run = rows // 8
    lane = lane_ids((run, LANES))
    to_west = jnp.zeros((run, LANES), F32)
    to_east = to_west
    for g in range(8):
        here = pl.ds(run * g, run)
        inside = lane // FRINGE == g
        value = forcing[0, here, :]
        to_west = jnp.where(inside, pltpu.roll(value, FRINGE * g, 1) if g else value, to_west)
        value = forcing[tiles - 1, here, :]
        to_east = jnp.where(inside, pltpu.roll(value, (FRINGE * (g + 1)) % LANES, 1) if g < 7 else value, to_east)
    west_pack[pl.ds(0, run), :] = to_west
    east_pack[pl.ds(0, run), :] = to_east
    ends = (pl.ds(0, FRINGE), pl.ds(rows - FRINGE, FRINGE))
    for at, here in zip((run, run + FRINGE), ends):
        west_pack[pl.ds(at, FRINGE), :] = forcing[0, here, :]
        east_pack[pl.ds(at, FRINGE), :] = forcing[tiles - 1, here, :]

    number = 2 + 3 * has_north.astype(I32) + 3 * has_south.astype(I32)
    pl.semaphore_wait(barrier, number)

    def remote(source, target, sems, where):
        return pltpu.make_async_remote_copy(src_ref=source, dst_ref=target, send_sem=sems.at[0], recv_sem=sems.at[1],
                                            device_id=where, device_id_type=MESH)

    strip, low_end, high_end = pl.ds(0, run), pl.ds(run, FRINGE), pl.ds(run + FRINGE, FRINGE)
    to_north = remote(forcing.at[:, ends[1], :], south_got, row_sem.at[0], (my_lat + 1, my_lon))
    to_south = remote(forcing.at[:, ends[0], :], north_got, row_sem.at[1], (my_lat - 1, my_lon))
    go_east = remote(east_pack.at[strip], west_got.at[strip], pack_sem.at[0], (my_lat, east))
    go_west = remote(west_pack.at[strip], east_got.at[strip], pack_sem.at[1], (my_lat, west))
    north_east = remote(east_pack.at[high_end], west_got.at[low_end], corner_sem.at[0], (my_lat + 1, east))
    north_west = remote(west_pack.at[high_end], east_got.at[low_end], corner_sem.at[1], (my_lat + 1, west))
    south_east = remote(east_pack.at[low_end], west_got.at[high_end], corner_sem.at[2], (my_lat - 1, east))
    south_west = remote(west_pack.at[low_end], east_got.at[high_end], corner_sem.at[3], (my_lat - 1, west))
    northward, southward = (to_north, north_east, north_west), (to_south, south_east, south_west)

    @pl.when(has_north)
    def _():
        for copy in northward:
            copy.start()

    @pl.when(has_south)
    def _():
        for copy in southward:
            copy.start()

    go_east.start()
    go_west.start()

    load.wait()
    fields[0, pl.ds(0, tiles), pl.ds(HALO, rows), :] += forcing[...]

    @pl.when(has_south)
    def _():
        for copy in northward:
            copy.wait_recv()
        at = pl.ds(HALO - FRINGE, FRINGE)
        fields[0, pl.ds(0, tiles), at, :] += south_got[...]

    @pl.when(has_north)
    def _():
        for copy in southward:
            copy.wait_recv()
        at = pl.ds(HALO + rows, FRINGE)
        fields[0, pl.ds(0, tiles), at, :] += north_got[...]

    go_east.wait_recv()
    go_west.wait_recv()
    right = lane < FRINGE
    left = lane >= LANES - FRINGE
    from_east, from_west = east_got[strip, :], west_got[strip, :]
    for g in range(8):
        here = pl.ds(HALO + run * g, run)
        one = pltpu.roll(from_east, (LANES - FRINGE * g) % LANES, 1) if g else from_east
        two = pltpu.roll(from_west, (LANES - FRINGE * (g + 1)) % LANES, 1) if g < 7 else from_west
        fields[0, tiles, here, :] += jnp.where(right, one, jnp.where(left, two, 0.0))
    lane = lane_ids((FRINGE, LANES))
    right = lane < FRINGE
    left = lane >= LANES - FRINGE
    for has, end, at in ((has_south, low_end, HALO - FRINGE), (has_north, high_end, HALO + rows)):
        @pl.when(has)
        def _():
            fields[0, tiles, pl.ds(at, FRINGE), :] += jnp.where(right, east_got[end, :], jnp.where(left, west_got[end, :], 0.0))

    steps(fields, tiles, 1, ext // ROWS8 - 1, 4)
    steps(fields, tiles, 2, ext // ROWS8 - 2, HALF - 4)
    stores = []
    for t in range(tiles):
        store = pltpu.make_async_copy(fields.at[pl.ds(0, 3), t, pl.ds(HALO, rows), :],
                                      out.at[:, :, pl.ds(t * LANES, LANES)], store_sem.at[t])
        store.start()
        stores.append(store)

    @pl.when(has_north)
    def _():
        for copy in northward:
            copy.wait_send()

    @pl.when(has_south)
    def _():
        for copy in southward:
            copy.wait_send()

    go_east.wait_send()
    go_west.wait_send()
    for store in stores:
        store.wait()


def per_device(lat, lon, adjoint_state, face_depth, innovation, interp_weight, block_tile, block_count, obs_row, obs_col):
    rows, cols = adjoint_state.shape[1:]
    blocks, slots = innovation.shape
    tiles = cols // LANES
    dims = (rows, cols, lat, lon, blocks)
    ext = rows + 2 * HALO
    total = ext + ROWS8
    segments = CAP * lon
    vmem = pl.BlockSpec(memory_space=pltpu.VMEM)
    anywhere = pl.BlockSpec(memory_space=pl.ANY)
    dma = pltpu.SemaphoreType.DMA
    fields_shape = (5, tiles + 1, total, LANES)
    fields, recv, counts = pl.pallas_call(
        functools.partial(route_kernel, dims),
        name="route",
        out_shape=(
            jax.ShapeDtypeStruct(fields_shape, F32),
            jax.ShapeDtypeStruct((segments, PIECES, slots), F32),
            jax.ShapeDtypeStruct((ROWS8, segments), I32),
        ),
        in_specs=[anywhere] * 2 + [vmem] * 6,
        out_specs=(anywhere, anywhere, vmem),
        scratch_shapes=[
            pltpu.VMEM(fields_shape, F32),
            pltpu.VMEM((segments, PIECES, slots), F32),
            pltpu.VMEM((segments, PIECES, slots), F32),
            pltpu.VMEM((rows, LANES), F32),
            pltpu.VMEM((rows, LANES), F32),
            pltpu.VMEM((ext, LANES), F32),
            pltpu.VMEM((ext, LANES), F32),
            dma((2 * tiles,)), dma((2, 2)), dma((2, 2)), dma((4, 2)), dma((2,)), dma, dma((2,)),
        ],
        compiler_params=pltpu.CompilerParams(collective_id=0, has_side_effects=True, vmem_limit_bytes=32 << 20),
    )(adjoint_state, face_depth, innovation, interp_weight, block_tile, block_count, obs_row, obs_col)
    forcing = pl.pallas_call(
        functools.partial(spread_kernel, dims),
        name="spread",
        out_shape=jax.ShapeDtypeStruct((tiles, rows, LANES), F32),
        in_specs=[pl.BlockSpec(memory_space=pltpu.SMEM), vmem],
        out_specs=vmem,
        scratch_shapes=[
            pltpu.VMEM((segments + GROUP, PIECES, LANES), F32),
            pltpu.VMEM((2 * rows, cols), F32),
        ],
        compiler_params=pltpu.CompilerParams(vmem_limit_bytes=32 << 20),
    )(counts, recv)
    run = rows // 8 + 2 * FRINGE
    return pl.pallas_call(
        functools.partial(finish_kernel, dims),
        name="finish",
        out_shape=jax.ShapeDtypeStruct((3, rows, cols), F32),
        in_specs=[anywhere, vmem],
        out_specs=anywhere,
        scratch_shapes=[
            pltpu.VMEM(fields_shape, F32),
            pltpu.VMEM((run, LANES), F32),
            pltpu.VMEM((run, LANES), F32),
            pltpu.VMEM((run, LANES), F32),
            pltpu.VMEM((run, LANES), F32),
            pltpu.VMEM((tiles, FRINGE, LANES), F32),
            pltpu.VMEM((tiles, FRINGE, LANES), F32),
            dma, dma((2, 2)), dma((2, 2)), dma((4, 2)), dma((tiles,)),
        ],
        compiler_params=pltpu.CompilerParams(collective_id=1, has_side_effects=True, vmem_limit_bytes=32 << 20),
    )(fields, forcing)


def solution(mesh):
    return jax.shard_map(
        functools.partial(per_device, mesh.shape["lat"], mesh.shape["lon"]),
        mesh=mesh,
        in_specs=(
            P(None, "lat", "lon"),
            P(None, "lat", "lon"),
            P(("lat", "lon"), None),
            P(("lat", "lon"), None, None),
            P(("lat", "lon"), None),
            P(("lat", "lon"), None),
            P(("lat", "lon"), None),
            P(("lat", "lon"), None),
        ),
        out_specs=P(None, "lat", "lon"),
        check_vma=False,
    )
```

time: 670 us -> 132 us (0.20)
  the two profiles are of different devices: /device:TPU:1 before, /device:TPU:33 now
where the time goes in v1:
time: 132 us; the launch traced here: 131 us
  Pallas kernels  123 us (93%)
  local copies, waits for them, and re-layouts  8.24 us (6%)
    pallas_call x1, Pallas kernels, per_device(): pl.pallas_call(functools.partial(route_kernel, dims), name='route', out_s...  62.6 us
    pallas_call x1, Pallas kernels, per_device(): pl.pallas_call(functools.partial(finish_kernel, dims), name='finish', out...  53.8 us
    unnamed x15, local copies, waits for them, and re-layouts  8.24 us
    pallas_call x1, Pallas kernels, per_device(): pl.pallas_call(functools.partial(spread_kernel, dims), name='spread', out...  6.5 us

profile of v1, /device:TPU:33, one launch (start us, length us, event | category | flops | bytes accessed | tf_op | source)
XLA Modules:
  0.0 131.1 jit_solution(10937272976710338447)
XLA Ops:
  0.0 0.7 copy.9.tile
  0.7 0.7 copy.10.count
  1.5 0.0 copy-start
  1.5 1.4 %copy-done = f32[3,256,512]{2,1,0:T(8,128)S(1)} copy-done((f32[3,256,512]{2,1,0:T(8,128)S(1)}, f32[3,256,512]{2,1,0:T(8,128)}, u32[]{:S(2)}) %copy-start) | copy-done | bytes 1572888
  2.9 0.0 copy-start.1
  2.9 1.2 copy-done.1
  4.1 0.0 copy-start.2
  4.1 0.8 copy-done.2
  4.9 0.0 copy-start.3
  4.9 0.7 copy-done.3
  5.7 0.0 copy-start.4
  5.7 0.7 copy-done.4
  6.4 0.0 copy-start.5
  6.4 0.7 copy-done.5
  7.1 62.6 %route.1 = (f32[5,5,312,128]{3,2,1,0:T(8,128)S(1)}, f32[128,5,128]{2,1,0:T(8,128)S(1)}, s32[8,128]{1,0:T(8,128)S(1)}) custom-call(f32[3,256,512]{2,1,0:T(8,128)S(1)} %copy-done, f32[2,256,512]{2,1,0:T(8,128)S(1)} %copy-done.1, f32[32,128]{1,0:T(8,128)S(1)} %copy-done.3, f32[32,4,128]{2,1,0:T(4,128)S(1)} %copy-done.2, s32[32,1]{1,0:T(8,128)S(1)} %copy.9.tile, ...), custom_call_target="tpu_custom_call" | custom-call | tf_op jit(solution)/shard_map/route/pallas_call | solution.py:487
  69.7 6.5 %spread.1.forcing = f32[4,256,128]{2,1,0:T(8,128)S(1)} custom-call(s32[8,128]{1,0:T(8,128)S(1)} %get-tuple-element.9.counts, f32[128,5,128]{2,1,0:T(8,128)S(1)} %get-tuple-element.10.recv), custom_call_target="tpu_custom_call" | custom-call | tf_op jit(solution)/shard_map/spread/pallas_call | solution.py:509
  76.2 53.8 %finish.1 = f32[3,256,512]{2,1,0:T(8,128)S(1)} custom-call(f32[5,5,312,128]{3,2,1,0:T(8,128)S(1)} %get-tuple-element.8.fields_in, f32[4,256,128]{2,1,0:T(8,128)S(1)} %spread.1.forcing), custom_call_target="tpu_custom_call" | custom-call | tf_op jit(solution)/shard_map/finish/pallas_call | solution.py:522
  130.0 1.1 copy.12
Async XLA Ops:
  1.5 1.4 %copy-start = (f32[3,256,512]{2,1,0:T(8,128)S(1)}, f32[3,256,512]{2,1,0:T(8,128)}, u32[]{:S(2)}) copy-start(f32[3,256,512]{2,1,0:T(8,128)} %state.1) | copy-start | bytes 4718596
  2.9 1.2 copy-start.1
  4.1 0.8 copy-start.2
  4.9 0.7 copy-start.3
  5.7 0.7 copy-start.4
  6.4 0.7 copy-start.5

commit v2 on v1

--- a/solution.py
+++ b/solution.py
@@ -36,58 +36,103 @@
     return (z * 4 + y) * 2 + x
 
 
-def steps(fields, tiles, first, last, number):
-    cols = tiles + 1
+def columns_at(width):
+    part = LANES // width
     lane = lane_ids((ROWS8, LANES))
-    sub = lax.broadcasted_iota(I32, (ROWS8, LANES), 0)
-    last_lane = lane == LANES - 1
-    first_lane = lane == 0
-    first_sub = sub == 0
-
-    def group(index, above):
-        base = pl.multiple_of(index * ROWS8, ROWS8)
-        here = pl.ds(base, ROWS8)
-        north = pl.ds(base + 1, ROWS8)
-        height = [fields[0, t, here, :] for t in range(cols)]
-        height_n = [fields[0, t, north, :] for t in range(cols)]
-        turned = [pltpu.roll(x, LANES - 1, 1) for x in height]
-        height_e = [jnp.where(last_lane, turned[(t + 1) % cols], turned[t]) for t in range(cols)]
-        east = [fields[1, t, here, :] + fields[3, t, here, :] * (height_e[t] - height[t]) for t in range(cols)]
-        north_v = [fields[2, t, here, :] + fields[4, t, here, :] * (height_n[t] - height[t]) for t in range(cols)]
-        turned = [pltpu.roll(x, 1, 1) for x in east]
-        below = [pltpu.roll(x, 1, 0) for x in north_v]
-        for t in range(cols):
-            west = jnp.where(first_lane, turned[(t - 1) % cols], turned[t])
-            south = jnp.where(first_sub, above[t], below[t])
-            fields[0, t, here, :] = height[t] + east[t] - west + north_v[t] - south
-            fields[1, t, here, :] = east[t]
-            fields[2, t, here, :] = north_v[t]
-        return tuple(below)
-
-    def step(_, carry):
-        lax.fori_loop(first, last, group, tuple(jnp.zeros((ROWS8, LANES), F32) for _ in range(cols)), unroll=2)
-        return carry
-
-    lax.fori_loop(0, number, step, 0)
-
-
-def route_kernel(dims, state, depth, innov, weight, tile, count, obs_row, obs_col, fields_out, recv_out, count_out,
-                 fields, send, recv, east_pack, west_pack, east_got, west_got,
-                 load_sem, row_sem, pack_sem, corner_sem, a2a_sem, own_sem, store_sem):
+    part_of, inside = lane // part, lane % part
+    cuts = [(width * part * t - HALO) % LANES for t in range(width)]
+    into = [(width * part * t - HALO + LANES + width * inside + (part_of + width - t) % width) % LANES for t in range(width)]
+    turn = [part * ((part_of + c) % width) + inside for c in range(width)]
+    back = [part * ((part_of + width - c) % width) + inside for c in range(width)]
+    out = []
+    for t in range(width):
+        along = (lane + LANES - cuts[t]) % LANES
+        out.append(jnp.minimum(part * ((along + t) % width) + along // width, LANES - 1))
+    return lane, part_of, cuts, into, turn, back, out
+
+
+def take(values, index):
+    return jnp.take_along_axis(values, index, axis=1)
+
+
+def by_part(part_of, choices):
+    value = choices[-1]
+    for p in range(len(choices) - 1):
+        value = jnp.where(part_of == p, choices[p], value)
+    return value
+
+
+def to_runs(maps, values):
+    lane, part_of, cuts, into, turn, back, out = maps
+    width = len(values)
+    sorted_ = [take(jnp.where(lane >= cuts[t], values[t - 1], values[t]), into[t]) for t in range(width)]
+    mixed = [by_part(part_of, [sorted_[(p - c) % width] for p in range(width)]) for c in range(width)]
+    return [take(mixed[c], turn[c]) if c else mixed[c] for c in range(width)]
+
+
+def from_runs(maps, values):
+    lane, part_of, cuts, into, turn, back, out = maps
+    width = len(values)
+    mixed = [take(values[c], back[c]) if c else values[c] for c in range(width)]
+    sorted_ = [by_part(part_of, [mixed[(p - t) % width] for p in range(width)]) for t in range(width)]
+    windows = [take(sorted_[t], out[t]) for t in range(width)]
+    return [jnp.where(lane < cuts[t + 1], windows[t], windows[t + 1]) for t in range(width - 1)]
+
+
+def one_step(old, new, east_vel, north_vel, depth_east, depth_north):
+    width, number = east_vel.shape[:2]
+    cols = range(width)
+    for c in cols:
+        old[c, number] = pltpu.roll(old[c, 0], ROWS8 - 1, 0)
+    end = number - 1
+    south = [pltpu.roll(north_vel[c, end] + depth_north[c, end] * (old[c, number] - old[c, end]), 1, 0) for c in cols]
+    for k in range(number):
+        height = [old[c, k] for c in cols]
+        height_e = height[1:] + [pltpu.roll(height[0], LANES - 1, 1)]
+        east = [None] * width
+        for c in [width - 1] + list(range(width - 1)):
+            east[c] = east_vel[c, k] + depth_east[c, k] * (height_e[c] - height[c])
+        west = [pltpu.roll(east[-1], 1, 1)] + east[:-1]
+        north = [None] * width
+        for c in cols:
+            north[c] = north_vel[c, k] + depth_north[c, k] * (old[c, k + 1] - height[c])
+            new[c, k] = height[c] + (east[c] - west[c]) + (north[c] - south[c])
+            east_vel[c, k] = east[c]
+            north_vel[c, k] = north[c]
+        south = north
+
+
+def steps(number, height, other, *rest):
+    def two(_, carry):
+        one_step(height, other, *rest)
+        one_step(other, height, *rest)
+        return carry
+
+    lax.fori_loop(0, number // 2, two, 0)
+
+
+def route_kernel(dims, state, depth, innov_in, weight_in, tile_in, count_in, row_in, col_in, fields_out, recv_out, count_out,
+                 fields, height, other, east_vel, north_vel, depth_east, depth_north,
+                 innov, weight, tile_row, count_row, obs_row, obs_col, send, recv, east_pack, west_pack, east_got, west_got,
+                 load_sem, small_sem, row_sem, pack_sem, corner_sem, a2a_sem, own_sem, store_sem):
     rows, cols, lat, lon, blocks = dims
     tiles = cols // LANES
     ext = rows + 2 * HALO
-    total = fields.shape[2]
+    number = ext // ROWS8
     my_lat, my_lon = lax.axis_index("lat"), lax.axis_index("lon")
     east, west = lax.rem(my_lon + 1, lon), lax.rem(my_lon + lon - 1, lon)
     has_north, has_south = my_lat < lat - 1, my_lat > 0
 
+    small = [pltpu.make_async_copy(source, target, small_sem.at[i]) for i, (source, target) in enumerate((
+        (tile_in, tile_row), (count_in, count_row), (innov_in, innov), (weight_in, weight), (row_in, obs_row), (col_in, obs_col)))]
+    for load in small:
+        load.start()
     loads = []
     for t in range(tiles):
         span = pl.ds(t * LANES, LANES)
-        for source, start, number in ((state, 0, 3), (depth, 3, 2)):
+        for source, start, some in ((state, 0, 3), (depth, 3, 2)):
             loads.append(pltpu.make_async_copy(
-                source.at[:, :, span], fields.at[pl.ds(start, number), t, pl.ds(HALO, rows), :], load_sem.at[len(loads)]))
+                source.at[:, :, span], fields.at[pl.ds(start, some), t, pl.ds(HALO, rows), :], load_sem.at[len(loads)]))
     for load in loads:
         load.start()
 
@@ -104,16 +149,22 @@
                 pl.semaphore_signal(barrier, inc=1, device_id=(where, column), device_id_type=MESH)
     lax.fori_loop(1, lon, greet, 0)
 
+    for load in small:
+        load.wait()
     slots = innov.shape[1]
-    live = lane_ids((blocks, slots)) < count[...]
+    square = (blocks, blocks)
+    diagonal = lax.broadcasted_iota(I32, square, 0) == lane_ids(square)
+    tile = jnp.sum(jnp.where(diagonal, tile_row[...].astype(F32), 0.0), axis=1, keepdims=True)
+    count = jnp.sum(jnp.where(diagonal, count_row[...].astype(F32), 0.0), axis=1, keepdims=True)
+    live = lane_ids((blocks, slots)).astype(F32) < count
     masked = jnp.where(live, innov[...], 0.0)
     cell = jnp.where(live, obs_row[...] * cols + obs_col[...] + 1, 0).astype(F32)
     data = jnp.concatenate([weight[:, k, :] * masked for k in range(4)] + [cell], axis=0)
-    named = jnp.where(tile[...] == lane_ids((blocks, lon)), 1.0, 0.0).astype(F32)
-    earlier = (lax.broadcasted_iota(I32, (blocks, blocks), 0) > lane_ids((blocks, blocks))).astype(F32)
+    named = jnp.where(tile == lane_ids((blocks, lon)).astype(F32), 1.0, 0.0)
+    earlier = jnp.where(lax.broadcasted_iota(I32, square, 0) > lane_ids(square), 1.0, 0.0)
     before = jnp.dot(earlier.astype(BF16), named.astype(BF16), preferred_element_type=F32)
     rank = jnp.sum(before * named, axis=1, keepdims=True)
-    place = tile[...].astype(F32) * CAP + rank
+    place = tile * CAP + rank
     wide = (blocks, PIECES * blocks)
     ids = lane_ids(wide)
     row_of = jnp.where(lax.broadcasted_iota(I32, wide, 0) == ids % blocks, place * ROWS8 + (ids // blocks).astype(F32), 0.0)
@@ -129,7 +180,6 @@
     send[...] = sent.reshape(CAP * lon, ROWS8, slots)[:, :PIECES, :]
 
     zero_rows = jnp.zeros((5, tiles, HALO, LANES), F32)
-    fields[:, :, pl.ds(ext, total - ext), :] = jnp.zeros((5, tiles + 1, total - ext, LANES), F32)
 
     @pl.when(jnp.logical_not(has_south))
     def _():
@@ -173,8 +223,7 @@
 
     lax.fori_loop(0, rows // ROWS8, pack, 0, unroll=2)
 
-    number = lon - 1 + 3 * has_north.astype(I32) + 3 * has_south.astype(I32)
-    pl.semaphore_wait(barrier, number)
+    pl.semaphore_wait(barrier, lon - 1 + 3 * has_north.astype(I32) + 3 * has_south.astype(I32))
 
     def remote(source, target, sems, where):
         return pltpu.make_async_remote_copy(src_ref=source, dst_ref=target, send_sem=sems.at[0], recv_sem=sems.at[1],
@@ -260,18 +309,32 @@
     to_east.wait_send()
     to_west.wait_send()
 
-    steps(fields, tiles, 0, ext // ROWS8, 8)
-    steps(fields, tiles, 1, ext // ROWS8 - 1, HALF - 8)
-    stores = [pltpu.make_async_copy(fields, fields_out, store_sem.at[0])]
-    stores[0].start()
+    refs = (height, east_vel, north_vel, depth_east, depth_north)
+    maps = columns_at(tiles + 1)
+
+    def arrange(k, carry):
+        for f, ref in enumerate(refs):
+            values = to_runs(maps, [fields[f, t, pl.ds(k, ROWS8, stride=number), :] for t in range(tiles + 1)])
+            for c in range(tiles + 1):
+                ref[c, k] = values[c]
+        return carry
+
+    lax.fori_loop(0, number, arrange, 0, unroll=2)
+    inner = pl.ds(0, number)
+    stores = [pltpu.make_async_copy(ref.at[:, inner], fields_out.at[f], store_sem.at[f]) for f, ref in enumerate(refs)]
+    for store in stores[3:]:
+        store.start()
+    steps(HALF, height, other, *refs[1:])
+    for store in stores[:3]:
+        store.start()
 
     own.wait()
     others = pl.ds(0, CAP * (lon - 1))
     every = pltpu.make_async_remote_copy(src_ref=send.at[others], dst_ref=recv.at[others], send_sem=a2a_sem.at[0],
                                          recv_sem=a2a_sem.at[1], device_id=(my_lat, east), device_id_type=MESH)
     every.wait_recv()
-    stores.append(pltpu.make_async_copy(recv, recv_out, store_sem.at[1]))
-    stores[1].start()
+    stores.append(pltpu.make_async_copy(recv, recv_out, store_sem.at[5]))
+    stores[5].start()
     filled = jnp.where(recv[:, PIECES - 1, :] > 0.0, 1.0, 0.0).astype(BF16)
     ones = jnp.ones((ROWS8, slots), BF16)
     live_of = lax.dot_general(ones, filled, (((1,), (1,)), ((), ())), preferred_element_type=F32)
@@ -300,7 +363,7 @@
         return fill, current
 
     zero = jnp.zeros((PIECES, LANES), F32)
-    fill, current = lax.fori_loop(0, segments, append, (jnp.int32(0), zero), unroll=4)
+    fill, current = lax.fori_loop(0, segments, append, (jnp.int32(0), zero), unroll=min(32, segments))
     chunk = fill // LANES
     packed[chunk] = jnp.where(lane < fill - chunk * LANES, current, 0.0)
     for extra in range(1, GROUP):
@@ -343,17 +406,21 @@
         out[t] = total[pl.ds(0, rows), pl.ds(t * LANES, LANES)] + jnp.where(lane == 0, before, turned[t])
 
 
-def finish_kernel(dims, fields_in, forcing, out, fields, east_pack, west_pack, east_got, west_got, south_got, north_got,
-                  load_sem, row_sem, pack_sem, corner_sem, store_sem):
+def finish_kernel(dims, fields_in, forcing_in, out, forcing, height, other, east_vel, north_vel, depth_east, depth_north, done,
+                  east_pack, west_pack, east_got, west_got, load_sem, row_sem, pack_sem, corner_sem, store_sem):
     rows, cols, lat, lon, blocks = dims
     tiles = cols // LANES
     ext = rows + 2 * HALO
+    number = ext // ROWS8
     my_lat, my_lon = lax.axis_index("lat"), lax.axis_index("lon")
     east, west = lax.rem(my_lon + 1, lon), lax.rem(my_lon + lon - 1, lon)
     has_north, has_south = my_lat < lat - 1, my_lat > 0
-
-    load = pltpu.make_async_copy(fields_in, fields, load_sem)
-    load.start()
+    refs = (height, east_vel, north_vel, depth_east, depth_north)
+    inner = pl.ds(0, number)
+    loads = [pltpu.make_async_copy(forcing_in, forcing.at[pl.ds(0, tiles), pl.ds(HALO, rows), :], load_sem.at[5])]
+    loads += [pltpu.make_async_copy(fields_in.at[f], ref.at[:, inner], load_sem.at[f]) for f, ref in enumerate(refs)]
+    for load in loads:
+        load.start()
     barrier = pltpu.get_barrier_semaphore()
     for has, where in ((has_north, my_lat + 1), (has_south, my_lat - 1)):
         @pl.when(has)
@@ -363,12 +430,21 @@
     for column in (west, east):
         pl.semaphore_signal(barrier, inc=1, device_id=(my_lat, column), device_id_type=MESH)
 
+    beyond = HALO - FRINGE
+    for at in (0, ext - beyond):
+        forcing[:, pl.ds(at, beyond), :] = jnp.zeros((tiles + 1, beyond, LANES), F32)
+    for has, at in ((has_south, beyond), (has_north, HALO + rows)):
+        @pl.when(jnp.logical_not(has))
+        def _():
+            forcing[:, pl.ds(at, FRINGE), :] = jnp.zeros((tiles + 1, FRINGE, LANES), F32)
+
+    loads[0].wait()
     run = rows // 8
     lane = lane_ids((run, LANES))
     to_west = jnp.zeros((run, LANES), F32)
     to_east = to_west
     for g in range(8):
-        here = pl.ds(run * g, run)
+        here = pl.ds(HALO + run * g, run)
         inside = lane // FRINGE == g
         value = forcing[0, here, :]
         to_west = jnp.where(inside, pltpu.roll(value, FRINGE * g, 1) if g else value, to_west)
@@ -376,21 +452,22 @@
         to_east = jnp.where(inside, pltpu.roll(value, (FRINGE * (g + 1)) % LANES, 1) if g < 7 else value, to_east)
     west_pack[pl.ds(0, run), :] = to_west
     east_pack[pl.ds(0, run), :] = to_east
-    ends = (pl.ds(0, FRINGE), pl.ds(rows - FRINGE, FRINGE))
+    ends = (pl.ds(HALO, FRINGE), pl.ds(HALO + rows - FRINGE, FRINGE))
+    outer = (pl.ds(HALO - FRINGE, FRINGE), pl.ds(HALO + rows, FRINGE))
     for at, here in zip((run, run + FRINGE), ends):
         west_pack[pl.ds(at, FRINGE), :] = forcing[0, here, :]
         east_pack[pl.ds(at, FRINGE), :] = forcing[tiles - 1, here, :]
 
-    number = 2 + 3 * has_north.astype(I32) + 3 * has_south.astype(I32)
-    pl.semaphore_wait(barrier, number)
+    pl.semaphore_wait(barrier, 2 + 3 * has_north.astype(I32) + 3 * has_south.astype(I32))
 
     def remote(source, target, sems, where):
         return pltpu.make_async_remote_copy(src_ref=source, dst_ref=target, send_sem=sems.at[0], recv_sem=sems.at[1],
                                             device_id=where, device_id_type=MESH)
 
+    main = pl.ds(0, tiles)
     strip, low_end, high_end = pl.ds(0, run), pl.ds(run, FRINGE), pl.ds(run + FRINGE, FRINGE)
-    to_north = remote(forcing.at[:, ends[1], :], south_got, row_sem.at[0], (my_lat + 1, my_lon))
-    to_south = remote(forcing.at[:, ends[0], :], north_got, row_sem.at[1], (my_lat - 1, my_lon))
+    to_north = remote(forcing.at[main, ends[1], :], forcing.at[main, outer[0], :], row_sem.at[0], (my_lat + 1, my_lon))
+    to_south = remote(forcing.at[main, ends[0], :], forcing.at[main, outer[1], :], row_sem.at[1], (my_lat - 1, my_lon))
     go_east = remote(east_pack.at[strip], west_got.at[strip], pack_sem.at[0], (my_lat, east))
     go_west = remote(west_pack.at[strip], east_got.at[strip], pack_sem.at[1], (my_lat, west))
     north_east = remote(east_pack.at[high_end], west_got.at[low_end], corner_sem.at[0], (my_lat + 1, east))
@@ -412,22 +489,18 @@
     go_east.start()
     go_west.start()
 
-    load.wait()
-    fields[0, pl.ds(0, tiles), pl.ds(HALO, rows), :] += forcing[...]
+    for load in loads[1:]:
+        load.wait()
 
     @pl.when(has_south)
     def _():
         for copy in northward:
             copy.wait_recv()
-        at = pl.ds(HALO - FRINGE, FRINGE)
-        fields[0, pl.ds(0, tiles), at, :] += south_got[...]
 
     @pl.when(has_north)
     def _():
         for copy in southward:
             copy.wait_recv()
-        at = pl.ds(HALO + rows, FRINGE)
-        fields[0, pl.ds(0, tiles), at, :] += north_got[...]
 
     go_east.wait_recv()
     go_west.wait_recv()
@@ -438,23 +511,38 @@
         here = pl.ds(HALO + run * g, run)
         one = pltpu.roll(from_east, (LANES - FRINGE * g) % LANES, 1) if g else from_east
         two = pltpu.roll(from_west, (LANES - FRINGE * (g + 1)) % LANES, 1) if g < 7 else from_west
-        fields[0, tiles, here, :] += jnp.where(right, one, jnp.where(left, two, 0.0))
+        forcing[tiles, here, :] = jnp.where(right, one, jnp.where(left, two, 0.0))
     lane = lane_ids((FRINGE, LANES))
     right = lane < FRINGE
     left = lane >= LANES - FRINGE
     for has, end, at in ((has_south, low_end, HALO - FRINGE), (has_north, high_end, HALO + rows)):
         @pl.when(has)
         def _():
-            fields[0, tiles, pl.ds(at, FRINGE), :] += jnp.where(right, east_got[end, :], jnp.where(left, west_got[end, :], 0.0))
-
-    steps(fields, tiles, 1, ext // ROWS8 - 1, 4)
-    steps(fields, tiles, 2, ext // ROWS8 - 2, HALF - 4)
+            forcing[tiles, pl.ds(at, FRINGE), :] = jnp.where(right, east_got[end, :], jnp.where(left, west_got[end, :], 0.0))
+
+    maps = columns_at(tiles + 1)
+
+    def add(k, carry):
+        values = to_runs(maps, [forcing[t, pl.ds(k, ROWS8, stride=number), :] for t in range(tiles + 1)])
+        for c in range(tiles + 1):
+            height[c, k] += values[c]
+        return carry
+
+    lax.fori_loop(0, number, add, 0, unroll=2)
+    steps(HALF, height, other, *refs[1:])
     stores = []
-    for t in range(tiles):
-        store = pltpu.make_async_copy(fields.at[pl.ds(0, 3), t, pl.ds(HALO, rows), :],
-                                      out.at[:, :, pl.ds(t * LANES, LANES)], store_sem.at[t])
-        store.start()
-        stores.append(store)
+    for f in range(3):
+        def leave(k, carry):
+            for t, value in enumerate(from_runs(maps, [refs[f][c, k] for c in range(tiles + 1)])):
+                done[f, t, pl.ds(k, ROWS8, stride=number), :] = value
+            return carry
+
+        lax.fori_loop(0, number, leave, 0, unroll=2)
+        for t in range(tiles):
+            store = pltpu.make_async_copy(done.at[f, t, pl.ds(HALO, rows), :],
+                                          out.at[f, :, pl.ds(t * LANES, LANES)], store_sem.at[f, t])
+            store.start()
+            stores.append(store)
 
     @pl.when(has_north)
     def _():
@@ -478,34 +566,43 @@
     tiles = cols // LANES
     dims = (rows, cols, lat, lon, blocks)
     ext = rows + 2 * HALO
-    total = ext + ROWS8
     segments = CAP * lon
     vmem = pl.BlockSpec(memory_space=pltpu.VMEM)
     anywhere = pl.BlockSpec(memory_space=pl.ANY)
     dma = pltpu.SemaphoreType.DMA
-    fields_shape = (5, tiles + 1, total, LANES)
+    number = ext // ROWS8
+    natural = pltpu.VMEM((5, tiles + 1, ext, LANES), F32)
+    runs = [pltpu.VMEM((tiles + 1, number + 1, ROWS8, LANES), F32)] * 2 + [pltpu.VMEM((tiles + 1, number, ROWS8, LANES), F32)] * 4
+    params = functools.partial(pltpu.CompilerParams, has_side_effects=True, vmem_limit_bytes=56 << 20)
     fields, recv, counts = pl.pallas_call(
         functools.partial(route_kernel, dims),
         name="route",
         out_shape=(
-            jax.ShapeDtypeStruct(fields_shape, F32),
+            jax.ShapeDtypeStruct((5, tiles + 1, number, ROWS8, LANES), F32),
             jax.ShapeDtypeStruct((segments, PIECES, slots), F32),
             jax.ShapeDtypeStruct((ROWS8, segments), I32),
         ),
-        in_specs=[anywhere] * 2 + [vmem] * 6,
+        in_specs=[anywhere] * 8,
         out_specs=(anywhere, anywhere, vmem),
         scratch_shapes=[
-            pltpu.VMEM(fields_shape, F32),
+            natural, *runs,
+            pltpu.VMEM((blocks, slots), F32),
+            pltpu.VMEM((blocks, 4, slots), F32),
+            pltpu.VMEM((1, blocks), I32),
+            pltpu.VMEM((1, blocks), I32),
+            pltpu.VMEM((blocks, slots), I32),
+            pltpu.VMEM((blocks, slots), I32),
             pltpu.VMEM((segments, PIECES, slots), F32),
             pltpu.VMEM((segments, PIECES, slots), F32),
             pltpu.VMEM((rows, LANES), F32),
             pltpu.VMEM((rows, LANES), F32),
             pltpu.VMEM((ext, LANES), F32),
             pltpu.VMEM((ext, LANES), F32),
-            dma((2 * tiles,)), dma((2, 2)), dma((2, 2)), dma((4, 2)), dma((2,)), dma, dma((2,)),
+            dma((2 * tiles,)), dma((6,)), dma((2, 2)), dma((2, 2)), dma((4, 2)), dma((2,)), dma, dma((6,)),
         ],
-        compiler_params=pltpu.CompilerParams(collective_id=0, has_side_effects=True, vmem_limit_bytes=32 << 20),
-    )(adjoint_state, face_depth, innovation, interp_weight, block_tile, block_count, obs_row, obs_col)
+        compiler_params=params(collective_id=0),
+    )(adjoint_state, face_depth, innovation, interp_weight, block_tile.reshape(1, blocks), block_count.reshape(1, blocks),
+      obs_row, obs_col)
     forcing = pl.pallas_call(
         functools.partial(spread_kernel, dims),
         name="spread",
@@ -516,26 +613,26 @@
             pltpu.VMEM((segments + GROUP, PIECES, LANES), F32),
             pltpu.VMEM((2 * rows, cols), F32),
         ],
-        compiler_params=pltpu.CompilerParams(vmem_limit_bytes=32 << 20),
+        compiler_params=pltpu.CompilerParams(vmem_limit_bytes=56 << 20),
     )(counts, recv)
     run = rows // 8 + 2 * FRINGE
     return pl.pallas_call(
         functools.partial(finish_kernel, dims),
         name="finish",
         out_shape=jax.ShapeDtypeStruct((3, rows, cols), F32),
-        in_specs=[anywhere, vmem],
+        in_specs=[anywhere] * 2,
         out_specs=anywhere,
         scratch_shapes=[
-            pltpu.VMEM(fields_shape, F32),
+            pltpu.VMEM((tiles + 1, ext, LANES), F32),
+            *runs,
+            pltpu.VMEM((3, tiles, ext, LANES), F32),
             pltpu.VMEM((run, LANES), F32),
             pltpu.VMEM((run, LANES), F32),
             pltpu.VMEM((run, LANES), F32),
             pltpu.VMEM((run, LANES), F32),
-            pltpu.VMEM((tiles, FRINGE, LANES), F32),
-            pltpu.VMEM((tiles, FRINGE, LANES), F32),
-            dma, dma((2, 2)), dma((2, 2)), dma((4, 2)), dma((tiles,)),
+            dma((6,)), dma((2, 2)), dma((2, 2)), dma((4, 2)), dma((3, tiles)),
         ],
-        compiler_params=pltpu.CompilerParams(collective_id=1, has_side_effects=True, vmem_limit_bytes=32 << 20),
+        compiler_params=params(collective_id=1),
     )(fields, forcing)
 
 

time: 132 us -> 86 us (0.65)
  the two profiles are of different devices: /device:TPU:33 before, /device:TPU:35 now
where the time goes in v2:
time: 86 us; the launch traced here: 85.9 us
  Pallas kernels  83.2 us (97%)
  local copies, waits for them, and re-layouts  2.67 us (3%)
    pallas_call x1, Pallas kernels, per_device(): pl.pallas_call(functools.partial(route_kernel, dims), name='route', out_s...  39.8 us
    pallas_call x1, Pallas kernels, per_device(): pl.pallas_call(functools.partial(finish_kernel, dims), name='finish', out...  31.2 us
    pallas_call x1, Pallas kernels, per_device(): pl.pallas_call(functools.partial(spread_kernel, dims), name='spread', out...  12.2 us
    unnamed x1, local copies, waits for them, and re-layouts  2.67 us

profile of v2, /device:TPU:35, one launch (start us, length us, event | category | flops | bytes accessed | tf_op | source)
XLA Modules:
  0.0 85.9 jit_solution(16469960173500254942)
XLA Ops:
  0.0 39.8 %route.1 = (f32[5,5,38,8,128]{4,3,2,1,0:T(8,128)}, f32[128,5,128]{2,1,0:T(8,128)}, s32[8,128]{1,0:T(8,128)}) custom-call(f32[3,256,512]{2,1,0:T(8,128)} %state.1, f32[2,256,512]{2,1,0:T(8,128)} %depth.1, f32[32,128]{1,0:T(8,128)} %innov_in.1, f32[32,4,128]{2,1,0:T(4,128)} %weight_in.1, s32[1,32]{1,0:T(1,128)} %bitcast.2, s32[1,32]{1,0:T(1,128)} %bitcast.3, ...), custom_call_target="tpu_custom_call" | custom-call | tf_op jit(solution)/shard_map/route/pallas_call | solution.py:577
  39.8 12.2 %spread.1.forcing_in = f32[4,256,128]{2,1,0:T(8,128)} custom-call(s32[8,128]{1,0:T(8,128)} %get-tuple-element.9.counts, f32[128,5,128]{2,1,0:T(8,128)} %get-tuple-element.10.recv), custom_call_target="tpu_custom_call" | custom-call | tf_op jit(solution)/shard_map/spread/pallas_call | solution.py:606
  52.0 31.2 %finish.1 = f32[3,256,512]{2,1,0:T(8,128)} custom-call(f32[5,5,38,8,128]{4,3,2,1,0:T(8,128)} %get-tuple-element.8.fields_in, f32[4,256,128]{2,1,0:T(8,128)} %spread.1.forcing_in), custom_call_target="tpu_custom_call" | custom-call | tf_op jit(solution)/shard_map/finish/pallas_call | solution.py:619
  83.2 2.7 %copy.10 = f32[3,256,512]{2,1,0:T(8,128)} copy(f32[3,256,512]{2,1,0:T(8,128)} %finish.1) | data formatting | bytes 3145728

commit v3 on v2

--- a/solution.py
+++ b/solution.py
@@ -16,7 +16,12 @@
 HALF = HALO // 2
 FRINGE = 16
 PIECES = 5
-GROUP = 2
+GROUP = 8
+ROW_BINS = 1
+COL_BINS = 2
+BINS = ROW_BINS * COL_BINS
+UNROLL = 32
+IDS = jnp.int16
 MESH = pl.DeviceIdType.MESH
 F32 = jnp.float32
 BF16 = jnp.bfloat16
@@ -62,21 +67,54 @@
     return value
 
 
-def to_runs(maps, values):
+def over(number, body):
+    unroll = max(d for d in range(1, 20) if number % d == 0)
+
+    def one(k, carry):
+        body(k)
+        return carry
+
+    lax.fori_loop(0, number, one, 0, unroll=unroll)
+
+
+def to_runs(maps, natural, temp, number, keep):
     lane, part_of, cuts, into, turn, back, out = maps
-    width = len(values)
-    sorted_ = [take(jnp.where(lane >= cuts[t], values[t - 1], values[t]), into[t]) for t in range(width)]
-    mixed = [by_part(part_of, [sorted_[(p - c) % width] for p in range(width)]) for c in range(width)]
-    return [take(mixed[c], turn[c]) if c else mixed[c] for c in range(width)]
-
-
-def from_runs(maps, values):
+    width = len(cuts)
+    for t in range(width):
+        for f, ref in enumerate(natural):
+            def sort(k):
+                rows = pl.ds(k, ROWS8, stride=number)
+                temp[f, t, k] = take(jnp.where(lane >= cuts[t], ref[(t - 1) % width, rows, :], ref[t, rows, :]), into[t])
+
+            over(number, sort)
+    for c in range(width):
+        for f in range(len(natural)):
+            def mix(k):
+                value = by_part(part_of, [temp[f, (p - c) % width, k] for p in range(width)])
+                keep(f, c, k, take(value, turn[c]) if c else value)
+
+            over(number, mix)
+
+
+def from_runs(maps, ref, temp, number, natural):
     lane, part_of, cuts, into, turn, back, out = maps
-    width = len(values)
-    mixed = [take(values[c], back[c]) if c else values[c] for c in range(width)]
-    sorted_ = [by_part(part_of, [mixed[(p - t) % width] for p in range(width)]) for t in range(width)]
-    windows = [take(sorted_[t], out[t]) for t in range(width)]
-    return [jnp.where(lane < cuts[t + 1], windows[t], windows[t + 1]) for t in range(width - 1)]
+    width = len(cuts)
+    for c in range(1, width):
+        def unmix(k):
+            temp[0, c, k] = take(ref[c, k], back[c])
+
+        over(number, unmix)
+    for t in range(width):
+        def unsort(k):
+            value = by_part(part_of, [temp[0, (p - t) % width, k] if (p - t) % width else ref[0, k] for p in range(width)])
+            temp[1, t, k] = take(value, out[t])
+
+        over(number, unsort)
+    for t in range(width - 1):
+        def join(k):
+            natural[t, pl.ds(k, ROWS8, stride=number), :] = jnp.where(lane < cuts[t + 1], temp[1, t, k], temp[1, t + 1, k])
+
+        over(number, join)
 
 
 def one_step(old, new, east_vel, north_vel, depth_east, depth_north):
@@ -113,7 +151,7 @@
 
 def route_kernel(dims, state, depth, innov_in, weight_in, tile_in, count_in, row_in, col_in, fields_out, recv_out, count_out,
                  fields, height, other, east_vel, north_vel, depth_east, depth_north,
-                 innov, weight, tile_row, count_row, obs_row, obs_col, send, recv, east_pack, west_pack, east_got, west_got,
+                 innov, weight, tile_row, count_row, obs_row, obs_col, spots, cells, ordered, temp, send, recv, east_pack, west_pack, east_got, west_got,
                  load_sem, small_sem, row_sem, pack_sem, corner_sem, a2a_sem, own_sem, store_sem):
     rows, cols, lat, lon, blocks = dims
     tiles = cols // LANES
@@ -157,20 +195,48 @@
     tile = jnp.sum(jnp.where(diagonal, tile_row[...].astype(F32), 0.0), axis=1, keepdims=True)
     count = jnp.sum(jnp.where(diagonal, count_row[...].astype(F32), 0.0), axis=1, keepdims=True)
     live = lane_ids((blocks, slots)).astype(F32) < count
-    masked = jnp.where(live, innov[...], 0.0)
-    cell = jnp.where(live, obs_row[...] * cols + obs_col[...] + 1, 0).astype(F32)
-    data = jnp.concatenate([weight[:, k, :] * masked for k in range(4)] + [cell], axis=0)
+    bin_rows, bin_cols = rows // ROW_BINS, cols // COL_BINS
+    row_at, col_at = obs_row[...], obs_col[...]
+    bin_at = row_at // bin_rows * COL_BINS + col_at // bin_cols
+    cell = (bin_at * bin_rows + row_at % bin_rows) * bin_cols + col_at % bin_cols + 1
+    member = [jnp.where(jnp.logical_and(live, bin_at == b), 1.0, 0.0) for b in range(BINS)]
+    to_left = jnp.where(lax.broadcasted_iota(I32, (slots, slots), 0) < lane_ids((slots, slots)), 1.0, 0.0).astype(BF16)
+    ahead = jnp.dot(jnp.concatenate(member, axis=0).astype(BF16), to_left, preferred_element_type=F32)
+    begin = jnp.ones((blocks, 1), F32)
+    spot = jnp.zeros((blocks, slots), F32)
+    for b in range(BINS):
+        spot += member[b] * (ahead[b * blocks:(b + 1) * blocks] + begin)
+        begin += jnp.sum(member[b], axis=1, keepdims=True)
+    spots[...] = spot
+    innov[...] = jnp.where(live, innov[...], 0.0)
+    cells[...] = jnp.where(live, cell, 0).astype(F32)
+    ranks = (lax.broadcasted_iota(I32, (slots, slots), 0) + 1).astype(F32)
+    sub = lax.broadcasted_iota(I32, (ROWS8 - 4, slots), 0)
+
+    def order(b, carry):
+        move = jnp.where(ranks == spots[pl.ds(b, 1), :], 1.0, 0.0).astype(BF16)
+        values = weight[b] * innov[pl.ds(b, 1), :]
+        data = jnp.concatenate([values, jnp.where(sub == 0, cells[pl.ds(b, 1), :], 0.0)], axis=0)
+        high = data.astype(BF16).astype(F32)
+        mid = (data - high).astype(BF16).astype(F32)
+        parts = jnp.concatenate([high, mid, data - high - mid], axis=0).astype(BF16)
+        moved = lax.dot_general(parts, move, (((1,), (1,)), ((), ())), preferred_element_type=F32)
+        ordered[pl.ds(pl.multiple_of(b * ROWS8, ROWS8), ROWS8), :] = moved[:ROWS8] + moved[ROWS8:2 * ROWS8] + moved[2 * ROWS8:]
+        return carry
+
+    lax.fori_loop(0, blocks, order, 0, unroll=max(d for d in range(1, 9) if blocks % d == 0))
     named = jnp.where(tile == lane_ids((blocks, lon)).astype(F32), 1.0, 0.0)
     earlier = jnp.where(lax.broadcasted_iota(I32, square, 0) > lane_ids(square), 1.0, 0.0)
     before = jnp.dot(earlier.astype(BF16), named.astype(BF16), preferred_element_type=F32)
     rank = jnp.sum(before * named, axis=1, keepdims=True)
     place = tile * CAP + rank
-    wide = (blocks, PIECES * blocks)
+    wide = (blocks, ROWS8 * blocks)
     ids = lane_ids(wide)
-    row_of = jnp.where(lax.broadcasted_iota(I32, wide, 0) == ids % blocks, place * ROWS8 + (ids // blocks).astype(F32), 0.0)
+    row_of = jnp.where(lax.broadcasted_iota(I32, wide, 0) == ids // ROWS8, place * ROWS8 + (ids % ROWS8).astype(F32), 0.0)
     row_of = jnp.sum(row_of, axis=0, keepdims=True)
-    pick = lax.broadcasted_iota(I32, (CAP * lon * ROWS8, PIECES * blocks), 0).astype(F32) == row_of
+    pick = lax.broadcasted_iota(I32, (CAP * lon * ROWS8, ROWS8 * blocks), 0).astype(F32) == row_of
     pick = jnp.where(pick, 1.0, 0.0).astype(BF16)
+    data = ordered[...]
     high = data.astype(BF16)
     rest = data - high.astype(F32)
     mid = rest.astype(BF16)
@@ -312,14 +378,10 @@
     refs = (height, east_vel, north_vel, depth_east, depth_north)
     maps = columns_at(tiles + 1)
 
-    def arrange(k, carry):
-        for f, ref in enumerate(refs):
-            values = to_runs(maps, [fields[f, t, pl.ds(k, ROWS8, stride=number), :] for t in range(tiles + 1)])
-            for c in range(tiles + 1):
-                ref[c, k] = values[c]
-        return carry
-
-    lax.fori_loop(0, number, arrange, 0, unroll=2)
+    def keep(f, c, k, value):
+        refs[f][c, k] = value
+
+    to_runs(maps, [fields.at[f] for f in range(5)], temp, number, keep)
     inner = pl.ds(0, number)
     stores = [pltpu.make_async_copy(ref.at[:, inner], fields_out.at[f], store_sem.at[f]) for f, ref in enumerate(refs)]
     for store in stores[3:]:
@@ -335,78 +397,126 @@
     every.wait_recv()
     stores.append(pltpu.make_async_copy(recv, recv_out, store_sem.at[5]))
     stores[5].start()
-    filled = jnp.where(recv[:, PIECES - 1, :] > 0.0, 1.0, 0.0).astype(BF16)
+    cell = recv[:, PIECES - 1, :]
     ones = jnp.ones((ROWS8, slots), BF16)
-    live_of = lax.dot_general(ones, filled, (((1,), (1,)), ((), ())), preferred_element_type=F32)
-    count_out[...] = live_of.astype(I32)
+    area = float(bin_rows * bin_cols)
+    for b in range(BINS):
+        within = jnp.logical_and(cell > b * area, cell <= (b + 1) * area)
+        live_of = lax.dot_general(ones, jnp.where(within, 1.0, 0.0).astype(BF16), (((1,), (1,)), ((), ())), preferred_element_type=F32)
+        count_out[pl.ds(b, 1), :] = live_of[:1].astype(I32)
+    count_out[pl.ds(BINS, ROWS8 - BINS), :] = jnp.zeros((ROWS8 - BINS, CAP * lon), I32)
     every.wait_send()
     for store in stores:
         store.wait()
 
 
-def spread_kernel(dims, counts, recv, out, packed, total):
+def spread_kernel(dims, counts, recv, out, packed, total, left_a, left_b, right_a, right_b):
     rows, cols, lat, lon, blocks = dims
     tiles = cols // LANES
     segments = CAP * lon
+    bin_rows, bin_cols = rows // ROW_BINS, cols // COL_BINS
+    bins = ROW_BINS * COL_BINS
+    padded = left_a.shape[0] // 2
+    depth = GROUP * LANES
+    room = segments + GROUP
     lane = lane_ids((PIECES, LANES))
+    zero = jnp.zeros((PIECES, LANES), F32)
 
     def append(segment, carry):
-        fill, current = carry
-        number = counts[0, segment]
-        chunk = fill // LANES
-        shift = fill - chunk * LANES
-        turned = pltpu.roll(recv[segment], shift, 1)
-        current = jnp.where(lane >= shift, turned, current)
-        packed[chunk] = current
-        fill = fill + number
-        current = jnp.where(fill // LANES > chunk, turned, current)
-        return fill, current
-
-    zero = jnp.zeros((PIECES, LANES), F32)
-    fill, current = lax.fori_loop(0, segments, append, (jnp.int32(0), zero), unroll=min(32, segments))
-    chunk = fill // LANES
-    packed[chunk] = jnp.where(lane < fill - chunk * LANES, current, 0.0)
-    for extra in range(1, GROUP):
-        packed[chunk + extra] = zero
+        block = recv[segment]
+        begin = 0
+        after = []
+        for b, (fill, current) in enumerate(carry):
+            number = counts[b, segment]
+            chunk = lax.shift_right_logical(fill, 7)
+            turned = pltpu.roll(block, (fill - begin) & (LANES - 1), 1)
+            current = jnp.where(lane >= (fill & (LANES - 1)), turned, current)
+            packed[chunk + b * room] = current
+            begin = begin + number
+            fill = fill + number
+            after.append((fill, jnp.where(lax.shift_right_logical(fill, 7) > chunk, turned, current)))
+        return tuple(after)
+
+    filled = lax.fori_loop(0, segments, append, ((jnp.int32(0), zero),) * bins, unroll=min(UNROLL, segments))
+    jobs, starts = [], [0]
+    for b, (fill, current) in enumerate(filled):
+        chunk = lax.shift_right_logical(fill, 7) + b * room
+        packed[chunk] = jnp.where(lane < (fill & (LANES - 1)), current, 0.0)
+        for extra in range(1, GROUP):
+            packed[chunk + extra] = zero
+        starts.append(starts[-1] + (fill + depth - 1) // depth)
+    for extra in range(GROUP):
+        packed[bins * room + extra] = zero
     total[...] = jnp.zeros_like(total)
-    groups = (fill + GROUP * LANES - 1) // (GROUP * LANES)
-
-    depth = GROUP * LANES
-    row_ids = lax.broadcasted_iota(I32, (rows, depth), 0)
-    col_ids = lax.broadcasted_iota(I32, (cols, depth), 0)
-
-    def add_group(index, carry):
-        part = [packed[index * GROUP + j] for j in range(GROUP)]
-        both = jnp.concatenate(part, axis=1)
-        cell = both[PIECES - 1:, :].astype(I32) - 1
-        row_at = cell // cols
-        col_at = cell - row_at * cols
-        here = row_ids == row_at
-        past = row_ids == row_at + 1
-        column = jnp.where(col_ids == col_at, 1.0, 0.0).astype(BF16)
+    count = starts[-1]
+
+    def place(job):
+        which = 0
+        begin = 0
+        for b in range(1, bins):
+            past = job >= starts[b]
+            which = jnp.where(past, b, which)
+            begin = jnp.where(past, starts[b], begin)
+        chunk = which * room + (job - begin) * GROUP
+        return jnp.where(job < count, chunk, bins * room), jnp.where(job < count, which, 0)
+
+    row_ids = lax.broadcasted_iota(IDS, (padded, depth), 0)
+    col_ids = lax.broadcasted_iota(IDS, (bin_cols, depth), 0)
+    one, none = jnp.array(1, BF16), jnp.array(0, BF16)
+
+    def build(job, left, right):
+        chunk, which = place(job)
+        both = jnp.concatenate([packed[chunk + j] for j in range(GROUP)], axis=1)
+        cell = both[4:5, :].astype(I32) - 1 - which * (bin_rows * bin_cols)
+        row_at = cell // bin_cols if bin_cols & (bin_cols - 1) else lax.shift_right_arithmetic(cell, bin_cols.bit_length() - 1)
+        col_at = cell - row_at * bin_cols
+
+        def wide(value, kind, number):
+            return jnp.broadcast_to(value, (number, depth)).astype(kind)
+
+        here = row_ids == wide(row_at, IDS, padded)
+        past = row_ids == wide(row_at + 1, IDS, padded)
+        column = jnp.where(col_ids == wide(col_at, IDS, bin_cols), one, none)
+        right[:, :depth] = column
+        right[:, depth:] = column
         high = both[:4, :].astype(BF16).astype(F32)
-        low = both[:4, :] - high
-
-        def side(value, k):
-            return jnp.where(here, value[k:k + 1, :], jnp.where(past, value[k + 2:k + 3, :], 0.0)).astype(BF16)
-
-        left = jnp.concatenate([side(high, 0), side(low, 0)], axis=1)
-        right = jnp.concatenate([side(high, 1), side(low, 1)], axis=1)
-        both_sides = jnp.concatenate([left, right], axis=0)
-        columns = jnp.concatenate([column, column], axis=1)
-        total[...] += lax.dot_general(both_sides, columns, (((1,), (1,)), ((), ())), preferred_element_type=F32)
+        for part, values in enumerate((high, both[:4, :] - high)):
+            for side in range(2):
+                at = wide(values[side:side + 1, :], BF16, padded)
+                above = wide(values[side + 2:side + 3, :], BF16, padded)
+                left[pl.ds(side * padded, padded), pl.ds(part * depth, depth)] = jnp.where(here, at, jnp.where(past, above, none))
+
+    def add(job, left, right):
+        _, which = place(job)
+        total[which] += lax.dot_general(left[...], right[...], (((1,), (1,)), ((), ())), preferred_element_type=F32)
+
+    build(0, left_a, right_a)
+
+    def pair(index, carry):
+        build(2 * index + 1, left_b, right_b)
+        add(2 * index, left_a, right_a)
+        build(2 * index + 2, left_a, right_a)
+        add(2 * index + 1, left_b, right_b)
         return carry
 
-    lax.fori_loop(0, groups, add_group, 0)
-
-    lane = lane_ids((rows, LANES))
-    turned = [pltpu.roll(total[pl.ds(rows, rows), pl.ds(t * LANES, LANES)], 1, 1) for t in range(tiles)]
-    for t in range(tiles):
-        before = turned[t - 1] if t else jnp.zeros((rows, LANES), F32)
-        out[t] = total[pl.ds(0, rows), pl.ds(t * LANES, LANES)] + jnp.where(lane == 0, before, turned[t])
-
-
-def finish_kernel(dims, fields_in, forcing_in, out, forcing, height, other, east_vel, north_vel, depth_east, depth_north, done,
+    lax.fori_loop(0, (count + 1) // 2, pair, 0)
+
+    bin_tiles = bin_cols // LANES
+    lane = lane_ids((bin_rows, LANES))
+    for i in range(ROW_BINS):
+        if i:
+            for j in range(COL_BINS):
+                for at in (0, padded):
+                    total[i * COL_BINS + j, pl.ds(at, ROWS8), :] += total[(i - 1) * COL_BINS + j, pl.ds(at + bin_rows, ROWS8), :]
+        before = jnp.zeros((bin_rows, LANES), F32)
+        for t in range(tiles):
+            which, span = i * COL_BINS + t // bin_tiles, pl.ds(t % bin_tiles * LANES, LANES)
+            turned = pltpu.roll(total[which, pl.ds(padded, bin_rows), span], 1, 1)
+            out[t, pl.ds(i * bin_rows, bin_rows), :] = total[which, pl.ds(0, bin_rows), span] + jnp.where(lane == 0, before, turned)
+            before = turned
+
+
+def finish_kernel(dims, fields_in, forcing_in, out, forcing, height, other, east_vel, north_vel, depth_east, depth_north, temp, done,
                   east_pack, west_pack, east_got, west_got, load_sem, row_sem, pack_sem, corner_sem, store_sem):
     rows, cols, lat, lon, blocks = dims
     tiles = cols // LANES
@@ -522,22 +632,14 @@
 
     maps = columns_at(tiles + 1)
 
-    def add(k, carry):
-        values = to_runs(maps, [forcing[t, pl.ds(k, ROWS8, stride=number), :] for t in range(tiles + 1)])
-        for c in range(tiles + 1):
-            height[c, k] += values[c]
-        return carry
-
-    lax.fori_loop(0, number, add, 0, unroll=2)
+    def keep(f, c, k, value):
+        height[c, k] += value
+
+    to_runs(maps, [forcing], temp, number, keep)
     steps(HALF, height, other, *refs[1:])
     stores = []
     for f in range(3):
-        def leave(k, carry):
-            for t, value in enumerate(from_runs(maps, [refs[f][c, k] for c in range(tiles + 1)])):
-                done[f, t, pl.ds(k, ROWS8, stride=number), :] = value
-            return carry
-
-        lax.fori_loop(0, number, leave, 0, unroll=2)
+        from_runs(maps, refs[f], temp, number, done.at[f])
         for t in range(tiles):
             store = pltpu.make_async_copy(done.at[f, t, pl.ds(HALO, rows), :],
                                           out.at[f, :, pl.ds(t * LANES, LANES)], store_sem.at[f, t])
@@ -573,7 +675,7 @@
     number = ext // ROWS8
     natural = pltpu.VMEM((5, tiles + 1, ext, LANES), F32)
     runs = [pltpu.VMEM((tiles + 1, number + 1, ROWS8, LANES), F32)] * 2 + [pltpu.VMEM((tiles + 1, number, ROWS8, LANES), F32)] * 4
-    params = functools.partial(pltpu.CompilerParams, has_side_effects=True, vmem_limit_bytes=56 << 20)
+    params = functools.partial(pltpu.CompilerParams, has_side_effects=True)
     fields, recv, counts = pl.pallas_call(
         functools.partial(route_kernel, dims),
         name="route",
@@ -592,6 +694,10 @@
             pltpu.VMEM((1, blocks), I32),
             pltpu.VMEM((blocks, slots), I32),
             pltpu.VMEM((blocks, slots), I32),
+            pltpu.VMEM((blocks, slots), F32),
+            pltpu.VMEM((blocks, slots), F32),
+            pltpu.VMEM((ROWS8 * blocks, slots), F32),
+            pltpu.VMEM((5, tiles + 1, number, ROWS8, LANES), F32),
             pltpu.VMEM((segments, PIECES, slots), F32),
             pltpu.VMEM((segments, PIECES, slots), F32),
             pltpu.VMEM((rows, LANES), F32),
@@ -600,9 +706,10 @@
             pltpu.VMEM((ext, LANES), F32),
             dma((2 * tiles,)), dma((6,)), dma((2, 2)), dma((2, 2)), dma((4, 2)), dma((2,)), dma, dma((6,)),
         ],
-        compiler_params=params(collective_id=0),
+        compiler_params=params(collective_id=0, vmem_limit_bytes=56 << 20),
     )(adjoint_state, face_depth, innovation, interp_weight, block_tile.reshape(1, blocks), block_count.reshape(1, blocks),
       obs_row, obs_col)
+    padded = rows if ROW_BINS == 1 else rows // ROW_BINS + 16
     forcing = pl.pallas_call(
         functools.partial(spread_kernel, dims),
         name="spread",
@@ -610,10 +717,12 @@
         in_specs=[pl.BlockSpec(memory_space=pltpu.SMEM), vmem],
         out_specs=vmem,
         scratch_shapes=[
-            pltpu.VMEM((segments + GROUP, PIECES, LANES), F32),
-            pltpu.VMEM((2 * rows, cols), F32),
+            pltpu.VMEM((BINS * (segments + GROUP) + GROUP, PIECES, LANES), F32),
+            pltpu.VMEM((BINS, 2 * padded, cols // COL_BINS), F32),
+            *[pltpu.VMEM((2 * padded, 2 * GROUP * LANES), BF16)] * 2,
+            *[pltpu.VMEM((cols // COL_BINS, 2 * GROUP * LANES), BF16)] * 2,
         ],
-        compiler_params=pltpu.CompilerParams(vmem_limit_bytes=56 << 20),
+        compiler_params=pltpu.CompilerParams(vmem_limit_bytes=24 << 20),
     )(counts, recv)
     run = rows // 8 + 2 * FRINGE
     return pl.pallas_call(
@@ -625,6 +734,7 @@
         scratch_shapes=[
             pltpu.VMEM((tiles + 1, ext, LANES), F32),
             *runs,
+            pltpu.VMEM((2, tiles + 1, number, ROWS8, LANES), F32),
             pltpu.VMEM((3, tiles, ext, LANES), F32),
             pltpu.VMEM((run, LANES), F32),
             pltpu.VMEM((run, LANES), F32),
@@ -632,7 +742,7 @@
             pltpu.VMEM((run, LANES), F32),
             dma((6,)), dma((2, 2)), dma((2, 2)), dma((4, 2)), dma((3, tiles)),
         ],
-        compiler_params=params(collective_id=1),
+        compiler_params=params(collective_id=1, vmem_limit_bytes=50 << 20),
     )(fields, forcing)
 
 

time: 86 us -> 71 us (0.83)
  the two profiles are of different devices: /device:TPU:35 before, /device:TPU:1 now
where the time goes in v3:
time: 71 us; the launch traced here: 70.2 us
  Pallas kernels  67.3 us (95%)
  local copies, waits for them, and re-layouts  2.86 us (4%)
    pallas_call x1, Pallas kernels, per_device(): pl.pallas_call(functools.partial(route_kernel, dims), name='route', out_s...  43.1 us
    pallas_call x1, Pallas kernels, per_device(): pl.pallas_call(functools.partial(finish_kernel, dims), name='finish', out...  20.3 us
    pallas_call x1, Pallas kernels, per_device(): pl.pallas_call(functools.partial(spread_kernel, dims), name='spread', out...  3.92 us
    unnamed x5, local copies, waits for them, and re-layouts  2.86 us

profile of v3, /device:TPU:1, one launch (start us, length us, event | category | flops | bytes accessed | tf_op | source)
XLA Modules:
  0.0 70.2 jit_solution(7577373771846703228)
XLA Ops:
  0.0 43.1 %route.1 = (f32[5,5,38,8,128]{4,3,2,1,0:T(8,128)}, f32[128,5,128]{2,1,0:T(8,128)}, s32[8,128]{1,0:T(8,128)}) custom-call(f32[3,256,512]{2,1,0:T(8,128)} %state.1, f32[2,256,512]{2,1,0:T(8,128)} %depth.1, f32[32,128]{1,0:T(8,128)} %innov_in.1, f32[32,4,128]{2,1,0:T(4,128)} %weight_in.1, s32[1,32]{1,0:T(1,128)} %bitcast.2, s32[1,32]{1,0:T(1,128)} %bitcast.3, ...), custom_call_target="tpu_custom_call" | custom-call | tf_op jit(solution)/shard_map/route/pallas_call | solution.py:679
  43.1 0.0 copy-start
  43.1 1.0 %copy-done = f32[128,5,128]{2,1,0:T(8,128)S(1)} copy-done((f32[128,5,128]{2,1,0:T(8,128)S(1)}, f32[128,5,128]{2,1,0:T(8,128)}, u32[]{:S(2)}) %copy-start) | copy-done | bytes 327704
  44.1 0.0 copy-start.1
  44.1 0.7 copy-done.1
  44.8 3.9 %spread.1.forcing_in = f32[4,256,128]{2,1,0:T(8,128)S(1)} custom-call(s32[8,128]{1,0:T(8,128)S(1)} %copy-done.1, f32[128,5,128]{2,1,0:T(8,128)S(1)} %copy-done), custom_call_target="tpu_custom_call" | custom-call | tf_op jit(solution)/shard_map/spread/pallas_call | solution.py:713
  48.8 20.3 %finish.1 = f32[3,256,512]{2,1,0:T(8,128)S(1)} custom-call(f32[5,5,38,8,128]{4,3,2,1,0:T(8,128)} %get-tuple-element.8.fields_in, f32[4,256,128]{2,1,0:T(8,128)S(1)} %spread.1.forcing_in), custom_call_target="tpu_custom_call" | custom-call | tf_op jit(solution)/shard_map/finish/pallas_call | solution.py:728
  69.1 1.1 %copy.10 = f32[3,256,512]{2,1,0:T(8,128)} copy(f32[3,256,512]{2,1,0:T(8,128)S(1)} %finish.1) | data formatting | bytes 3145728
Async XLA Ops:
  43.1 1.0 %copy-start = (f32[128,5,128]{2,1,0:T(8,128)S(1)}, f32[128,5,128]{2,1,0:T(8,128)}, u32[]{:S(2)}) copy-start(f32[128,5,128]{2,1,0:T(8,128)} %get-tuple-element.10.recv) | copy-start | bytes 983044
  44.1 0.7 copy-start.1

commit v4 on v3

--- a/solution.py
+++ b/solution.py
@@ -67,8 +67,8 @@
     return value
 
 
-def over(number, body):
-    unroll = max(d for d in range(1, 20) if number % d == 0)
+def over(number, body, most):
+    unroll = max(d for d in range(1, number + 1) if number % d == 0 and d <= max(most, 1))
 
     def one(k, carry):
         body(k)
@@ -80,41 +80,49 @@
 def to_runs(maps, natural, temp, number, keep):
     lane, part_of, cuts, into, turn, back, out = maps
     width = len(cuts)
+    most = 100 // len(natural)
     for t in range(width):
-        for f, ref in enumerate(natural):
-            def sort(k):
-                rows = pl.ds(k, ROWS8, stride=number)
+        def sort(k):
+            rows = pl.ds(k, ROWS8, stride=number)
+            for f, ref in enumerate(natural):
                 temp[f, t, k] = take(jnp.where(lane >= cuts[t], ref[(t - 1) % width, rows, :], ref[t, rows, :]), into[t])
 
-            over(number, sort)
+        over(number, sort, most)
     for c in range(width):
-        for f in range(len(natural)):
-            def mix(k):
+        def mix(k):
+            for f in range(len(natural)):
                 value = by_part(part_of, [temp[f, (p - c) % width, k] for p in range(width)])
                 keep(f, c, k, take(value, turn[c]) if c else value)
 
-            over(number, mix)
-
-
-def from_runs(maps, ref, temp, number, natural):
+        over(number, mix, most)
+
+
+def from_runs(maps, refs, temp, number, natural, finished):
     lane, part_of, cuts, into, turn, back, out = maps
-    width = len(cuts)
+    width, fields = len(cuts), len(refs)
+    most = 120 // fields
     for c in range(1, width):
         def unmix(k):
-            temp[0, c, k] = take(ref[c, k], back[c])
-
-        over(number, unmix)
+            for f in range(fields):
+                temp[f, c, k] = take(refs[f][c, k], back[c])
+
+        over(number, unmix, most)
     for t in range(width):
         def unsort(k):
-            value = by_part(part_of, [temp[0, (p - t) % width, k] if (p - t) % width else ref[0, k] for p in range(width)])
-            temp[1, t, k] = take(value, out[t])
-
-        over(number, unsort)
-    for t in range(width - 1):
-        def join(k):
-            natural[t, pl.ds(k, ROWS8, stride=number), :] = jnp.where(lane < cuts[t + 1], temp[1, t, k], temp[1, t + 1, k])
-
-        over(number, join)
+            for f in range(fields):
+                parts = [(p - t) % width for p in range(width)]
+                value = by_part(part_of, [temp[f, c, k] if c else refs[f][0, k] for c in parts])
+                temp[fields + f, t, k] = take(value, out[t])
+
+        over(number, unsort, most)
+        if t:
+            def join(k):
+                for f in range(fields):
+                    value = jnp.where(lane < cuts[t], temp[fields + f, t - 1, k], temp[fields + f, t, k])
+                    natural[f, t - 1, pl.ds(k, ROWS8, stride=number), :] = value
+
+            over(number, join, most)
+            finished(t - 1)
 
 
 def one_step(old, new, east_vel, north_vel, depth_east, depth_north):
@@ -224,7 +232,7 @@
         ordered[pl.ds(pl.multiple_of(b * ROWS8, ROWS8), ROWS8), :] = moved[:ROWS8] + moved[ROWS8:2 * ROWS8] + moved[2 * ROWS8:]
         return carry
 
-    lax.fori_loop(0, blocks, order, 0, unroll=max(d for d in range(1, 9) if blocks % d == 0))
+    lax.fori_loop(0, blocks, order, 0, unroll=max(d for d in range(1, 17) if blocks % d == 0))
     named = jnp.where(tile == lane_ids((blocks, lon)).astype(F32), 1.0, 0.0)
     earlier = jnp.where(lax.broadcasted_iota(I32, square, 0) > lane_ids(square), 1.0, 0.0)
     before = jnp.dot(earlier.astype(BF16), named.astype(BF16), preferred_element_type=F32)
@@ -287,7 +295,7 @@
         east_pack[pl.ds(base, ROWS8), :] = to_east
         return carry
 
-    lax.fori_loop(0, rows // ROWS8, pack, 0, unroll=2)
+    lax.fori_loop(0, rows // ROWS8, pack, 0, unroll=8)
 
     pl.semaphore_wait(barrier, lon - 1 + 3 * has_north.astype(I32) + 3 * has_south.astype(I32))
 
@@ -348,7 +356,7 @@
     to_east.wait_recv()
     to_west.wait_recv()
 
-    def unpack(index, carry):
+    def unpack(index):
         here = pl.ds(pl.multiple_of(index * ROWS8, ROWS8), ROWS8)
         from_east, from_west = east_got[here, :], west_got[here, :]
         for f in range(5):
@@ -358,9 +366,8 @@
             left = jnp.logical_and(lane >= first, lane < first + HALO)
             both = jnp.where(right, from_east, jnp.where(left, from_west, 0.0))
             fields[f, tiles, here, :] = pltpu.roll(both, LANES - HALO * f, 1) if f else both
-        return carry
-
-    lax.fori_loop(0, ext // ROWS8, unpack, 0, unroll=2)
+
+    over(ext // ROWS8, unpack, 19)
 
     @pl.when(has_north)
     def _():
@@ -410,7 +417,7 @@
         store.wait()
 
 
-def spread_kernel(dims, counts, recv, out, packed, total, left_a, left_b, right_a, right_b):
+def spread_kernel(dims, counts_in, recv_in, out, counts, recv, packed, total, left_a, left_b, right_a, right_b, load_sem):
     rows, cols, lat, lon, blocks = dims
     tiles = cols // LANES
     segments = CAP * lon
@@ -419,6 +426,12 @@
     padded = left_a.shape[0] // 2
     depth = GROUP * LANES
     room = segments + GROUP
+    loads = [pltpu.make_async_copy(counts_in, counts, load_sem.at[0]), pltpu.make_async_copy(recv_in, recv, load_sem.at[1])]
+    for load in loads:
+        load.start()
+    total[...] = jnp.zeros_like(total)
+    for load in loads:
+        load.wait()
     lane = lane_ids((PIECES, LANES))
     zero = jnp.zeros((PIECES, LANES), F32)
 
@@ -447,7 +460,6 @@
         starts.append(starts[-1] + (fill + depth - 1) // depth)
     for extra in range(GROUP):
         packed[bins * room + extra] = zero
-    total[...] = jnp.zeros_like(total)
     count = starts[-1]
 
     def place(job):
@@ -638,13 +650,13 @@
     to_runs(maps, [forcing], temp, number, keep)
     steps(HALF, height, other, *refs[1:])
     stores = []
-    for f in range(3):
-        from_runs(maps, refs[f], temp, number, done.at[f])
-        for t in range(tiles):
-            store = pltpu.make_async_copy(done.at[f, t, pl.ds(HALO, rows), :],
-                                          out.at[f, :, pl.ds(t * LANES, LANES)], store_sem.at[f, t])
-            store.start()
-            stores.append(store)
+
+    def finished(t):
+        store = pltpu.make_async_copy(done.at[:, t, pl.ds(HALO, rows), :], out.at[:, :, pl.ds(t * LANES, LANES)], store_sem.at[t])
+        store.start()
+        stores.append(store)
+
+    from_runs(maps, refs[:3], temp, number, done, finished)
 
     @pl.when(has_north)
     def _():
@@ -714,15 +726,18 @@
         functools.partial(spread_kernel, dims),
         name="spread",
         out_shape=jax.ShapeDtypeStruct((tiles, rows, LANES), F32),
-        in_specs=[pl.BlockSpec(memory_space=pltpu.SMEM), vmem],
+        in_specs=[anywhere] * 2,
         out_specs=vmem,
         scratch_shapes=[
+            pltpu.SMEM((ROWS8, segments), I32),
+            pltpu.VMEM((segments, PIECES, slots), F32),
             pltpu.VMEM((BINS * (segments + GROUP) + GROUP, PIECES, LANES), F32),
             pltpu.VMEM((BINS, 2 * padded, cols // COL_BINS), F32),
             *[pltpu.VMEM((2 * padded, 2 * GROUP * LANES), BF16)] * 2,
             *[pltpu.VMEM((cols // COL_BINS, 2 * GROUP * LANES), BF16)] * 2,
+            dma((2,)),
         ],
-        compiler_params=pltpu.CompilerParams(vmem_limit_bytes=24 << 20),
+        compiler_params=pltpu.CompilerParams(vmem_limit_bytes=56 << 20),
     )(counts, recv)
     run = rows // 8 + 2 * FRINGE
     return pl.pallas_call(
@@ -734,13 +749,13 @@
         scratch_shapes=[
             pltpu.VMEM((tiles + 1, ext, LANES), F32),
             *runs,
-            pltpu.VMEM((2, tiles + 1, number, ROWS8, LANES), F32),
+            pltpu.VMEM((6, tiles + 1, number, ROWS8, LANES), F32),
             pltpu.VMEM((3, tiles, ext, LANES), F32),
             pltpu.VMEM((run, LANES), F32),
             pltpu.VMEM((run, LANES), F32),
             pltpu.VMEM((run, LANES), F32),
             pltpu.VMEM((run, LANES), F32),
-            dma((6,)), dma((2, 2)), dma((2, 2)), dma((4, 2)), dma((3, tiles)),
+            dma((6,)), dma((2, 2)), dma((2, 2)), dma((4, 2)), dma((tiles,)),
         ],
         compiler_params=params(collective_id=1, vmem_limit_bytes=50 << 20),
     )(fields, forcing)

time: 71 us -> 59.2 us (0.83)
  Pallas kernels: 67.3 us -> 56.9 us
    pallas_call x1, Pallas kernels: 43.1 us -> 36.9 us  [per_device(): pl.pallas_call(functools.partial(route_kernel, dims), name='route', out_s...]
    pallas_call x1, Pallas kernels: 20.3 us -> 14.9 us  [per_device(): pl.pallas_call(functools.partial(finish_kernel, dims), name='finish', out...]
    pallas_call x1, Pallas kernels: 3.92 us -> 5.06 us  [per_device(): pl.pallas_call(functools.partial(spread_kernel, dims), name='spread', out...]
    unnamed x5 -> x3, local copies, waits for them, and re-layouts: 2.86 us -> 2.18 us
where the time goes in v4:
time: 59.2 us; the launch traced here: 59.1 us
  Pallas kernels  56.9 us (96%)
  local copies, waits for them, and re-layouts  2.18 us (4%)
    pallas_call x1, Pallas kernels, per_device(): pl.pallas_call(functools.partial(route_kernel, dims), name='route', out_s...  36.9 us
    pallas_call x1, Pallas kernels, per_device(): pl.pallas_call(functools.partial(finish_kernel, dims), name='finish', out...  14.9 us
    pallas_call x1, Pallas kernels, per_device(): pl.pallas_call(functools.partial(spread_kernel, dims), name='spread', out...  5.06 us
    unnamed x3, local copies, waits for them, and re-layouts  2.18 us

profile of v4, /device:TPU:1, one launch (start us, length us, event | category | flops | bytes accessed | tf_op | source)
XLA Modules:
  0.0 59.1 jit_solution(13488120017141475382)
XLA Ops:
  0.0 36.9 %route.1 = (f32[5,5,38,8,128]{4,3,2,1,0:T(8,128)}, f32[128,5,128]{2,1,0:T(8,128)}, s32[8,128]{1,0:T(8,128)}) custom-call(f32[3,256,512]{2,1,0:T(8,128)} %state.1, f32[2,256,512]{2,1,0:T(8,128)} %depth.1, f32[32,128]{1,0:T(8,128)} %innov_in.1, f32[32,4,128]{2,1,0:T(4,128)} %weight_in.1, s32[1,32]{1,0:T(1,128)} %bitcast.2, s32[1,32]{1,0:T(1,128)} %bitcast.3, ...), custom_call_target="tpu_custom_call" | custom-call | tf_op jit(solution)/shard_map/route/pallas_call | solution.py:691
  36.9 5.1 %spread.1.forcing_in = f32[4,256,128]{2,1,0:T(8,128)} custom-call(s32[8,128]{1,0:T(8,128)} %get-tuple-element.9.counts_in, f32[128,5,128]{2,1,0:T(8,128)} %get-tuple-element.10.recv_in), custom_call_target="tpu_custom_call" | custom-call | tf_op jit(solution)/shard_map/spread/pallas_call | solution.py:725
  42.0 0.0 copy-start
  42.0 1.0 %copy-done = f32[4,256,128]{2,1,0:T(8,128)S(1)} copy-done((f32[4,256,128]{2,1,0:T(8,128)S(1)}, f32[4,256,128]{2,1,0:T(8,128)}, u32[]{:S(2)}) %copy-start) | copy-done | bytes 524312
  43.0 14.9 %finish.1 = f32[3,256,512]{2,1,0:T(8,128)S(1)} custom-call(f32[5,5,38,8,128]{4,3,2,1,0:T(8,128)} %get-tuple-element.8.fields_in, f32[4,256,128]{2,1,0:T(8,128)S(1)} %copy-done), custom_call_target="tpu_custom_call" | custom-call | tf_op jit(solution)/shard_map/finish/pallas_call | solution.py:743
  58.0 1.1 %copy.10 = f32[3,256,512]{2,1,0:T(8,128)} copy(f32[3,256,512]{2,1,0:T(8,128)S(1)} %finish.1) | data formatting | bytes 3145728
Async XLA Ops:
  42.0 1.0 %copy-start = (f32[4,256,128]{2,1,0:T(8,128)S(1)}, f32[4,256,128]{2,1,0:T(8,128)}, u32[]{:S(2)}) copy-start(f32[4,256,128]{2,1,0:T(8,128)} %spread.1.forcing_in) | copy-start | bytes 1572868

commit v5 on v4

--- a/solution.py
+++ b/solution.py
@@ -33,12 +33,8 @@
 
 
 def shift_to(me, index, lon):
-    if lon != 64:
-        return lax.rem(me + index, lon)
-    z = (me // 8 + index % 8) % 8
-    y = (me // 2 + index // 8) % 4
-    x = (me + index // 32) % 2
-    return (z * 4 + y) * 2 + x
+    where = me + index
+    return jnp.where(where >= lon, where - lon, where)
 
 
 def columns_at(width):
@@ -67,34 +63,46 @@
     return value
 
 
-def over(number, body, most):
-    unroll = max(d for d in range(1, number + 1) if number % d == 0 and d <= max(most, 1))
-
-    def one(k, carry):
-        body(k)
+def piece(number, most):
+    return max(d for d in range(1, number + 1) if number % d == 0 and d <= max(most, 1))
+
+
+def over(number, body, most, also=None):
+    size = piece(number, most)
+
+    def one(p, carry):
+        for j in range(size):
+            body(p * size + j)
+        if also is not None:
+            also(p)
         return carry
 
-    lax.fori_loop(0, number, one, 0, unroll=unroll)
-
-
-def to_runs(maps, natural, temp, number, keep):
+    lax.fori_loop(0, number // size, one, 0)
+
+
+def to_runs(maps, natural, temp, number, keep, also=None):
     lane, part_of, cuts, into, turn, back, out = maps
     width = len(cuts)
     most = 100 // len(natural)
+    pieces = number // piece(number, most)
+
+    def beside(turn_number):
+        return None if also is None else lambda p: also(turn_number * pieces + p)
+
     for t in range(width):
         def sort(k):
             rows = pl.ds(k, ROWS8, stride=number)
             for f, ref in enumerate(natural):
                 temp[f, t, k] = take(jnp.where(lane >= cuts[t], ref[(t - 1) % width, rows, :], ref[t, rows, :]), into[t])
 
-        over(number, sort, most)
+        over(number, sort, most, beside(t))
     for c in range(width):
         def mix(k):
             for f in range(len(natural)):
                 value = by_part(part_of, [temp[f, (p - c) % width, k] for p in range(width)])
                 keep(f, c, k, take(value, turn[c]) if c else value)
 
-        over(number, mix, most)
+        over(number, mix, most, beside(width + c))
 
 
 def from_runs(maps, refs, temp, number, natural, finished):
@@ -193,7 +201,8 @@
         def _():
             for column in (west, my_lon, east):
                 pl.semaphore_signal(barrier, inc=1, device_id=(where, column), device_id_type=MESH)
-    lax.fori_loop(1, lon, greet, 0)
+    greetings = (lon - 1) // blocks
+    lax.fori_loop(1 + greetings * blocks, lon, greet, 0)
 
     for load in small:
         load.wait()
@@ -222,6 +231,8 @@
     sub = lax.broadcasted_iota(I32, (ROWS8 - 4, slots), 0)
 
     def order(b, carry):
+        for j in range(greetings):
+            greet(1 + b * greetings + j, 0)
         move = jnp.where(ranks == spots[pl.ds(b, 1), :], 1.0, 0.0).astype(BF16)
         values = weight[b] * innov[pl.ds(b, 1), :]
         data = jnp.concatenate([values, jnp.where(sub == 0, cells[pl.ds(b, 1), :], 0.0)], axis=0)
@@ -338,7 +349,9 @@
         block_copy(index).start()
         return carry
 
-    lax.fori_loop(1, lon, send_blocks, 0)
+    pieces = 2 * (tiles + 1) * (number // piece(number, 20))
+    beside = (lon - 1) // pieces
+    lax.fori_loop(1, lon - beside * pieces, send_blocks, 0)
     mine = pl.ds(CAP * my_lon, CAP)
     own = pltpu.make_async_copy(send.at[mine], recv.at[mine], own_sem)
     own.start()
@@ -388,7 +401,11 @@
     def keep(f, c, k, value):
         refs[f][c, k] = value
 
-    to_runs(maps, [fields.at[f] for f in range(5)], temp, number, keep)
+    def send_some(p):
+        for j in range(beside):
+            block_copy(lon - beside * pieces + p * beside + j).start()
+
+    to_runs(maps, [fields.at[f] for f in range(5)], temp, number, keep, send_some)
     inner = pl.ds(0, number)
     stores = [pltpu.make_async_copy(ref.at[:, inner], fields_out.at[f], store_sem.at[f]) for f, ref in enumerate(refs)]
     for store in stores[3:]:
@@ -737,7 +754,7 @@
             *[pltpu.VMEM((cols // COL_BINS, 2 * GROUP * LANES), BF16)] * 2,
             dma((2,)),
         ],
-        compiler_params=pltpu.CompilerParams(vmem_limit_bytes=56 << 20),
+        compiler_params=pltpu.CompilerParams(vmem_limit_bytes=24 << 20),
     )(counts, recv)
     run = rows // 8 + 2 * FRINGE
     return pl.pallas_call(

time: 59.2 us -> 62 us (1.047)
  Pallas kernels: 56.9 us -> 58.9 us
  local copies, waits for them, and re-layouts: 2.18 us -> 2.86 us
    pallas_call x1, Pallas kernels: 36.9 us -> 40 us  [per_device(): pl.pallas_call(functools.partial(route_kernel, dims), name='route', out_s...]
    pallas_call x1, Pallas kernels: 5.06 us -> 3.9 us  [per_device(): pl.pallas_call(functools.partial(spread_kernel, dims), name='spread', out...]
    unnamed x3 -> x5, local copies, waits for them, and re-layouts: 2.18 us -> 2.86 us
where the time goes in v5:
time: 62 us; the launch traced here: 61.8 us
  Pallas kernels  58.9 us (95%)
  local copies, waits for them, and re-layouts  2.86 us (5%)
    pallas_call x1, Pallas kernels, per_device(): pl.pallas_call(functools.partial(route_kernel, dims), name='route', out_s...  40 us
    pallas_call x1, Pallas kernels, per_device(): pl.pallas_call(functools.partial(finish_kernel, dims), name='finish', out...  15.1 us
    pallas_call x1, Pallas kernels, per_device(): pl.pallas_call(functools.partial(spread_kernel, dims), name='spread', out...  3.9 us
    unnamed x5, local copies, waits for them, and re-layouts  2.86 us

profile of v5, /device:TPU:1, one launch (start us, length us, event | category | flops | bytes accessed | tf_op | source)
XLA Modules:
  0.0 61.8 jit_solution(14864758724910975099)
XLA Ops:
  0.0 40.0 %route.1 = (f32[5,5,38,8,128]{4,3,2,1,0:T(8,128)}, f32[128,5,128]{2,1,0:T(8,128)}, s32[8,128]{1,0:T(8,128)}) custom-call(f32[3,256,512]{2,1,0:T(8,128)} %state.1, f32[2,256,512]{2,1,0:T(8,128)} %depth.1, f32[32,128]{1,0:T(8,128)} %innov_in.1, f32[32,4,128]{2,1,0:T(4,128)} %weight_in.1, s32[1,32]{1,0:T(1,128)} %bitcast.2, s32[1,32]{1,0:T(1,128)} %bitcast.3, ...), custom_call_target="tpu_custom_call" | custom-call | tf_op jit(solution)/shard_map/route/pallas_call | solution.py:708
  40.0 0.0 copy-start
  40.0 1.0 %copy-done = f32[128,5,128]{2,1,0:T(8,128)S(1)} copy-done((f32[128,5,128]{2,1,0:T(8,128)S(1)}, f32[128,5,128]{2,1,0:T(8,128)}, u32[]{:S(2)}) %copy-start) | copy-done | bytes 327704
  41.0 0.0 copy-start.1
  41.0 0.7 %copy-done.1 = s32[8,128]{1,0:T(8,128)S(1)} copy-done((s32[8,128]{1,0:T(8,128)S(1)}, s32[8,128]{1,0:T(8,128)}, u32[]{:S(2)}) %copy-start.1) | copy-done | bytes 4120
  41.7 3.9 %spread.1.forcing_in = f32[4,256,128]{2,1,0:T(8,128)S(1)} custom-call(s32[8,128]{1,0:T(8,128)S(1)} %copy-done.1, f32[128,5,128]{2,1,0:T(8,128)S(1)} %copy-done), custom_call_target="tpu_custom_call" | custom-call | tf_op jit(solution)/shard_map/spread/pallas_call | solution.py:742
  45.6 15.1 %finish.1 = f32[3,256,512]{2,1,0:T(8,128)S(1)} custom-call(f32[5,5,38,8,128]{4,3,2,1,0:T(8,128)} %get-tuple-element.8.fields_in, f32[4,256,128]{2,1,0:T(8,128)S(1)} %spread.1.forcing_in), custom_call_target="tpu_custom_call" | custom-call | tf_op jit(solution)/shard_map/finish/pallas_call | solution.py:760
  60.7 1.1 %copy.10 = f32[3,256,512]{2,1,0:T(8,128)} copy(f32[3,256,512]{2,1,0:T(8,128)S(1)} %finish.1) | data formatting | bytes 3145728
Async XLA Ops:
  40.0 1.0 %copy-start = (f32[128,5,128]{2,1,0:T(8,128)S(1)}, f32[128,5,128]{2,1,0:T(8,128)}, u32[]{:S(2)}) copy-start(f32[128,5,128]{2,1,0:T(8,128)} %get-tuple-element.10.recv_in) | copy-start | bytes 983044
  41.0 0.7 %copy-start.1 = (s32[8,128]{1,0:T(8,128)S(1)}, s32[8,128]{1,0:T(8,128)}, u32[]{:S(2)}) copy-start(s32[8,128]{1,0:T(8,128)} %get-tuple-element.9.counts_in) | copy-start | bytes 12292

commit v6 on v4

--- a/solution.py
+++ b/solution.py
@@ -33,12 +33,8 @@
 
 
 def shift_to(me, index, lon):
-    if lon != 64:
-        return lax.rem(me + index, lon)
-    z = (me // 8 + index % 8) % 8
-    y = (me // 2 + index // 8) % 4
-    x = (me + index // 32) % 2
-    return (z * 4 + y) * 2 + x
+    where = me + index
+    return jnp.where(where >= lon, where - lon, where)
 
 
 def columns_at(width):
@@ -68,13 +64,14 @@
 
 
 def over(number, body, most):
-    unroll = max(d for d in range(1, number + 1) if number % d == 0 and d <= max(most, 1))
-
-    def one(k, carry):
-        body(k)
+    size = max(d for d in range(1, number + 1) if number % d == 0 and d <= max(most, 1))
+
+    def one(p, carry):
+        for j in range(size):
+            body(p * size + j)
         return carry
 
-    lax.fori_loop(0, number, one, 0, unroll=unroll)
+    lax.fori_loop(0, number // size, one, 0)
 
 
 def to_runs(maps, natural, temp, number, keep):
@@ -157,9 +154,9 @@
     lax.fori_loop(0, number // 2, two, 0)
 
 
-def route_kernel(dims, state, depth, innov_in, weight_in, tile_in, count_in, row_in, col_in, fields_out, recv_out, count_out,
+def route_kernel(dims, state, depth, innov_in, weight_in, tile_in, count_in, row_in, col_in, fields_out, recv,
                  fields, height, other, east_vel, north_vel, depth_east, depth_north,
-                 innov, weight, tile_row, count_row, obs_row, obs_col, spots, cells, ordered, temp, send, recv, east_pack, west_pack, east_got, west_got,
+                 innov, weight, tile_row, count_row, obs_row, obs_col, spots, cells, ordered, temp, send, east_pack, west_pack, east_got, west_got,
                  load_sem, small_sem, row_sem, pack_sem, corner_sem, a2a_sem, own_sem, store_sem):
     rows, cols, lat, lon, blocks = dims
     tiles = cols // LANES
@@ -194,6 +191,83 @@
             for column in (west, my_lon, east):
                 pl.semaphore_signal(barrier, inc=1, device_id=(where, column), device_id_type=MESH)
     lax.fori_loop(1, lon, greet, 0)
+
+    zero_rows = jnp.zeros((5, tiles, HALO, LANES), F32)
+
+    @pl.when(jnp.logical_not(has_south))
+    def _():
+        fields[:, pl.ds(0, tiles), pl.ds(0, HALO), :] = zero_rows
+        east_got[pl.ds(0, HALO), :] = zero_rows[0, 0]
+        west_got[pl.ds(0, HALO), :] = zero_rows[0, 0]
+
+    @pl.when(jnp.logical_not(has_north))
+    def _():
+        fields[:, pl.ds(0, tiles), pl.ds(HALO + rows, HALO), :] = zero_rows
+        east_got[pl.ds(HALO + rows, HALO), :] = zero_rows[0, 0]
+        west_got[pl.ds(HALO + rows, HALO), :] = zero_rows[0, 0]
+
+    for load in loads:
+        load.wait()
+
+    @pl.when(jnp.logical_not(has_north))
+    def _():
+        wall = pl.ds(HALO + rows - ROWS8, ROWS8)
+        keep = lax.broadcasted_iota(I32, (tiles, ROWS8, LANES), 1) < ROWS8 - 1
+        fields[4, pl.ds(0, tiles), wall, :] = jnp.where(keep, fields[4, pl.ds(0, tiles), wall, :], 0.0)
+
+    lane = lane_ids((ROWS8, LANES))
+
+    def pack(index, carry):
+        base = pl.multiple_of(index * ROWS8, ROWS8)
+        here = pl.ds(HALO + base, ROWS8)
+        to_west = jnp.zeros((ROWS8, LANES), F32)
+        to_east = to_west
+        for f in range(5):
+            first = HALO * f
+            inside = jnp.logical_and(lane >= first, lane < first + HALO)
+            to_west = jnp.where(inside, pltpu.roll(fields[f, 0, here, :], first, 1) if f else fields[f, 0, here, :], to_west)
+            first = (LANES - HALO + HALO * f) % LANES
+            inside = jnp.logical_and(lane >= first, lane < first + HALO)
+            value = fields[f, tiles - 1, here, :]
+            to_east = jnp.where(inside, pltpu.roll(value, HALO * f, 1) if f else value, to_east)
+        west_pack[pl.ds(base, ROWS8), :] = to_west
+        east_pack[pl.ds(base, ROWS8), :] = to_east
+        return carry
+
+    lax.fori_loop(0, rows // ROWS8, pack, 0, unroll=8)
+
+    pl.semaphore_wait(barrier, lon - 1 + 3 * has_north.astype(I32) + 3 * has_south.astype(I32))
+
+    def remote(source, target, sems, where):
+        return pltpu.make_async_remote_copy(src_ref=source, dst_ref=target, send_sem=sems.at[0], recv_sem=sems.at[1],
+                                            device_id=where, device_id_type=MESH)
+
+    main = pl.ds(HALO, rows)
+    low_rows, high_rows = pl.ds(0, HALO), pl.ds(HALO + rows, HALO)
+    inner = pl.ds(0, tiles)
+    to_north = remote(fields.at[:, inner, pl.ds(rows, HALO), :], fields.at[:, inner, low_rows, :], row_sem.at[0], (my_lat + 1, my_lon))
+    to_south = remote(fields.at[:, inner, pl.ds(HALO, HALO), :], fields.at[:, inner, high_rows, :], row_sem.at[1], (my_lat - 1, my_lon))
+    to_east = remote(east_pack, west_got.at[main], pack_sem.at[0], (my_lat, east))
+    to_west = remote(west_pack, east_got.at[main], pack_sem.at[1], (my_lat, west))
+    tail = pl.ds(rows - HALO, HALO)
+    north_east = remote(east_pack.at[tail], west_got.at[low_rows], corner_sem.at[0], (my_lat + 1, east))
+    north_west = remote(west_pack.at[tail], east_got.at[low_rows], corner_sem.at[1], (my_lat + 1, west))
+    south_east = remote(east_pack.at[low_rows], west_got.at[high_rows], corner_sem.at[2], (my_lat - 1, east))
+    south_west = remote(west_pack.at[low_rows], east_got.at[high_rows], corner_sem.at[3], (my_lat - 1, west))
+    northward, southward = (to_north, north_east, north_west), (to_south, south_east, south_west)
+
+    @pl.when(has_north)
+    def _():
+        for copy in northward:
+            copy.start()
+
+    @pl.when(has_south)
+    def _():
+        for copy in southward:
+            copy.start()
+
+    to_east.start()
+    to_west.start()
 
     for load in small:
         load.wait()
@@ -253,83 +327,6 @@
             + jnp.dot(pick, low, preferred_element_type=F32))
     send[...] = sent.reshape(CAP * lon, ROWS8, slots)[:, :PIECES, :]
 
-    zero_rows = jnp.zeros((5, tiles, HALO, LANES), F32)
-
-    @pl.when(jnp.logical_not(has_south))
-    def _():
-        fields[:, pl.ds(0, tiles), pl.ds(0, HALO), :] = zero_rows
-        east_got[pl.ds(0, HALO), :] = zero_rows[0, 0]
-        west_got[pl.ds(0, HALO), :] = zero_rows[0, 0]
-
-    @pl.when(jnp.logical_not(has_north))
-    def _():
-        fields[:, pl.ds(0, tiles), pl.ds(HALO + rows, HALO), :] = zero_rows
-        east_got[pl.ds(HALO + rows, HALO), :] = zero_rows[0, 0]
-        west_got[pl.ds(HALO + rows, HALO), :] = zero_rows[0, 0]
-
-    for load in loads:
-        load.wait()
-
-    @pl.when(jnp.logical_not(has_north))
-    def _():
-        wall = pl.ds(HALO + rows - ROWS8, ROWS8)
-        keep = lax.broadcasted_iota(I32, (tiles, ROWS8, LANES), 1) < ROWS8 - 1
-        fields[4, pl.ds(0, tiles), wall, :] = jnp.where(keep, fields[4, pl.ds(0, tiles), wall, :], 0.0)
-
-    lane = lane_ids((ROWS8, LANES))
-
-    def pack(index, carry):
-        base = pl.multiple_of(index * ROWS8, ROWS8)
-        here = pl.ds(HALO + base, ROWS8)
-        to_west = jnp.zeros((ROWS8, LANES), F32)
-        to_east = to_west
-        for f in range(5):
-            first = HALO * f
-            inside = jnp.logical_and(lane >= first, lane < first + HALO)
-            to_west = jnp.where(inside, pltpu.roll(fields[f, 0, here, :], first, 1) if f else fields[f, 0, here, :], to_west)
-            first = (LANES - HALO + HALO * f) % LANES
-            inside = jnp.logical_and(lane >= first, lane < first + HALO)
-            value = fields[f, tiles - 1, here, :]
-            to_east = jnp.where(inside, pltpu.roll(value, HALO * f, 1) if f else value, to_east)
-        west_pack[pl.ds(base, ROWS8), :] = to_west
-        east_pack[pl.ds(base, ROWS8), :] = to_east
-        return carry
-
-    lax.fori_loop(0, rows // ROWS8, pack, 0, unroll=8)
-
-    pl.semaphore_wait(barrier, lon - 1 + 3 * has_north.astype(I32) + 3 * has_south.astype(I32))
-
-    def remote(source, target, sems, where):
-        return pltpu.make_async_remote_copy(src_ref=source, dst_ref=target, send_sem=sems.at[0], recv_sem=sems.at[1],
-                                            device_id=where, device_id_type=MESH)
-
-    main = pl.ds(HALO, rows)
-    low_rows, high_rows = pl.ds(0, HALO), pl.ds(HALO + rows, HALO)
-    inner = pl.ds(0, tiles)
-    to_north = remote(fields.at[:, inner, pl.ds(rows, HALO), :], fields.at[:, inner, low_rows, :], row_sem.at[0], (my_lat + 1, my_lon))
-    to_south = remote(fields.at[:, inner, pl.ds(HALO, HALO), :], fields.at[:, inner, high_rows, :], row_sem.at[1], (my_lat - 1, my_lon))
-    to_east = remote(east_pack, west_got.at[main], pack_sem.at[0], (my_lat, east))
-    to_west = remote(west_pack, east_got.at[main], pack_sem.at[1], (my_lat, west))
-    tail = pl.ds(rows - HALO, HALO)
-    north_east = remote(east_pack.at[tail], west_got.at[low_rows], corner_sem.at[0], (my_lat + 1, east))
-    north_west = remote(west_pack.at[tail], east_got.at[low_rows], corner_sem.at[1], (my_lat + 1, west))
-    south_east = remote(east_pack.at[low_rows], west_got.at[high_rows], corner_sem.at[2], (my_lat - 1, east))
-    south_west = remote(west_pack.at[low_rows], east_got.at[high_rows], corner_sem.at[3], (my_lat - 1, west))
-    northward, southward = (to_north, north_east, north_west), (to_south, south_east, south_west)
-
-    @pl.when(has_north)
-    def _():
-        for copy in northward:
-            copy.start()
-
-    @pl.when(has_south)
-    def _():
-        for copy in southward:
-            copy.start()
-
-    to_east.start()
-    to_west.start()
-
     def block_copy(index):
         where = shift_to(my_lon, index, lon)
         return remote(send.at[pl.ds(CAP * where, CAP)], recv.at[pl.ds(CAP * my_lon, CAP)], a2a_sem, (my_lat, where))
@@ -402,22 +399,12 @@
     every = pltpu.make_async_remote_copy(src_ref=send.at[others], dst_ref=recv.at[others], send_sem=a2a_sem.at[0],
                                          recv_sem=a2a_sem.at[1], device_id=(my_lat, east), device_id_type=MESH)
     every.wait_recv()
-    stores.append(pltpu.make_async_copy(recv, recv_out, store_sem.at[5]))
-    stores[5].start()
-    cell = recv[:, PIECES - 1, :]
-    ones = jnp.ones((ROWS8, slots), BF16)
-    area = float(bin_rows * bin_cols)
-    for b in range(BINS):
-        within = jnp.logical_and(cell > b * area, cell <= (b + 1) * area)
-        live_of = lax.dot_general(ones, jnp.where(within, 1.0, 0.0).astype(BF16), (((1,), (1,)), ((), ())), preferred_element_type=F32)
-        count_out[pl.ds(b, 1), :] = live_of[:1].astype(I32)
-    count_out[pl.ds(BINS, ROWS8 - BINS), :] = jnp.zeros((ROWS8 - BINS, CAP * lon), I32)
     every.wait_send()
     for store in stores:
         store.wait()
 
 
-def spread_kernel(dims, counts_in, recv_in, out, counts, recv, packed, total, left_a, left_b, right_a, right_b, load_sem):
+def spread_kernel(dims, recv, out, counts, found, packed, total, left_a, left_b, right_a, right_b, load_sem):
     rows, cols, lat, lon, blocks = dims
     tiles = cols // LANES
     segments = CAP * lon
@@ -426,12 +413,18 @@
     padded = left_a.shape[0] // 2
     depth = GROUP * LANES
     room = segments + GROUP
-    loads = [pltpu.make_async_copy(counts_in, counts, load_sem.at[0]), pltpu.make_async_copy(recv_in, recv, load_sem.at[1])]
-    for load in loads:
-        load.start()
+    cell = recv[:, PIECES - 1, :]
+    ones = jnp.ones((ROWS8, LANES), BF16)
+    area = float(bin_rows * bin_cols)
+    for b in range(bins):
+        within = jnp.logical_and(cell > b * area, cell <= (b + 1) * area)
+        live_of = lax.dot_general(ones, jnp.where(within, 1.0, 0.0).astype(BF16), (((1,), (1,)), ((), ())), preferred_element_type=F32)
+        found[pl.ds(b, 1), :] = live_of[:1].astype(I32)
+    found[pl.ds(bins, ROWS8 - bins), :] = jnp.zeros((ROWS8 - bins, segments), I32)
+    load = pltpu.make_async_copy(found, counts, load_sem)
+    load.start()
     total[...] = jnp.zeros_like(total)
-    for load in loads:
-        load.wait()
+    load.wait()
     lane = lane_ids((PIECES, LANES))
     zero = jnp.zeros((PIECES, LANES), F32)
 
@@ -688,16 +681,15 @@
     natural = pltpu.VMEM((5, tiles + 1, ext, LANES), F32)
     runs = [pltpu.VMEM((tiles + 1, number + 1, ROWS8, LANES), F32)] * 2 + [pltpu.VMEM((tiles + 1, number, ROWS8, LANES), F32)] * 4
     params = functools.partial(pltpu.CompilerParams, has_side_effects=True)
-    fields, recv, counts = pl.pallas_call(
+    fields, recv = pl.pallas_call(
         functools.partial(route_kernel, dims),
         name="route",
         out_shape=(
             jax.ShapeDtypeStruct((5, tiles + 1, number, ROWS8, LANES), F32),
             jax.ShapeDtypeStruct((segments, PIECES, slots), F32),
-            jax.ShapeDtypeStruct((ROWS8, segments), I32),
         ),
         in_specs=[anywhere] * 8,
-        out_specs=(anywhere, anywhere, vmem),
+        out_specs=(anywhere, anywhere),
         scratch_shapes=[
             natural, *runs,
             pltpu.VMEM((blocks, slots), F32),
@@ -711,12 +703,11 @@
             pltpu.VMEM((ROWS8 * blocks, slots), F32),
             pltpu.VMEM((5, tiles + 1, number, ROWS8, LANES), F32),
             pltpu.VMEM((segments, PIECES, slots), F32),
-            pltpu.VMEM((segments, PIECES, slots), F32),
             pltpu.VMEM((rows, LANES), F32),
             pltpu.VMEM((rows, LANES), F32),
             pltpu.VMEM((ext, LANES), F32),
             pltpu.VMEM((ext, LANES), F32),
-            dma((2 * tiles,)), dma((6,)), dma((2, 2)), dma((2, 2)), dma((4, 2)), dma((2,)), dma, dma((6,)),
+            dma((2 * tiles,)), dma((6,)), dma((2, 2)), dma((2, 2)), dma((4, 2)), dma((2,)), dma, dma((5,)),
         ],
         compiler_params=params(collective_id=0, vmem_limit_bytes=56 << 20),
     )(adjoint_state, face_depth, innovation, interp_weight, block_tile.reshape(1, blocks), block_count.reshape(1, blocks),
@@ -726,19 +717,19 @@
         functools.partial(spread_kernel, dims),
         name="spread",
         out_shape=jax.ShapeDtypeStruct((tiles, rows, LANES), F32),
-        in_specs=[anywhere] * 2,
+        in_specs=[vmem],
         out_specs=vmem,
         scratch_shapes=[
             pltpu.SMEM((ROWS8, segments), I32),
-            pltpu.VMEM((segments, PIECES, slots), F32),
+            pltpu.VMEM((ROWS8, segments), I32),
             pltpu.VMEM((BINS * (segments + GROUP) + GROUP, PIECES, LANES), F32),
             pltpu.VMEM((BINS, 2 * padded, cols // COL_BINS), F32),
             *[pltpu.VMEM((2 * padded, 2 * GROUP * LANES), BF16)] * 2,
             *[pltpu.VMEM((cols // COL_BINS, 2 * GROUP * LANES), BF16)] * 2,
-            dma((2,)),
+            dma,
         ],
-        compiler_params=pltpu.CompilerParams(vmem_limit_bytes=56 << 20),
-    )(counts, recv)
+        compiler_params=pltpu.CompilerParams(vmem_limit_bytes=24 << 20),
+    )(recv)
     run = rows // 8 + 2 * FRINGE
     return pl.pallas_call(
         functools.partial(finish_kernel, dims),

time: 59.2 us -> 56.4 us (0.953)
  Pallas kernels: 56.9 us -> 54 us
    pallas_call x1, Pallas kernels: 36.9 us -> 34.6 us  [per_device(): pl.pallas_call(functools.partial(route_kernel, dims), name='route', out_s...]
    pallas_call x1, Pallas kernels: 5.06 us -> 4.33 us  [per_device(): pl.pallas_call(functools.partial(spread_kernel, dims), name='spread', out...]
where the time goes in v6:
time: 56.4 us; the launch traced here: 56.2 us
  Pallas kernels  54 us (96%)
  local copies, waits for them, and re-layouts  2.18 us (4%)
    pallas_call x1, Pallas kernels, per_device(): pl.pallas_call(functools.partial(route_kernel, dims), name='route', out_s...  34.6 us
    pallas_call x1, Pallas kernels, per_device(): pl.pallas_call(functools.partial(finish_kernel, dims), name='finish', out...  15.1 us
    pallas_call x1, Pallas kernels, per_device(): pl.pallas_call(functools.partial(spread_kernel, dims), name='spread', out...  4.33 us
    unnamed x3, local copies, waits for them, and re-layouts  2.18 us

profile of v6, /device:TPU:1, one launch (start us, length us, event | category | flops | bytes accessed | tf_op | source)
XLA Modules:
  0.0 56.2 jit_solution(3060888726780235558)
XLA Ops:
  0.0 34.6 %route.1 = (f32[5,5,38,8,128]{4,3,2,1,0:T(8,128)}, f32[128,5,128]{2,1,0:T(8,128)}) custom-call(f32[3,256,512]{2,1,0:T(8,128)} %state.1, f32[2,256,512]{2,1,0:T(8,128)} %depth.1, f32[32,128]{1,0:T(8,128)} %innov_in.1, f32[32,4,128]{2,1,0:T(4,128)} %weight_in.1, s32[1,32]{1,0:T(1,128)} %bitcast.2, s32[1,32]{1,0:T(1,128)} %bitcast.3, s32[32,128]{1,0:T(8,128)} %row_in.1, ...), custom_call_target="tpu_custom_call" | custom-call | tf_op jit(solution)/shard_map/route/pallas_call | solution.py:684
  34.6 0.0 copy-start
  34.6 1.0 %copy-done = f32[128,5,128]{2,1,0:T(8,128)S(1)} copy-done((f32[128,5,128]{2,1,0:T(8,128)S(1)}, f32[128,5,128]{2,1,0:T(8,128)}, u32[]{:S(2)}) %copy-start) | copy-done | bytes 327704
  35.6 4.3 %spread.1.forcing_in = f32[4,256,128]{2,1,0:T(8,128)S(1)} custom-call(f32[128,5,128]{2,1,0:T(8,128)S(1)} %copy-done), custom_call_target="tpu_custom_call" | custom-call | tf_op jit(solution)/shard_map/spread/pallas_call | solution.py:716
  40.0 15.1 %finish.1 = f32[3,256,512]{2,1,0:T(8,128)S(1)} custom-call(f32[5,5,38,8,128]{4,3,2,1,0:T(8,128)} %get-tuple-element.7.fields_in, f32[4,256,128]{2,1,0:T(8,128)S(1)} %spread.1.forcing_in), custom_call_target="tpu_custom_call" | custom-call | tf_op jit(solution)/shard_map/finish/pallas_call | solution.py:734
  55.1 1.1 %copy.10 = f32[3,256,512]{2,1,0:T(8,128)} copy(f32[3,256,512]{2,1,0:T(8,128)S(1)} %finish.1) | data formatting | bytes 3145728
Async XLA Ops:
  34.6 1.0 %copy-start = (f32[128,5,128]{2,1,0:T(8,128)S(1)}, f32[128,5,128]{2,1,0:T(8,128)}, u32[]{:S(2)}) copy-start(f32[128,5,128]{2,1,0:T(8,128)} %get-tuple-element.8.recv) | copy-start | bytes 983044

commit v7 on v4

--- a/solution.py
+++ b/solution.py
@@ -33,12 +33,8 @@
 
 
 def shift_to(me, index, lon):
-    if lon != 64:
-        return lax.rem(me + index, lon)
-    z = (me // 8 + index % 8) % 8
-    y = (me // 2 + index // 8) % 4
-    x = (me + index // 32) % 2
-    return (z * 4 + y) * 2 + x
+    where = me + index
+    return jnp.where(where >= lon, where - lon, where)
 
 
 def columns_at(width):
@@ -68,13 +64,14 @@
 
 
 def over(number, body, most):
-    unroll = max(d for d in range(1, number + 1) if number % d == 0 and d <= max(most, 1))
-
-    def one(k, carry):
-        body(k)
+    size = max(d for d in range(1, number + 1) if number % d == 0 and d <= max(most, 1))
+
+    def one(p, carry):
+        for j in range(size):
+            body(p * size + j)
         return carry
 
-    lax.fori_loop(0, number, one, 0, unroll=unroll)
+    lax.fori_loop(0, number // size, one, 0)
 
 
 def to_runs(maps, natural, temp, number, keep):
@@ -157,9 +154,9 @@
     lax.fori_loop(0, number // 2, two, 0)
 
 
-def route_kernel(dims, state, depth, innov_in, weight_in, tile_in, count_in, row_in, col_in, fields_out, recv_out, count_out,
+def route_kernel(dims, state, depth, innov_in, weight_in, tile_in, count_in, row_in, col_in, fields_out, recv,
                  fields, height, other, east_vel, north_vel, depth_east, depth_north,
-                 innov, weight, tile_row, count_row, obs_row, obs_col, spots, cells, ordered, temp, send, recv, east_pack, west_pack, east_got, west_got,
+                 innov, weight, tile_row, count_row, obs_row, obs_col, spots, cells, ordered, temp, send, east_pack, west_pack, east_got, west_got,
                  load_sem, small_sem, row_sem, pack_sem, corner_sem, a2a_sem, own_sem, store_sem):
     rows, cols, lat, lon, blocks = dims
     tiles = cols // LANES
@@ -193,7 +190,7 @@
         def _():
             for column in (west, my_lon, east):
                 pl.semaphore_signal(barrier, inc=1, device_id=(where, column), device_id_type=MESH)
-    lax.fori_loop(1, lon, greet, 0)
+    lax.fori_loop(1, lon, greet, 0, unroll=max(d for d in range(1, 10) if (lon - 1) % d == 0))
 
     for load in small:
         load.wait()
@@ -338,7 +335,7 @@
         block_copy(index).start()
         return carry
 
-    lax.fori_loop(1, lon, send_blocks, 0)
+    lax.fori_loop(1, lon, send_blocks, 0, unroll=max(d for d in range(1, 10) if (lon - 1) % d == 0))
     mine = pl.ds(CAP * my_lon, CAP)
     own = pltpu.make_async_copy(send.at[mine], recv.at[mine], own_sem)
     own.start()
@@ -402,22 +399,12 @@
     every = pltpu.make_async_remote_copy(src_ref=send.at[others], dst_ref=recv.at[others], send_sem=a2a_sem.at[0],
                                          recv_sem=a2a_sem.at[1], device_id=(my_lat, east), device_id_type=MESH)
     every.wait_recv()
-    stores.append(pltpu.make_async_copy(recv, recv_out, store_sem.at[5]))
-    stores[5].start()
-    cell = recv[:, PIECES - 1, :]
-    ones = jnp.ones((ROWS8, slots), BF16)
-    area = float(bin_rows * bin_cols)
-    for b in range(BINS):
-        within = jnp.logical_and(cell > b * area, cell <= (b + 1) * area)
-        live_of = lax.dot_general(ones, jnp.where(within, 1.0, 0.0).astype(BF16), (((1,), (1,)), ((), ())), preferred_element_type=F32)
-        count_out[pl.ds(b, 1), :] = live_of[:1].astype(I32)
-    count_out[pl.ds(BINS, ROWS8 - BINS), :] = jnp.zeros((ROWS8 - BINS, CAP * lon), I32)
     every.wait_send()
     for store in stores:
         store.wait()
 
 
-def spread_kernel(dims, counts_in, recv_in, out, counts, recv, packed, total, left_a, left_b, right_a, right_b, load_sem):
+def spread_kernel(dims, recv, out, counts, found, packed, total, left_a, left_b, right_a, right_b, load_sem):
     rows, cols, lat, lon, blocks = dims
     tiles = cols // LANES
     segments = CAP * lon
@@ -426,12 +413,18 @@
     padded = left_a.shape[0] // 2
     depth = GROUP * LANES
     room = segments + GROUP
-    loads = [pltpu.make_async_copy(counts_in, counts, load_sem.at[0]), pltpu.make_async_copy(recv_in, recv, load_sem.at[1])]
-    for load in loads:
-        load.start()
+    cell = recv[:, PIECES - 1, :]
+    ones = jnp.ones((ROWS8, LANES), BF16)
+    area = float(bin_rows * bin_cols)
+    for b in range(bins):
+        within = jnp.logical_and(cell > b * area, cell <= (b + 1) * area)
+        live_of = lax.dot_general(ones, jnp.where(within, 1.0, 0.0).astype(BF16), (((1,), (1,)), ((), ())), preferred_element_type=F32)
+        found[pl.ds(b, 1), :] = live_of[:1].astype(I32)
+    found[pl.ds(bins, ROWS8 - bins), :] = jnp.zeros((ROWS8 - bins, segments), I32)
+    load = pltpu.make_async_copy(found, counts, load_sem)
+    load.start()
     total[...] = jnp.zeros_like(total)
-    for load in loads:
-        load.wait()
+    load.wait()
     lane = lane_ids((PIECES, LANES))
     zero = jnp.zeros((PIECES, LANES), F32)
 
@@ -688,16 +681,15 @@
     natural = pltpu.VMEM((5, tiles + 1, ext, LANES), F32)
     runs = [pltpu.VMEM((tiles + 1, number + 1, ROWS8, LANES), F32)] * 2 + [pltpu.VMEM((tiles + 1, number, ROWS8, LANES), F32)] * 4
     params = functools.partial(pltpu.CompilerParams, has_side_effects=True)
-    fields, recv, counts = pl.pallas_call(
+    fields, recv = pl.pallas_call(
         functools.partial(route_kernel, dims),
         name="route",
         out_shape=(
             jax.ShapeDtypeStruct((5, tiles + 1, number, ROWS8, LANES), F32),
             jax.ShapeDtypeStruct((segments, PIECES, slots), F32),
-            jax.ShapeDtypeStruct((ROWS8, segments), I32),
         ),
         in_specs=[anywhere] * 8,
-        out_specs=(anywhere, anywhere, vmem),
+        out_specs=(anywhere, anywhere),
         scratch_shapes=[
             natural, *runs,
             pltpu.VMEM((blocks, slots), F32),
@@ -711,12 +703,11 @@
             pltpu.VMEM((ROWS8 * blocks, slots), F32),
             pltpu.VMEM((5, tiles + 1, number, ROWS8, LANES), F32),
             pltpu.VMEM((segments, PIECES, slots), F32),
-            pltpu.VMEM((segments, PIECES, slots), F32),
             pltpu.VMEM((rows, LANES), F32),
             pltpu.VMEM((rows, LANES), F32),
             pltpu.VMEM((ext, LANES), F32),
             pltpu.VMEM((ext, LANES), F32),
-            dma((2 * tiles,)), dma((6,)), dma((2, 2)), dma((2, 2)), dma((4, 2)), dma((2,)), dma, dma((6,)),
+            dma((2 * tiles,)), dma((6,)), dma((2, 2)), dma((2, 2)), dma((4, 2)), dma((2,)), dma, dma((5,)),
         ],
         compiler_params=params(collective_id=0, vmem_limit_bytes=56 << 20),
     )(adjoint_state, face_depth, innovation, interp_weight, block_tile.reshape(1, blocks), block_count.reshape(1, blocks),
@@ -726,19 +717,19 @@
         functools.partial(spread_kernel, dims),
         name="spread",
         out_shape=jax.ShapeDtypeStruct((tiles, rows, LANES), F32),
-        in_specs=[anywhere] * 2,
+        in_specs=[vmem],
         out_specs=vmem,
         scratch_shapes=[
             pltpu.SMEM((ROWS8, segments), I32),
-            pltpu.VMEM((segments, PIECES, slots), F32),
+            pltpu.VMEM((ROWS8, segments), I32),
             pltpu.VMEM((BINS * (segments + GROUP) + GROUP, PIECES, LANES), F32),
             pltpu.VMEM((BINS, 2 * padded, cols // COL_BINS), F32),
             *[pltpu.VMEM((2 * padded, 2 * GROUP * LANES), BF16)] * 2,
             *[pltpu.VMEM((cols // COL_BINS, 2 * GROUP * LANES), BF16)] * 2,
-            dma((2,)),
+            dma,
         ],
-        compiler_params=pltpu.CompilerParams(vmem_limit_bytes=56 << 20),
-    )(counts, recv)
+        compiler_params=pltpu.CompilerParams(vmem_limit_bytes=24 << 20),
+    )(recv)
     run = rows // 8 + 2 * FRINGE
     return pl.pallas_call(
         functools.partial(finish_kernel, dims),

time: 59.2 us -> 56.4 us (0.953)
  Pallas kernels: 56.9 us -> 53.8 us
    pallas_call x1, Pallas kernels: 36.9 us -> 34.3 us  [per_device(): pl.pallas_call(functools.partial(route_kernel, dims), name='route', out_s...]
    pallas_call x1, Pallas kernels: 5.06 us -> 4.33 us  [per_device(): pl.pallas_call(functools.partial(spread_kernel, dims), name='spread', out...]
where the time goes in v7:
time: 56.4 us; the launch traced here: 56.1 us
  Pallas kernels  53.8 us (95%)
  local copies, waits for them, and re-layouts  2.18 us (4%)
    pallas_call x1, Pallas kernels, per_device(): pl.pallas_call(functools.partial(route_kernel, dims), name='route', out_s...  34.3 us
    pallas_call x1, Pallas kernels, per_device(): pl.pallas_call(functools.partial(finish_kernel, dims), name='finish', out...  15.2 us
    pallas_call x1, Pallas kernels, per_device(): pl.pallas_call(functools.partial(spread_kernel, dims), name='spread', out...  4.33 us
    unnamed x3, local copies, waits for them, and re-layouts  2.18 us

profile of v7, /device:TPU:1, one launch (start us, length us, event | category | flops | bytes accessed | tf_op | source)
XLA Modules:
  0.0 56.1 jit_solution(15643007353597508741)
XLA Ops:
  0.0 34.3 %route.1 = (f32[5,5,38,8,128]{4,3,2,1,0:T(8,128)}, f32[128,5,128]{2,1,0:T(8,128)}) custom-call(f32[3,256,512]{2,1,0:T(8,128)} %state.1, f32[2,256,512]{2,1,0:T(8,128)} %depth.1, f32[32,128]{1,0:T(8,128)} %innov_in.1, f32[32,4,128]{2,1,0:T(4,128)} %weight_in.1, s32[1,32]{1,0:T(1,128)} %bitcast.2, s32[1,32]{1,0:T(1,128)} %bitcast.3, s32[32,128]{1,0:T(8,128)} %row_in.1, ...), custom_call_target="tpu_custom_call" | custom-call | tf_op jit(solution)/shard_map/route/pallas_call | solution.py:684
  34.3 0.0 copy-start
  34.3 1.0 %copy-done = f32[128,5,128]{2,1,0:T(8,128)S(1)} copy-done((f32[128,5,128]{2,1,0:T(8,128)S(1)}, f32[128,5,128]{2,1,0:T(8,128)}, u32[]{:S(2)}) %copy-start) | copy-done | bytes 327704
  35.3 4.3 %spread.1.forcing_in = f32[4,256,128]{2,1,0:T(8,128)S(1)} custom-call(f32[128,5,128]{2,1,0:T(8,128)S(1)} %copy-done), custom_call_target="tpu_custom_call" | custom-call | tf_op jit(solution)/shard_map/spread/pallas_call | solution.py:716
  39.7 15.2 %finish.1 = f32[3,256,512]{2,1,0:T(8,128)S(1)} custom-call(f32[5,5,38,8,128]{4,3,2,1,0:T(8,128)} %get-tuple-element.7.fields_in, f32[4,256,128]{2,1,0:T(8,128)S(1)} %spread.1.forcing_in), custom_call_target="tpu_custom_call" | custom-call | tf_op jit(solution)/shard_map/finish/pallas_call | solution.py:734
  54.9 1.1 %copy.10 = f32[3,256,512]{2,1,0:T(8,128)} copy(f32[3,256,512]{2,1,0:T(8,128)S(1)} %finish.1) | data formatting | bytes 3145728
Async XLA Ops:
  34.3 1.0 %copy-start = (f32[128,5,128]{2,1,0:T(8,128)S(1)}, f32[128,5,128]{2,1,0:T(8,128)}, u32[]{:S(2)}) copy-start(f32[128,5,128]{2,1,0:T(8,128)} %get-tuple-element.8.recv) | copy-start | bytes 983044

commit v8 on v7

--- a/solution.py
+++ b/solution.py
@@ -155,7 +155,7 @@
 
 
 def route_kernel(dims, state, depth, innov_in, weight_in, tile_in, count_in, row_in, col_in, fields_out, recv,
-                 fields, height, other, east_vel, north_vel, depth_east, depth_north,
+                 fields, height, east_vel, north_vel, depth_east, depth_north,
                  innov, weight, tile_row, count_row, obs_row, obs_col, spots, cells, ordered, temp, send, east_pack, west_pack, east_got, west_got,
                  load_sem, small_sem, row_sem, pack_sem, corner_sem, a2a_sem, own_sem, store_sem):
     rows, cols, lat, lon, blocks = dims
@@ -388,10 +388,7 @@
     to_runs(maps, [fields.at[f] for f in range(5)], temp, number, keep)
     inner = pl.ds(0, number)
     stores = [pltpu.make_async_copy(ref.at[:, inner], fields_out.at[f], store_sem.at[f]) for f, ref in enumerate(refs)]
-    for store in stores[3:]:
-        store.start()
-    steps(HALF, height, other, *refs[1:])
-    for store in stores[:3]:
+    for store in stores:
         store.start()
 
     own.wait()
@@ -606,6 +603,7 @@
 
     for load in loads[1:]:
         load.wait()
+    steps(HALF, height, other, *refs[1:])
 
     @pl.when(has_south)
     def _():
@@ -691,7 +689,7 @@
         in_specs=[anywhere] * 8,
         out_specs=(anywhere, anywhere),
         scratch_shapes=[
-            natural, *runs,
+            natural, *runs[1:],
             pltpu.VMEM((blocks, slots), F32),
             pltpu.VMEM((blocks, 4, slots), F32),
             pltpu.VMEM((1, blocks), I32),

time: 56.4 us -> 55.6 us (0.986)
  Pallas kernels: 53.8 us -> 53.2 us
    pallas_call x1, Pallas kernels: 34.3 us -> 31.2 us  [per_device(): pl.pallas_call(functools.partial(route_kernel, dims), name='route', out_s...]
    pallas_call x1, Pallas kernels: 15.2 us -> 17.7 us  [per_device(): pl.pallas_call(functools.partial(finish_kernel, dims), name='finish', out...]
where the time goes in v8:
time: 55.6 us; the launch traced here: 55.4 us
  Pallas kernels  53.2 us (96%)
  local copies, waits for them, and re-layouts  2.18 us (4%)
    pallas_call x1, Pallas kernels, per_device(): pl.pallas_call(functools.partial(route_kernel, dims), name='route', out_s...  31.2 us
    pallas_call x1, Pallas kernels, per_device(): pl.pallas_call(functools.partial(finish_kernel, dims), name='finish', out...  17.7 us
    pallas_call x1, Pallas kernels, per_device(): pl.pallas_call(functools.partial(spread_kernel, dims), name='spread', out...  4.33 us
    unnamed x3, local copies, waits for them, and re-layouts  2.18 us

profile of v8, /device:TPU:1, one launch (start us, length us, event | category | flops | bytes accessed | tf_op | source)
XLA Modules:
  0.0 55.4 jit_solution(8143761741523402412)
XLA Ops:
  0.0 31.2 %route.1 = (f32[5,5,38,8,128]{4,3,2,1,0:T(8,128)}, f32[128,5,128]{2,1,0:T(8,128)}) custom-call(f32[3,256,512]{2,1,0:T(8,128)} %state.1, f32[2,256,512]{2,1,0:T(8,128)} %depth.1, f32[32,128]{1,0:T(8,128)} %innov_in.1, f32[32,4,128]{2,1,0:T(4,128)} %weight_in.1, s32[1,32]{1,0:T(1,128)} %bitcast.2, s32[1,32]{1,0:T(1,128)} %bitcast.3, s32[32,128]{1,0:T(8,128)} %row_in.1, ...), custom_call_target="tpu_custom_call" | custom-call | tf_op jit(solution)/shard_map/route/pallas_call | solution.py:682
  31.2 0.0 copy-start
  31.2 1.0 %copy-done = f32[128,5,128]{2,1,0:T(8,128)S(1)} copy-done((f32[128,5,128]{2,1,0:T(8,128)S(1)}, f32[128,5,128]{2,1,0:T(8,128)}, u32[]{:S(2)}) %copy-start) | copy-done | bytes 327704
  32.3 4.3 %spread.1.forcing_in = f32[4,256,128]{2,1,0:T(8,128)S(1)} custom-call(f32[128,5,128]{2,1,0:T(8,128)S(1)} %copy-done), custom_call_target="tpu_custom_call" | custom-call | tf_op jit(solution)/shard_map/spread/pallas_call | solution.py:714
  36.6 17.7 %finish.1 = f32[3,256,512]{2,1,0:T(8,128)S(1)} custom-call(f32[5,5,38,8,128]{4,3,2,1,0:T(8,128)} %get-tuple-element.7.fields_in, f32[4,256,128]{2,1,0:T(8,128)S(1)} %spread.1.forcing_in), custom_call_target="tpu_custom_call" | custom-call | tf_op jit(solution)/shard_map/finish/pallas_call | solution.py:732
  54.3 1.1 %copy.10 = f32[3,256,512]{2,1,0:T(8,128)} copy(f32[3,256,512]{2,1,0:T(8,128)S(1)} %finish.1) | data formatting | bytes 3145728
Async XLA Ops:
  31.2 1.0 %copy-start = (f32[128,5,128]{2,1,0:T(8,128)S(1)}, f32[128,5,128]{2,1,0:T(8,128)}, u32[]{:S(2)}) copy-start(f32[128,5,128]{2,1,0:T(8,128)} %get-tuple-element.8.recv) | copy-start | bytes 983044

commit v9 on v8

--- a/solution.py
+++ b/solution.py
@@ -74,10 +74,10 @@
     lax.fori_loop(0, number // size, one, 0)
 
 
-def to_runs(maps, natural, temp, number, keep):
+def to_runs(maps, natural, temp, number, keep, finished=None):
     lane, part_of, cuts, into, turn, back, out = maps
     width = len(cuts)
-    most = 100 // len(natural)
+    most = 200 // len(natural)
     for t in range(width):
         def sort(k):
             rows = pl.ds(k, ROWS8, stride=number)
@@ -92,6 +92,8 @@
                 keep(f, c, k, take(value, turn[c]) if c else value)
 
         over(number, mix, most)
+        if finished is not None:
+            finished(c)
 
 
 def from_runs(maps, refs, temp, number, natural, finished):
@@ -382,15 +384,17 @@
     refs = (height, east_vel, north_vel, depth_east, depth_north)
     maps = columns_at(tiles + 1)
 
+    stores = []
+
     def keep(f, c, k, value):
         refs[f][c, k] = value
 
-    to_runs(maps, [fields.at[f] for f in range(5)], temp, number, keep)
-    inner = pl.ds(0, number)
-    stores = [pltpu.make_async_copy(ref.at[:, inner], fields_out.at[f], store_sem.at[f]) for f, ref in enumerate(refs)]
-    for store in stores:
-        store.start()
-
+    def finished(c):
+        for f, ref in enumerate(refs):
+            stores.append(pltpu.make_async_copy(ref.at[c, pl.ds(0, number)], fields_out.at[f, c], store_sem.at[f, c]))
+            stores[-1].start()
+
+    to_runs(maps, [fields.at[f] for f in range(5)], temp, number, keep, finished)
     own.wait()
     others = pl.ds(0, CAP * (lon - 1))
     every = pltpu.make_async_remote_copy(src_ref=send.at[others], dst_ref=recv.at[others], send_sem=a2a_sem.at[0],
@@ -705,7 +709,7 @@
             pltpu.VMEM((rows, LANES), F32),
             pltpu.VMEM((ext, LANES), F32),
             pltpu.VMEM((ext, LANES), F32),
-            dma((2 * tiles,)), dma((6,)), dma((2, 2)), dma((2, 2)), dma((4, 2)), dma((2,)), dma, dma((5,)),
+            dma((2 * tiles,)), dma((6,)), dma((2, 2)), dma((2, 2)), dma((4, 2)), dma((2,)), dma, dma((5, tiles + 1)),
         ],
         compiler_params=params(collective_id=0, vmem_limit_bytes=56 << 20),
     )(adjoint_state, face_depth, innovation, interp_weight, block_tile.reshape(1, blocks), block_count.reshape(1, blocks),

time: 55.6 us -> 52.3 us (0.941); the launches traced: 55.4 us -> 51.2 us
  Pallas kernels: 53.2 us -> 49 us
    pallas_call x1, Pallas kernels: 17.7 us -> 15.5 us  [per_device(): pl.pallas_call(functools.partial(finish_kernel, dims), name='finish', out...]
    pallas_call x1, Pallas kernels: 31.2 us -> 29.2 us  [per_device(): pl.pallas_call(functools.partial(route_kernel, dims), name='route', out_s...]
where the time goes in v9:
time: 52.3 us; the launch traced here: 51.2 us
  Pallas kernels  49 us (94%)
  local copies, waits for them, and re-layouts  2.18 us (4%)
    pallas_call x1, Pallas kernels, per_device(): pl.pallas_call(functools.partial(route_kernel, dims), name='route', out_s...  29.2 us
    pallas_call x1, Pallas kernels, per_device(): pl.pallas_call(functools.partial(finish_kernel, dims), name='finish', out...  15.5 us
    pallas_call x1, Pallas kernels, per_device(): pl.pallas_call(functools.partial(spread_kernel, dims), name='spread', out...  4.33 us
    unnamed x3, local copies, waits for them, and re-layouts  2.18 us

profile of v9, /device:TPU:1, one launch (start us, length us, event | category | flops | bytes accessed | tf_op | source)
XLA Modules:
  0.0 51.2 jit_solution(11951549205802136973)
XLA Ops:
  0.0 29.2 %route.1 = (f32[5,5,38,8,128]{4,3,2,1,0:T(8,128)}, f32[128,5,128]{2,1,0:T(8,128)}) custom-call(f32[3,256,512]{2,1,0:T(8,128)} %state.1, f32[2,256,512]{2,1,0:T(8,128)} %depth.1, f32[32,128]{1,0:T(8,128)} %innov_in.1, f32[32,4,128]{2,1,0:T(4,128)} %weight_in.1, s32[1,32]{1,0:T(1,128)} %bitcast.2, s32[1,32]{1,0:T(1,128)} %bitcast.3, s32[32,128]{1,0:T(8,128)} %row_in.1, ...), custom_call_target="tpu_custom_call" | custom-call | tf_op jit(solution)/shard_map/route/pallas_call | solution.py:686
  29.2 0.0 copy-start
  29.3 1.0 %copy-done = f32[128,5,128]{2,1,0:T(8,128)S(1)} copy-done((f32[128,5,128]{2,1,0:T(8,128)S(1)}, f32[128,5,128]{2,1,0:T(8,128)}, u32[]{:S(2)}) %copy-start) | copy-done | bytes 327704
  30.3 4.3 %spread.1.forcing_in = f32[4,256,128]{2,1,0:T(8,128)S(1)} custom-call(f32[128,5,128]{2,1,0:T(8,128)S(1)} %copy-done), custom_call_target="tpu_custom_call" | custom-call | tf_op jit(solution)/shard_map/spread/pallas_call | solution.py:718
  34.6 15.5 %finish.1 = f32[3,256,512]{2,1,0:T(8,128)S(1)} custom-call(f32[5,5,38,8,128]{4,3,2,1,0:T(8,128)} %get-tuple-element.7.fields_in, f32[4,256,128]{2,1,0:T(8,128)S(1)} %spread.1.forcing_in), custom_call_target="tpu_custom_call" | custom-call | tf_op jit(solution)/shard_map/finish/pallas_call | solution.py:736
  50.1 1.1 %copy.10 = f32[3,256,512]{2,1,0:T(8,128)} copy(f32[3,256,512]{2,1,0:T(8,128)S(1)} %finish.1) | data formatting | bytes 3145728
Async XLA Ops:
  29.2 1.0 %copy-start = (f32[128,5,128]{2,1,0:T(8,128)S(1)}, f32[128,5,128]{2,1,0:T(8,128)}, u32[]{:S(2)}) copy-start(f32[128,5,128]{2,1,0:T(8,128)} %get-tuple-element.8.recv) | copy-start | bytes 983044
